TPU v7x, 32 devices: a whole 2x2x4 slice. The times are simulated.
32 devices in a mesh: pb: 8 (over y, x, core), ka: 4 (over z).
Axes of the slice: x: 2, y: 2, z: 4, core: 2. Of those that a mesh axis runs over, the one named last changes fastest.
Arguments:
- query_features: bfloat16 [32, 192, 256], P('pb'), may hold values from -6 to 6
- key_features: bfloat16 [192, 32, 256], P(None, 'ka'), may hold values from -6 to 6
- pyramid_grad: bfloat16 [6144, 4, 2040], P('pb', 'ka'), may hold values from -26.127891 to 26.127891
- query_image: bfloat16 [32, 192, 256], P('pb', 'ka'), may hold values from -0.125 to 0.125
- key_image: bfloat16 [192, 32, 256], P('pb', 'ka'), may hold values from -0.125 to 0.125
- conv_weight: bfloat16 [3, 3, 256, 256], replicated, may hold values from -0.125 to 0.125
Outputs:
- query_image_grad: bfloat16 [32, 192, 256], P('pb', 'ka')
- key_image_grad: bfloat16 [192, 32, 256], P('pb', 'ka')
- weight_grad: float32 [3, 3, 256, 256], replicated
All inputs are finite; a program needn't handle non-finite values.
Results may differ from a plain program's by a relative error of at most 0.0056.
Values may be sent and summed in bfloat16 or wider, within the bound.
No kernel may reach another device: no remote copies, remote signals or barrier semaphores. Data moves between devices by JAX's collectives and lax.ppermute only.
A program may use at most 128 MiB of HBM per device.

v0:
```python
import jax
import jax.numpy as jnp
from jax import lax
from jax.sharding import PartitionSpec as P

D = 256
LEVELS = 4


def padded(cells, sides, width):
    for axis, dim in sides:
        count = lax.axis_size(axis)
        ends = count - 1
        head = lax.slice_in_dim(cells, 0, width, axis=dim)
        tail = lax.slice_in_dim(cells, cells.shape[dim] - width, cells.shape[dim], axis=dim)
        cells = jnp.concatenate(
            [
                lax.ppermute(tail, axis, [(i, (i + 1) % count) for i in range(ends)]),
                cells,
                lax.ppermute(head, axis, [((i + 1) % count, i) for i in range(ends)]),
            ],
            axis=dim,
        )
    return cells


def pool_levels(strip):
    strip_float = strip.astype(jnp.float32)
    result = []
    for level_index in range(LEVELS):
        factor = 2**level_index
        cell_cols, key_rows, channels = strip_float.shape
        pooled = strip_float.reshape(
            cell_cols // factor, factor, key_rows // factor, factor, channels
        ).mean(axis=(1, 3))
        result.append(pooled.astype(jnp.bfloat16))
    return result


def conv_backward(padded_input, padded_grad, kernel):
    tile_rows = padded_grad.shape[0] - 2
    tile_cols = padded_grad.shape[1] - 2
    out_channels = padded_grad.shape[2]
    in_channels = kernel.shape[2]
    interior = padded_grad[1 : 1 + tile_rows, 1 : 1 + tile_cols].reshape(-1, out_channels)
    input_acc = jnp.zeros((tile_rows * tile_cols, in_channels), jnp.float32)
    kernel_rows = []
    for row_shift in range(3):
        kernel_row = []
        for col_shift in range(3):
            shifted = padded_grad[
                2 - row_shift : 2 - row_shift + tile_rows, 2 - col_shift : 2 - col_shift + tile_cols
            ].reshape(-1, out_channels)
            input_acc = input_acc + lax.dot_general(
                shifted,
                kernel[row_shift, col_shift],
                (((1,), (1,)), ((), ())),
                preferred_element_type=jnp.float32,
            )
            window = padded_input[
                row_shift : row_shift + tile_rows, col_shift : col_shift + tile_cols
            ].reshape(-1, in_channels)
            weight_term = lax.dot_general(
                window, interior, (((0,), (0,)), ((), ())), preferred_element_type=jnp.float32
            )
            kernel_row.append(weight_term)
        kernel_rows.append(jnp.stack(kernel_row))
    return (input_acc.reshape(tile_rows, tile_cols, in_channels), jnp.stack(kernel_rows))


def body(query_features, key_features, pyramid_grad, query_image, key_image, conv_weight):
    norm_scale = D ** (-0.5)
    strip_rows, width_cells, channels = query_features.shape
    key_rows = key_features.shape[1]
    queries = query_features.reshape(strip_rows * width_cells, channels)
    strip_grads = pyramid_grad.reshape(pyramid_grad.shape[0], pyramid_grad.shape[2])
    pooled = pool_levels(key_features)
    query_part = jnp.zeros((queries.shape[0], channels), jnp.float32)
    coarse_sum = jnp.zeros((width_cells, key_rows, channels), jnp.float32)
    level_zero = None
    offset = 0
    for level_index in range(LEVELS):
        factor = 2**level_index
        grid_rows = key_rows // factor
        grid_cols = width_cells // factor
        cell_count = grid_rows * grid_cols
        grad_block = strip_grads[:, offset : offset + cell_count]
        offset = offset + cell_count
        ordered = jnp.transpose(pooled[level_index], (1, 0, 2)).reshape(cell_count, channels)
        query_part = query_part + jnp.dot(grad_block, ordered, preferred_element_type=jnp.float32)
        if level_index == 0:
            level_zero = grad_block.reshape(-1, grid_rows, grid_cols)
        else:
            coarse = lax.dot_general(
                grad_block, queries, (((0,), (0,)), ((), ())), preferred_element_type=jnp.float32
            )
            coarse = jnp.transpose(coarse.reshape(grid_rows, grid_cols, channels), (1, 0, 2))
            spread = jnp.broadcast_to(
                coarse[:, None, :, None, :], (grid_cols, factor, grid_rows, factor, channels)
            ).reshape(width_cells, key_rows, channels)
            coarse_sum = coarse_sum + spread / 4.0**level_index
    query_grad = lax.psum_scatter(
        (query_part * norm_scale).reshape(strip_rows, width_cells, channels),
        "ka",
        scatter_dimension=1,
        tiled=True,
    ).astype(jnp.bfloat16)
    fine_term = jnp.einsum("qhw,qd->whd", level_zero, queries, preferred_element_type=jnp.float32)
    key_grad = lax.psum_scatter(
        (fine_term + coarse_sum) * norm_scale, "pb", scatter_dimension=0, tiled=True
    ).astype(jnp.bfloat16)
    padded_query_image, padded_query_grad, padded_key_image, padded_key_grad = (
        padded(query_image, (("pb", 0), ("ka", 1)), 1),
        padded(query_grad, (("pb", 0), ("ka", 1)), 1),
        padded(key_image, (("pb", 0), ("ka", 1)), 1),
        padded(key_grad, (("pb", 0), ("ka", 1)), 1),
    )
    kernel_swapped = jnp.transpose(conv_weight, (1, 0, 2, 3))
    grad_first, weight_first = conv_backward(padded_query_image, padded_query_grad, conv_weight)
    grad_second, weight_swapped = conv_backward(padded_key_image, padded_key_grad, kernel_swapped)
    local_weight = weight_first + jnp.transpose(weight_swapped, (1, 0, 2, 3))
    weight_grad = lax.psum(local_weight, ("pb", "ka"))
    return (grad_first.astype(jnp.bfloat16), grad_second.astype(jnp.bfloat16), weight_grad)


def solution(mesh):
    placed = (
        P("pb", None, None),
        P(None, "ka", None),
        P("pb", "ka", None),
        P("pb", "ka", None),
        P("pb", "ka", None),
        P(),
    )
    return jax.shard_map(
        body,
        mesh=mesh,
        in_specs=placed,
        out_specs=(P("pb", "ka", None), P("pb", "ka", None), P()),
        check_vma=False,
    )
```

profile of v0, /device:TPU:0, one launch (start us, length us, event | category | flops | bytes accessed | tf_op | source)
XLA Modules:
  0.0 261.9 jit_solution(2991542261399580980)
XLA Ops:
  9.5 2.3 collective-permute-start.12
  11.8 1.3 collective-permute-start.13
  13.1 2.6 reshape.145
  17.8 1.9 reduce_sum.39
  21.1 3.4 %fusion.2 = f32[768,256]{1,0:T(8,128)} fusion(bf16[1536,256]{1,0:T(8,128)(2,1)S(1)} %bitcast.276, bf16[768,2040]{0,1:T(8,128)(2,1)} %bitcast.279), kind=kOutput, calls=%fused_computation.4 | convolution fusion | flops 603979776 | bytes 3932160 | tf_op jit(solution)/shard_map/dot_general | solution.py:90
  25.6 2.4 reduce_sum.38
  29.1 2.7 %fusion.7 = f32[768,256]{1,0:T(8,128)} fusion(f32[768,256]{1,0:T(8,128)S(1)} %convolution_bitcast_fusion.1, f32[768,256]{1,0:T(8,128)S(1)} %convolution_bitcast_fusion.2, f32[768,256]{1,0:T(8,128)} %fusion.2, bf16[384,256]{1,0:T(8,128)(2,1)S(1)} %bitcast.277, bf16[768,2040]{0,1:T(8,128)(2,1)} %bitcast.281), kind=kOutput, calls=%fused_computation.11 | convolution fusion | flops 151781376 | bytes 3932160 | tf_op jit(solution)/shard_map/dot_general | solution.py:90
  32.5 5.7 %collective-permute-start.8 = (bf16[1,48,256]{2,1,0:T(8,128)(2,1)}, bf16[1,48,256]{2,1,0:T(8,128)(2,1)}, u32[]{:S(2)}, u32[]{:S(2)}) collective-permute-start(bf16[1,48,256]{2,1,0:T(8,128)(2,1)} %get-tuple-element.32), channel_id=1, source_target_pairs={{0,4},{4,8},{8,12},{12,16},{16,20},{20,24},{24,28},{1,5},{5,9},{9,... | collective-permute-start | bytes 73736 | tf_op jit(solution)/shard_map/ppermute | solution.py:18
  43.9 1.9 fusion
  49.1 1.7 div.61
  51.6 3.5 %collective-permute-start.14 = (bf16[26,1,256]{2,0,1:T(8,128)(2,1)S(1)}, bf16[26,1,256]{2,0,1:T(8,128)(2,1)S(1)}, u32[]{:S(2)}, u32[]{:S(2)}) collective-permute-start(bf16[26,1,256]{2,0,1:T(8,128)(2,1)S(1)} %get-tuple-element.23), channel_id=1, source_target_pairs={{0,1},{1,2},{2,3},{4,5},{5,6},{6,7},{8,9},{9,10},{10,11},{12,13},{... | collective-permute-start | bytes 39944 | tf_op jit(solution)/shard_map/ppermute | solution.py:18
  56.4 3.4 %add_multiply_fusion = f32[192,8,256]{2,0,1:T(8,128)} fusion(f32[192,8,256]{2,0,1:T(8,128)} %bitcast.275, f32[192,8,256]{2,0,1:T(8,128)S(1)} %div.57, f32[192,8,256]{2,0,1:T(8,128)} %div.61, f32[192,256]{1,0:T(8,128)} %broadcast_bitcast_fusion), kind=kLoop, calls=%fused_computation.6 | loop fusion | flops 1572864 | bytes 6488064 | tf_op jit(solution)/shard_map/mul | solution.py:110
  64.3 5.1 %collective-permute-start.10 = (bf16[6,1,256]{2,1,0:T(2,128)(2,1)S(1)}, bf16[6,1,256]{2,1,0:T(2,128)(2,1)S(1)}, u32[]{:S(2)}, u32[]{:S(2)}) collective-permute-start(bf16[6,1,256]{2,1,0:T(2,128)(2,1)S(1)} %get-tuple-element.9), channel_id=1, source_target_pairs={{0,1},{1,2},{2,3},{4,5},{5,6},{6,7},{8,9},{9,10},{10,11},{12,13},{... | collective-permute-start | bytes 9224 | tf_op jit(solution)/shard_map/ppermute | solution.py:18
  70.6 2.9 %collective-permute-start = (bf16[1,48,256]{2,1,0:T(8,128)(2,1)S(1)}, bf16[1,48,256]{2,1,0:T(8,128)(2,1)S(1)}, u32[]{:S(2)}, u32[]{:S(2)}) collective-permute-start(bf16[1,48,256]{2,1,0:T(8,128)(2,1)S(1)} %get-tuple-element.39), channel_id=1, source_target_pairs={{0,4},{4,8},{8,12},{12,16},{16,20},{20,24},{24,28},{1,5},{5,9},{9,... | collective-permute-start | bytes 73736 | tf_op jit(solution)/shard_map/ppermute | solution.py:18
  73.4 1.5 collective-permute-start.1
  79.6 1.3 collective-permute-start.2
  80.9 4.5 %collective-permute-start.3 = (bf16[6,1,256]{2,1,0:T(2,128)(2,1)S(1)}, bf16[6,1,256]{2,1,0:T(2,128)(2,1)S(1)}, u32[]{:S(2)}, u32[]{:S(2)}) collective-permute-start(bf16[6,1,256]{2,1,0:T(2,128)(2,1)S(1)} %get-tuple-element.20), channel_id=1, source_target_pairs={{0,1},{1,2},{2,3},{4,5},{5,6},{6,7},{8,9},{9,10},{10,11},{12,13},{... | collective-permute-start | bytes 9224 | tf_op jit(solution)/shard_map/ppermute | solution.py:18
  89.2 14.2 %reduce-scatter.5.cloned.1.call-done = f32[24,8,256]{2,0,1:T(8,128)} async-done(((f32[192,8,256]{2,0,1:T(8,128)}), f32[24,8,256]{2,0,1:T(8,128)}) %reduce-scatter.5.cloned.1.call-update) | async-done | bytes 196624 | tf_op jit(solution)/shard_map/reduce_scatter | solution.py:109
  107.1 1.7 collective-permute-start.4
  111.8 1.7 maximum_add_fusion
  114.8 4.5 %collective-permute-start.7 = (bf16[26,1,256]{2,0,1:T(8,128)(2,1)S(1)}, bf16[26,1,256]{2,0,1:T(8,128)(2,1)S(1)}, u32[]{:S(2)}, u32[]{:S(2)}) collective-permute-start(bf16[26,1,256]{2,0,1:T(8,128)(2,1)S(1)} %get-tuple-element.27), channel_id=1, source_target_pairs={{0,1},{1,2},{2,3},{4,5},{5,6},{6,7},{8,9},{9,10},{10,11},{12,13},{... | collective-permute-start | bytes 39944 | tf_op jit(solution)/shard_map/ppermute | solution.py:18
  119.5 1.3 collective-permute-done.7
  123.6 128.5 %all-reduce.2.cloned.1.call-done = f32[3,3,256,256]{3,2,1,0:T(8,128)} async-done(((f32[3,3,256,256]{3,2,1,0:T(8,128)}), f32[3,3,256,256]{3,2,1,0:T(8,128)}) %all-reduce.2.cloned.1.call-update) | async-done | bytes 2359312 | tf_op jit(solution)/shard_map/psum | solution.py:122
  252.1 3.2 %copy.135 = f32[3,3,256,256]{3,2,1,0:T(8,128)} copy(f32[3,3,256,256]{3,2,1,0:T(8,128)} %all-reduce.2.cloned.1.call-done) | data formatting | bytes 4718592
  (131 shorter events, 44.1 us)
Async XLA Ops:
  7.2 32.3 %copy-start = (bf16[4,192,256]{2,1,0:T(8,128)(2,1)S(1)}, bf16[4,192,256]{2,1,0:T(8,128)(2,1)}, u32[]{:S(2)}) copy-start(bf16[4,192,256]{2,1,0:T(8,128)(2,1)} %param.6) | copy-start | bytes 1179652
  7.2 8.6 %copy-start.1 = (bf16[192,8,256]{2,1,0:T(8,128)(2,1)S(1)}, bf16[192,8,256]{2,1,0:T(8,128)(2,1)}, u32[]{:S(2)}) copy-start(bf16[192,8,256]{2,1,0:T(8,128)(2,1)} %param.7) | copy-start | bytes 2359300
  7.2 62.2 %reduce-scatter.3.cloned.1.call-start = ((), (), s32[]{:S(2)}) async-start(), calls=%async_computation.2 | async-start | bytes 983040 | tf_op jit(solution)/shard_map/reduce_scatter | solution.py:102
  9.5 41.3 %collective-permute-start.12 = (bf16[1,8,256]{2,0,1:T(2,128)(2,1)}, bf16[1,8,256]{2,0,1:T(2,128)(2,1)S(1)}, u32[]{:S(2)}, u32[]{:S(2)}) collective-permute-start(bf16[1,8,256]{2,0,1:T(2,128)(2,1)} %get-tuple-element.29), channel_id=1, source_target_pairs={{0,4},{4,8},{8,12},{12,16},{16,20},{20,24},{24,28},{1,5},{5,9},{9,... | collective-permute-start | bytes 12296 | tf_op jit(solution)/shard_map/ppermute | solution.py:18
  11.8 39.0 %collective-permute-start.13 = (bf16[1,8,256]{2,0,1:T(2,128)(2,1)}, bf16[1,8,256]{2,0,1:T(2,128)(2,1)S(1)}, u32[]{:S(2)}, u32[]{:S(2)}) collective-permute-start(bf16[1,8,256]{2,0,1:T(2,128)(2,1)} %get-tuple-element.30), channel_id=1, source_target_pairs={{4,0},{8,4},{12,8},{16,12},{20,16},{24,20},{28,24},{5,1},{9,5},{13... | collective-permute-start | bytes 12296 | tf_op jit(solution)/shard_map/ppermute | solution.py:20
  21.1 3.4 %copy-start.6 = (f32[192,256]{1,0:T(8,128)S(1)}, f32[192,256]{1,0:T(8,128)}, u32[]{:S(2)}) copy-start(f32[192,256]{1,0:T(8,128)} %convert_reduce_fusion) | copy-start | bytes 589828
  31.8 71.7 %reduce-scatter.5.cloned.1.call-start = ((), (), s32[]{:S(2)}) async-start(), calls=%async_computation.3 | async-start | bytes 1769472 | tf_op jit(solution)/shard_map/reduce_scatter | solution.py:109
  32.5 28.9 %collective-permute-start.8 = (bf16[1,48,256]{2,1,0:T(8,128)(2,1)}, bf16[1,48,256]{2,1,0:T(8,128)(2,1)}, u32[]{:S(2)}, u32[]{:S(2)}) collective-permute-start(bf16[1,48,256]{2,1,0:T(8,128)(2,1)} %get-tuple-element.32), channel_id=1, source_target_pairs={{0,4},{4,8},{8,12},{12,16},{16,20},{20,24},{24,28},{1,5},{5,9},{9,... | collective-permute-start | bytes 73736 | tf_op jit(solution)/shard_map/ppermute | solution.py:18
  38.2 24.0 %collective-permute-start.9 = (bf16[1,48,256]{2,1,0:T(8,128)(2,1)}, bf16[1,48,256]{2,1,0:T(8,128)(2,1)}, u32[]{:S(2)}, u32[]{:S(2)}) collective-permute-start(bf16[1,48,256]{2,1,0:T(8,128)(2,1)} %get-tuple-element.31), channel_id=1, source_target_pairs={{4,0},{8,4},{12,8},{16,12},{20,16},{24,20},{28,24},{5,1},{9,5},{13... | collective-permute-start | bytes 73736 | tf_op jit(solution)/shard_map/ppermute | solution.py:20
  40.4 3.4 %copy-start.7 = (bf16[768,1,2040]{0,2,1:T(8,128)(2,1)S(1)}, bf16[768,1,2040]{0,2,1:T(8,128)(2,1)}, u32[]{:S(2)}) copy-start(bf16[768,1,2040]{0,2,1:T(8,128)(2,1)} %param.8) | copy-start | bytes 9400324
  51.6 8.2 %collective-permute-start.14 = (bf16[26,1,256]{2,0,1:T(8,128)(2,1)S(1)}, bf16[26,1,256]{2,0,1:T(8,128)(2,1)S(1)}, u32[]{:S(2)}, u32[]{:S(2)}) collective-permute-start(bf16[26,1,256]{2,0,1:T(8,128)(2,1)S(1)} %get-tuple-element.23), channel_id=1, source_target_pairs={{0,1},{1,2},{2,3},{4,5},{5,6},{6,7},{8,9},{9,10},{10,11},{12,13},{... | collective-permute-start | bytes 39944 | tf_op jit(solution)/shard_map/ppermute | solution.py:18
  55.1 5.6 %collective-permute-start.15 = (bf16[26,1,256]{2,0,1:T(8,128)(2,1)S(1)}, bf16[26,1,256]{2,0,1:T(8,128)(2,1)S(1)}, u32[]{:S(2)}, u32[]{:S(2)}) collective-permute-start(bf16[26,1,256]{2,0,1:T(8,128)(2,1)S(1)} %get-tuple-element.24), channel_id=1, source_target_pairs={{1,0},{2,1},{3,2},{5,4},{6,5},{7,6},{9,8},{10,9},{11,10},{13,12},{... | collective-permute-start | bytes 39944 | tf_op jit(solution)/shard_map/ppermute | solution.py:20
  59.8 192.4 %all-reduce.2.cloned.1.call-start = ((), (), s32[]{:S(2)}) async-start(), calls=%async_computation.4 | async-start | bytes 4718592 | tf_op jit(solution)/shard_map/psum | solution.py:122
  63.0 12.0 %collective-permute-start.11 = (bf16[6,1,256]{2,1,0:T(2,128)(2,1)S(1)}, bf16[6,1,256]{2,1,0:T(2,128)(2,1)S(1)}, u32[]{:S(2)}, u32[]{:S(2)}) collective-permute-start(bf16[6,1,256]{2,1,0:T(2,128)(2,1)S(1)} %get-tuple-element.10), channel_id=1, source_target_pairs={{1,0},{2,1},{3,2},{5,4},{6,5},{7,6},{9,8},{10,9},{11,10},{13,12},{... | collective-permute-start | bytes 9224 | tf_op jit(solution)/shard_map/ppermute | solution.py:20
  64.3 11.2 %collective-permute-start.10 = (bf16[6,1,256]{2,1,0:T(2,128)(2,1)S(1)}, bf16[6,1,256]{2,1,0:T(2,128)(2,1)S(1)}, u32[]{:S(2)}, u32[]{:S(2)}) collective-permute-start(bf16[6,1,256]{2,1,0:T(2,128)(2,1)S(1)} %get-tuple-element.9), channel_id=1, source_target_pairs={{0,1},{1,2},{2,3},{4,5},{5,6},{6,7},{8,9},{9,10},{10,11},{12,13},{... | collective-permute-start | bytes 9224 | tf_op jit(solution)/shard_map/ppermute | solution.py:18
  70.6 8.9 %collective-permute-start = (bf16[1,48,256]{2,1,0:T(8,128)(2,1)S(1)}, bf16[1,48,256]{2,1,0:T(8,128)(2,1)S(1)}, u32[]{:S(2)}, u32[]{:S(2)}) collective-permute-start(bf16[1,48,256]{2,1,0:T(8,128)(2,1)S(1)} %get-tuple-element.39), channel_id=1, source_target_pairs={{0,4},{4,8},{8,12},{12,16},{16,20},{20,24},{24,28},{1,5},{5,9},{9,... | collective-permute-start | bytes 73736 | tf_op jit(solution)/shard_map/ppermute | solution.py:18
  73.4 6.1 %collective-permute-start.1 = (bf16[1,48,256]{2,1,0:T(8,128)(2,1)S(1)}, bf16[1,48,256]{2,1,0:T(8,128)(2,1)S(1)}, u32[]{:S(2)}, u32[]{:S(2)}) collective-permute-start(bf16[1,48,256]{2,1,0:T(8,128)(2,1)S(1)} %get-tuple-element.40), channel_id=1, source_target_pairs={{4,0},{8,4},{12,8},{16,12},{20,16},{24,20},{28,24},{5,1},{9,5},{13... | collective-permute-start | bytes 73736 | tf_op jit(solution)/shard_map/ppermute | solution.py:20
  78.1 7.3 %copy-start.2 = (bf16[3,3,256,256]{3,2,1,0:T(8,128)(2,1)S(1)}, bf16[3,3,256,256]{3,2,1,0:T(8,128)(2,1)}, u32[]{:S(2)}) copy-start(bf16[3,3,256,256]{3,2,1,0:T(8,128)(2,1)} %param.11) | copy-start | bytes 3538948
  79.6 6.1 %collective-permute-start.2 = (bf16[6,1,256]{2,1,0:T(2,128)(2,1)S(1)}, bf16[6,1,256]{2,1,0:T(2,128)(2,1)S(1)}, u32[]{:S(2)}, u32[]{:S(2)}) collective-permute-start(bf16[6,1,256]{2,1,0:T(2,128)(2,1)S(1)} %get-tuple-element.19), channel_id=1, source_target_pairs={{1,0},{2,1},{3,2},{5,4},{6,5},{7,6},{9,8},{10,9},{11,10},{13,12},{... | collective-permute-start | bytes 9224 | tf_op jit(solution)/shard_map/ppermute | solution.py:20
  80.9 5.9 %collective-permute-start.3 = (bf16[6,1,256]{2,1,0:T(2,128)(2,1)S(1)}, bf16[6,1,256]{2,1,0:T(2,128)(2,1)S(1)}, u32[]{:S(2)}, u32[]{:S(2)}) collective-permute-start(bf16[6,1,256]{2,1,0:T(2,128)(2,1)S(1)} %get-tuple-element.20), channel_id=1, source_target_pairs={{0,1},{1,2},{2,3},{4,5},{5,6},{6,7},{8,9},{9,10},{10,11},{12,13},{... | collective-permute-start | bytes 9224 | tf_op jit(solution)/shard_map/ppermute | solution.py:18
  107.1 6.4 %collective-permute-start.4 = (bf16[1,8,256]{2,0,1:T(2,128)(2,1)S(1)}, bf16[1,8,256]{2,0,1:T(2,128)(2,1)S(1)}, u32[]{:S(2)}, u32[]{:S(2)}) collective-permute-start(bf16[1,8,256]{2,0,1:T(2,128)(2,1)S(1)} %get-tuple-element.35), channel_id=1, source_target_pairs={{0,4},{4,8},{8,12},{12,16},{16,20},{20,24},{24,28},{1,5},{5,9},{9,... | collective-permute-start | bytes 12296 | tf_op jit(solution)/shard_map/ppermute | solution.py:18
  108.8 4.7 %collective-permute-start.5 = (bf16[1,8,256]{2,0,1:T(2,128)(2,1)S(1)}, bf16[1,8,256]{2,0,1:T(2,128)(2,1)S(1)}, u32[]{:S(2)}, u32[]{:S(2)}) collective-permute-start(bf16[1,8,256]{2,0,1:T(2,128)(2,1)S(1)} %get-tuple-element.36), channel_id=1, source_target_pairs={{4,0},{8,4},{12,8},{16,12},{20,16},{24,20},{28,24},{5,1},{9,5},{13... | collective-permute-start | bytes 12296 | tf_op jit(solution)/shard_map/ppermute | solution.py:20
  113.5 5.9 %collective-permute-start.6 = (bf16[26,1,256]{2,0,1:T(8,128)(2,1)S(1)}, bf16[26,1,256]{2,0,1:T(8,128)(2,1)S(1)}, u32[]{:S(2)}, u32[]{:S(2)}) collective-permute-start(bf16[26,1,256]{2,0,1:T(8,128)(2,1)S(1)} %get-tuple-element.28), channel_id=1, source_target_pairs={{1,0},{2,1},{3,2},{5,4},{6,5},{7,6},{9,8},{10,9},{11,10},{13,12},{... | collective-permute-start | bytes 39944 | tf_op jit(solution)/shard_map/ppermute | solution.py:20
  114.8 6.0 %collective-permute-start.7 = (bf16[26,1,256]{2,0,1:T(8,128)(2,1)S(1)}, bf16[26,1,256]{2,0,1:T(8,128)(2,1)S(1)}, u32[]{:S(2)}, u32[]{:S(2)}) collective-permute-start(bf16[26,1,256]{2,0,1:T(8,128)(2,1)S(1)} %get-tuple-element.27), channel_id=1, source_target_pairs={{0,1},{1,2},{2,3},{4,5},{5,6},{6,7},{8,9},{9,10},{10,11},{12,13},{... | collective-permute-start | bytes 39944 | tf_op jit(solution)/shard_map/ppermute | solution.py:18
  (7 other events, 12.4 us)
Sparse Core Ops, SparseCore 0:
  31.9 27.9 reduce-scatter.2
  63.7 39.6 reduce-scatter.4
  113.6 138.4 all-reduce.1
where the time goes:
time: 263 us; the launch traced here: 262 us
  waiting for transfers between devices  146 us (56%)
  starting transfers between devices  40.9 us (16%)
  matrix products  24.1 us (9%)
  local copies, waits for them, and re-layouts  19.6 us (7%)
  other arithmetic  16.6 us (6%)
  between operations  14.4 us (5%)
    psum x1, waiting for transfers between devices, body(): weight_grad = lax.psum(local_weight, ('pb', 'ka'))  128 us
    ppermute x8, starting transfers between devices, padded(): lax.ppermute(tail, axis, [(i, (i + 1) % count) for i in range(ends)])  30.3 us
    reduce_scatter x1, waiting for transfers between devices, body(): lax.psum_scatter((fine_term + coarse_sum) * norm_scale, 'pb', scatter_dim...  14.2 us
    ppermute x8, starting transfers between devices, padded(): lax.ppermute(head, axis, [((i + 1) % count, i) for i in range(ends)])  10.5 us
    dot_general x4, matrix products, body(): jnp.dot(grad_block, ordered, preferred_element_type=jnp.float32)  8.37 us
    unnamed x29, local copies, waits for them, and re-layouts  6.82 us
    dot_general x18, matrix products, conv_backward(): lax.dot_general(window, interior, (((0,), (0,)), ((), ())), preferred_ele...  6.57 us
    reduce_sum x4, other arithmetic, pool_levels(): pooled = strip_float.reshape(cell_cols // factor, factor, key_rows // fac...  5.52 us
  transfers between devices with their start and end apart: 19, of which 5 were waited for; matrix products, arithmetic and copies ran while one was open for 19% of the time, Pallas kernels for 0%

commit v1 on v0

v1 whole, which is shorter than its diff:
```python
import functools

import jax
import jax.numpy as jnp
from jax import lax
from jax.experimental import pallas as pl
from jax.experimental.pallas import tpu as pltpu
from jax.sharding import PartitionSpec as P

LEVELS = 4
F32 = jnp.float32
BF16 = jnp.bfloat16
VMEM_BYTES = 56 * 2**20


def flip(count, mask):
    return [(i, i ^ mask) for i in range(count)]


def ordered(parts, index):
    count = len(parts)
    bit = 1
    while bit < count:
        swap = (index & bit) != 0
        parts = [jnp.where(swap, parts[a ^ bit], parts[a]) for a in range(count)]
        bit *= 2
    return parts


def pick(blocks, index):
    return lax.dynamic_index_in_dim(blocks, index, 0, keepdims=False)


def put(ref, rows, value):
    for lane in range(ref.shape[0]):
        ref[lane, rows, :] = value[:, lane * 128 : (lane + 1) * 128]


def get(ref, rows):
    return jnp.concatenate([ref[lane, rows, :] for lane in range(ref.shape[0])], axis=1)


def corr_kernel(width, key_rows, tile_q, tile_k, n_ka, n_quad, a_ref, q_ref, key_ref, *rest):
    q_outs = rest[:n_ka]
    send_ref, keep_ref, cells_ref, cells16_ref, coarse_ref, keyf_ref, tmp_ref, kpad_ref, qpad_ref, stage_ref = rest[n_ka:]
    step = pl.program_id(0)
    steps = pl.num_programs(0)
    channels = q_ref.shape[1]
    scale = channels ** (-0.5)
    z = lax.axis_index("ka")
    pb = lax.axis_index("pb")
    core = pb % 2
    quad = pb // 2

    @pl.when(step == 0)
    def _():
        put(keyf_ref, slice(None), key_ref[...].astype(F32))
        rows = [get(keyf_ref, pl.ds(r, width, stride=key_rows)) for r in range(key_rows)]
        offset = 0
        for level in range(LEVELS):
            w = width >> level
            if level:
                pairs = []
                for i in range(len(rows) // 2):
                    put(tmp_ref, slice(0, 2 * w), rows[2 * i] + rows[2 * i + 1])
                    pairs.append(get(tmp_ref, pl.ds(0, w, stride=2)) + get(tmp_ref, pl.ds(1, w, stride=2)))
                rows = pairs
            for row in rows:
                cells_ref[offset : offset + w, :] = row * (4.0**-level)
                offset += w
        cells16_ref[...] = cells_ref[...].astype(BF16)
        coarse_ref[...] = jnp.zeros_like(coarse_ref)
        qpad_ref[...] = jnp.zeros_like(qpad_ref)

    grads = a_ref[...]
    query = lax.dot_general(grads, cells16_ref[...], (((0,), (0,)), ((), ())), preferred_element_type=F32) * scale
    coarse_ref[...] += jnp.dot(grads, q_ref[...], preferred_element_type=F32)
    for half in range(q_ref.shape[0] // width):
        qpad_ref[8 : 8 + width, :] = query[half * width : (half + 1) * width]
        for k in range(n_ka):
            stage_ref[z ^ k, 0 : tile_q + 2, :] = qpad_ref[7 + tile_q * k : 9 + tile_q * (k + 1), :]
        for s in range(n_ka):
            q_outs[s][half] = stage_ref[s, 0 : tile_q + 2, :].astype(BF16)

    @pl.when(step == steps - 1)
    def _():
        offsets = [0]
        for level in range(LEVELS):
            offsets.append(offsets[-1] + (key_rows >> level) * (width >> level))
        finer = None
        for level in reversed(range(LEVELS)):
            w = width >> level
            here = []
            for r in range(key_rows >> level):
                start = offsets[level] + r * w
                value = coarse_ref[start : start + w, :] * (scale * 4.0**-level)
                if finer is not None:
                    value = value + finer[r // 2]
                here.append(value)
            if level:
                finer = []
                for value in here:
                    put(tmp_ref, pl.ds(0, w, stride=2), value)
                    put(tmp_ref, pl.ds(1, w, stride=2), value)
                    finer.append(get(tmp_ref, slice(0, 2 * w)))
        edge = jnp.zeros((key_rows, channels), F32)
        put(kpad_ref, slice(0, key_rows), edge)
        put(kpad_ref, slice((width + 1) * key_rows, (width + 2) * key_rows), edge)
        for r in range(key_rows):
            put(kpad_ref, pl.ds(key_rows + r, width, stride=key_rows), here[r])
        size = (tile_k + 2) * key_rows
        for s in range(n_quad):
            first = (quad ^ s) * 2 * tile_k * key_rows
            mine = pl.multiple_of(first + core * tile_k * key_rows, 8)
            other = pl.multiple_of(first + (1 - core) * tile_k * key_rows, 8)
            keep_ref[s] = get(kpad_ref, pl.ds(mine, size))
            send_ref[s] = get(kpad_ref, pl.ds(other, size)).astype(BF16)


def correlate(grads, queries, keys, width, key_rows, n_ka, n_quad):
    cells, count = grads.shape
    channels = queries.shape[1]
    rows = count // width
    tile_q = width // n_ka
    tile_k = width // (2 * n_quad)
    step_rows = 2
    size = (tile_k + 2) * key_rows
    whole2 = lambda i: (0, 0)
    whole3 = lambda i: (0, 0, 0)
    return pl.pallas_call(
        functools.partial(corr_kernel, width, key_rows, tile_q, tile_k, n_ka, n_quad),
        grid=(rows // step_rows,),
        in_specs=[
            pl.BlockSpec((cells, step_rows * width), lambda i: (0, i)),
            pl.BlockSpec((step_rows * width, channels), lambda i: (i, 0)),
            pl.BlockSpec((width * key_rows, channels), whole2),
        ],
        out_specs=[pl.BlockSpec((step_rows, tile_q + 2, channels), lambda i: (i, 0, 0))] * n_ka
        + [pl.BlockSpec((n_quad, size, channels), whole3)] * 2,
        out_shape=[jax.ShapeDtypeStruct((rows, tile_q + 2, channels), BF16)] * n_ka
        + [
            jax.ShapeDtypeStruct((n_quad, size, channels), BF16),
            jax.ShapeDtypeStruct((n_quad, size, channels), F32),
        ],
        scratch_shapes=[
            pltpu.VMEM((cells, channels), F32),
            pltpu.VMEM((cells, channels), BF16),
            pltpu.VMEM((cells, channels), F32),
            pltpu.VMEM((channels // 128, width * key_rows, 128), F32),
            pltpu.VMEM((channels // 128, width, 128), F32),
            pltpu.VMEM((channels // 128, (width + 2) * key_rows, 128), F32),
            pltpu.VMEM((width + 16, channels), F32),
            pltpu.VMEM((n_ka, tile_q + 8, channels), F32),
        ],
        compiler_params=pltpu.CompilerParams(vmem_limit_bytes=VMEM_BYTES),
        name="correlate",
    )(grads, queries, keys)


def fill(gq_ref, gtop_ref, gbot_ref, gk_ref, ktop_ref, kbot_ref, qext_ref, kext_ref):
    rows, wide, channels = gq_ref.shape
    tall = ktop_ref.shape[0]
    key_rows = gk_ref.shape[0] // tall
    qext_ref[0:1, 0:wide, :] = gtop_ref[...].astype(F32)
    qext_ref[1 : rows + 1, 0:wide, :] = gq_ref[...].astype(F32)
    qext_ref[rows + 1 : rows + 2, 0:wide, :] = gbot_ref[...].astype(F32)
    kext_ref[:, 8 : 8 + key_rows, :] = gk_ref[...].astype(F32).reshape(tall, key_rows, channels)
    kext_ref[:, 7:8, :] = ktop_ref[...].astype(F32)
    kext_ref[:, 8 + key_rows : 9 + key_rows, :] = kbot_ref[...].astype(F32)


def shifted(qext_ref, kext_ref, rows, tile_q, tile_k, key_rows, a, b):
    channels = qext_ref.shape[2]
    first = qext_ref[1 - a : 1 - a + rows, 1 - b : 1 - b + tile_q, :].reshape(rows * tile_q, channels)
    second = kext_ref[1 - b : 1 - b + tile_k, 8 - a : 8 - a + key_rows, :].reshape(tile_k * key_rows, channels)
    return jnp.concatenate([first.astype(BF16), second.astype(BF16)], axis=0)


def weight_kernel(gq, gtop, gbot, gk, ktop, kbot, qi_ref, ki_ref, send_ref, keep_ref, qext_ref, kext_ref, acc_ref):
    rows, wide, channels = gq.shape
    tall = ktop.shape[0]
    key_rows = gk.shape[0] // tall
    fill(gq, gtop, gbot, gk, ktop, kbot, qext_ref, kext_ref)
    cin = qi_ref.shape[1]
    image = jnp.concatenate([qi_ref[...].astype(F32).T, ki_ref[...].astype(F32).T], axis=1).astype(BF16)
    for tap in range(9):
        a, b = tap // 3 - 1, tap % 3 - 1
        grad = shifted(qext_ref, kext_ref, rows, wide - 2, tall - 2, key_rows, a, b)
        acc_ref[tap * cin : (tap + 1) * cin, :] = jnp.dot(image, grad, preferred_element_type=F32)
    half = send_ref.shape[0]
    core = lax.axis_index("pb") % 2
    keep_ref[...] = acc_ref[pl.ds(pl.multiple_of(core * half, 8), half), :]
    send_ref[...] = acc_ref[pl.ds(pl.multiple_of((1 - core) * half, 8), half), :].astype(BF16)


def image_kernel(gq, gtop, gbot, gk, ktop, kbot, w_ref, qo_ref, ko_ref, qext_ref, kext_ref):
    rows, wide, channels = gq.shape
    tall = ktop.shape[0]
    key_rows = gk.shape[0] // tall
    fill(gq, gtop, gbot, gk, ktop, kbot, qext_ref, kext_ref)
    total = None
    for tap in range(9):
        a, b = tap // 3 - 1, tap % 3 - 1
        grad = shifted(qext_ref, kext_ref, rows, wide - 2, tall - 2, key_rows, a, b)
        part = lax.dot_general(grad, w_ref[tap], (((1,), (1,)), ((), ())), preferred_element_type=F32)
        total = part if total is None else total + part
    count = qo_ref.shape[0]
    qo_ref[...] = total[:count].astype(BF16)
    ko_ref[...] = total[count:].astype(BF16)


def body(query_features, key_features, pyramid_grad, query_image, key_image, conv_weight):
    n_pb = lax.axis_size("pb")
    n_ka = lax.axis_size("ka")
    n_quad = n_pb // 2
    pb = lax.axis_index("pb")
    z = lax.axis_index("ka")
    core = pb % 2
    quad = pb // 2
    strip_rows, width, channels = query_features.shape
    key_rows = key_features.shape[1]
    cin = conv_weight.shape[2]
    tile_q = width // n_ka
    tile_k = width // n_pb
    sibling = flip(n_pb, 1)

    grads = jnp.transpose(pyramid_grad.reshape(pyramid_grad.shape[0], pyramid_grad.shape[2]))
    *q_parts, k_send, k_keep = correlate(
        grads,
        query_features.reshape(strip_rows * width, channels),
        key_features.reshape(width * key_rows, channels),
        width,
        key_rows,
        n_ka,
        n_quad,
    )
    k_recv = lax.ppermute(k_send, "pb", sibling)
    q_recv = [lax.ppermute(q_parts[s], "ka", flip(n_ka, s)) for s in range(1, n_ka)]
    k_pair = [k_keep[s] + k_recv[s].astype(F32) for s in range(n_quad)]
    k_more = [lax.ppermute(k_pair[s].astype(BF16), "pb", flip(n_pb, 2 * s)) for s in range(1, n_quad)]
    gq = sum([x.astype(F32) for x in q_recv], q_parts[0].astype(F32)).astype(BF16)
    gk = sum([x.astype(F32) for x in k_more], k_pair[0]).astype(BF16)

    first, last = gq[:1], gq[strip_rows - 1 :]
    lower = core == 0
    from_sibling = lax.ppermute(jnp.where(lower, last, first), "pb", sibling)
    links = [(i, i + 1) for i in range(1, n_pb - 1, 2)]
    from_remote = lax.ppermute(jnp.where(lower, first, last), "pb", links + [(d, s) for s, d in links])
    gtop = jnp.where(lower, from_remote, from_sibling)
    gbot = jnp.where(lower, from_sibling, from_remote)
    gk_rows = gk.reshape(tile_k + 2, key_rows, channels)
    ups = [(i, i + 1) for i in range(n_ka - 1)]
    ktop = lax.ppermute(gk_rows[:, key_rows - 1 :], "ka", ups)
    kbot = lax.ppermute(gk_rows[:, :1], "ka", [(d, s) for s, d in ups])

    around = (gq, gtop, gbot, gk, ktop, kbot)
    ext = [
        pltpu.VMEM((strip_rows + 2, tile_q + 16 - tile_q % 8, channels), F32),
        pltpu.VMEM((tile_k + 2, key_rows + 16, channels), F32),
    ]
    taps = 9
    half = taps * cin // 2
    w_send, w_keep = pl.pallas_call(
        weight_kernel,
        out_shape=[jax.ShapeDtypeStruct((half, channels), BF16), jax.ShapeDtypeStruct((half, channels), F32)],
        scratch_shapes=ext + [pltpu.VMEM((taps * cin, channels), F32)],
        compiler_params=pltpu.CompilerParams(vmem_limit_bytes=VMEM_BYTES),
        name="weights",
    )(*around, query_image.reshape(-1, cin), key_image.reshape(-1, cin))
    q_out, k_out = pl.pallas_call(
        image_kernel,
        out_shape=[jax.ShapeDtypeStruct((strip_rows * tile_q, cin), BF16), jax.ShapeDtypeStruct((tile_k * key_rows, cin), BF16)],
        scratch_shapes=ext,
        compiler_params=pltpu.CompilerParams(vmem_limit_bytes=VMEM_BYTES),
        name="images",
    )(*around, conv_weight.reshape(taps, cin, channels))

    pair = w_keep + lax.ppermute(w_send, "pb", sibling).astype(F32)
    pieces = pair.reshape(n_quad, half // n_quad, channels)
    got = [lax.ppermute(pick(pieces, quad ^ s).astype(BF16), "pb", flip(n_pb, 2 * s)) for s in range(1, n_quad)]
    part = sum([x.astype(F32) for x in got], pick(pieces, quad))
    pieces = part.reshape(n_ka, half // (n_quad * n_ka), channels)
    got = [lax.ppermute(pick(pieces, z ^ s).astype(BF16), "ka", flip(n_ka, s)) for s in range(1, n_ka)]
    part = sum([x.astype(F32) for x in got], pick(pieces, z)).astype(BF16)
    part = jnp.concatenate(
        ordered([part] + [lax.ppermute(part, "ka", flip(n_ka, s)) for s in range(1, n_ka)], z), axis=0
    )
    part = jnp.concatenate(
        ordered([part] + [lax.ppermute(part, "pb", flip(n_pb, 2 * s)) for s in range(1, n_quad)], quad), axis=0
    )
    whole = jnp.concatenate(ordered([part, lax.ppermute(part, "pb", sibling)], core), axis=0)
    weight_grad = whole.astype(F32).reshape(conv_weight.shape)
    return (
        q_out.reshape(query_image.shape),
        k_out.reshape(key_image.shape),
        weight_grad,
    )


def solution(mesh):
    placed = (
        P("pb", None, None),
        P(None, "ka", None),
        P("pb", "ka", None),
        P("pb", "ka", None),
        P("pb", "ka", None),
        P(),
    )
    return jax.shard_map(
        body,
        mesh=mesh,
        in_specs=placed,
        out_specs=(P("pb", "ka", None), P("pb", "ka", None), P()),
        check_vma=False,
    )
```

time: 263 us -> 93.6 us (0.36)
  waiting for transfers between devices: 146 us -> 37.4 us
  matrix products: 24.1 us -> 0 us
  local copies, waits for them, and re-layouts: 19.6 us -> 0.72 us
  between operations: 14.4 us -> 0.83 us
  Pallas kernels: 0 us -> 13.2 us
  other arithmetic: 16.6 us -> 7.55 us
  starting transfers between devices: 40.9 us -> 33.5 us
    psum x1 -> x0, waiting for transfers between devices: 128 us -> none  [body(): weight_grad = lax.psum(local_weight, ('pb', 'ka'))]
    ppermute x16 -> x25, waiting for transfers between devices: 3.34 us -> 37.4 us  [the longest x3 9.45 us: body(): lax.ppermute(q_parts[s], 'ka', flip(n_ka, s))]
    dot_general x43 -> x0, matrix products: 22.2 us -> none  [the longest x4 8.37 us: body(): jnp.dot(grad_block, ordered, preferred_element_type=jnp.float32)]
    reduce_scatter x2 -> x0, waiting for transfers between devices: 14.3 us -> none  [the longest x1 14.2 us: body(): lax.psum_scatter((fine_term + coarse_sum) * norm_scale, 'pb', scatter_dim...]
    pallas_call x0 -> x3, Pallas kernels: none -> 13.2 us  [the longest x1 6.76 us: correlate(): pl.pallas_call(functools.partial(corr_kernel, width, key_rows, tile_q, ti...]
    ppermute x16 -> x25, starting transfers between devices: 40.8 us -> 33.5 us  [the longest x3 5.42 us: body(): lax.ppermute(pick(pieces, z ^ s).astype(BF16), 'ka', flip(n_ka, s))]
    unnamed x29 -> x8, local copies, waits for them, and re-layouts: 6.82 us -> 0.61 us
    reduce_sum x4 -> x0, other arithmetic: 5.52 us -> none  [pool_levels(): pooled = strip_float.reshape(cell_cols // factor, factor, key_rows // fac...]
  transfers between devices with their start and end apart: 19 -> 25, of which waited for: 5 -> 17; matrix products, arithmetic and copies ran while one was open for 19% -> 3% of each run, Pallas kernels for 0% -> 3%
where the time goes in v1:
time: 93.6 us; the launch traced here: 93.2 us
  waiting for transfers between devices  37.4 us (40%)
  starting transfers between devices  33.5 us (36%)
  Pallas kernels  13.2 us (14%)
  other arithmetic  7.55 us (8%)
    ppermute x3, waiting for transfers between devices, body(): lax.ppermute(q_parts[s], 'ka', flip(n_ka, s))  9.45 us
    ppermute x3, waiting for transfers between devices, body(): lax.ppermute(pick(pieces, quad ^ s).astype(BF16), 'pb', flip(n_pb, 2 * s))  7.43 us
    pallas_call x1, Pallas kernels, correlate(): pl.pallas_call(functools.partial(corr_kernel, width, key_rows, tile_q, ti...  6.76 us
    ppermute x3, starting transfers between devices, body(): lax.ppermute(pick(pieces, z ^ s).astype(BF16), 'ka', flip(n_ka, s))  5.42 us
    ppermute x3, starting transfers between devices, body(): lax.ppermute(q_parts[s], 'ka', flip(n_ka, s))  5.24 us
    ppermute x1, starting transfers between devices, body(): ktop = lax.ppermute(gk_rows[:, key_rows - 1:], 'ka', ups)  5.15 us
    ppermute x3, waiting for transfers between devices, body(): lax.ppermute(pick(pieces, z ^ s).astype(BF16), 'ka', flip(n_ka, s))  5.12 us
    ppermute x3, waiting for transfers between devices, body(): lax.ppermute(part, 'pb', flip(n_pb, 2 * s))  5.09 us
  transfers between devices with their start and end apart: 25, of which 17 were waited for; matrix products, arithmetic and copies ran while one was open for 3% of the time, Pallas kernels for 3%

profile of v1, /device:TPU:0, one launch (start us, length us, event | category | flops | bytes accessed | tf_op | source)
XLA Modules:
  0.0 93.2 jit_solution(8941563077023546900)
XLA Ops:
  0.6 6.8 %correlate.1 = (bf16[4,50,256]{2,1,0:T(8,128)(2,1)}, bf16[4,50,256]{2,1,0:T(8,128)(2,1)}, bf16[4,50,256]{2,1,0:T(8,128)(2,1)}, bf16[4,50,256]{2,1,0:T(8,128)(2,1...) custom-call(bf16[2040,768]{1,0:T(8,128)(2,1)} %bitcast.56, bf16[768,256]{1,0:T(8,128)(2,1)} %bitcast.64, ...), custom_call_target="tpu_custom_call" | custom-call | tf_op jit(solution)/shard_map/correlate/pallas_call | solution.py:130
  7.9 2.6 %collective-permute-start = (bf16[4,50,256]{2,1,0:T(8,128)(2,1)}, bf16[4,50,256]{2,1,0:T(8,128)(2,1)S(1)}, u32[]{:S(2)}, u32[]{:S(2)}) collective-permute-start(bf16[4,50,256]{2,1,0:T(8,128)(2,1)} %get-tuple-element.14), channel_id=1, source_target_pairs={{0,1},{1,0},{2,3},{3,2},{4,5},{5,4},{6,7},{7,6},{8,9},{9,8},{10,11... | collective-permute-start | bytes 307208 | tf_op jit(solution)/shard_map/ppermute | solution.py:238
  10.6 2.6 %collective-permute-start.1 = (bf16[4,50,256]{2,1,0:T(8,128)(2,1)}, bf16[4,50,256]{2,1,0:T(8,128)(2,1)S(1)}, u32[]{:S(2)}, u32[]{:S(2)}) collective-permute-start(bf16[4,50,256]{2,1,0:T(8,128)(2,1)} %get-tuple-element.15), channel_id=1, source_target_pairs={{0,2},{1,3},{2,0},{3,1},{4,6},{5,7},{6,4},{7,5},{8,10},{9,11},{10,... | collective-permute-start | bytes 307208 | tf_op jit(solution)/shard_map/ppermute | solution.py:238
  14.5 8.1 %collective-permute-done.1 = bf16[4,50,256]{2,1,0:T(8,128)(2,1)S(1)} collective-permute-done((bf16[4,50,256]{2,1,0:T(8,128)(2,1)}, bf16[4,50,256]{2,1,0:T(8,128)(2,1)S(1)}, u32[]{:S(2)}, u32[]{:S(2)}) %collective-permute-start.1) | collective-permute-done | bytes 102432 | tf_op jit(solution)/shard_map/ppermute | solution.py:238
  24.8 1.6 %collective-permute-start.6 = (bf16[208,256]{1,0:T(8,128)(2,1)S(1)}, bf16[208,256]{1,0:T(8,128)(2,1)S(1)}, u32[]{:S(2)}, u32[]{:S(2)}) collective-permute-start(bf16[208,256]{1,0:T(8,128)(2,1)S(1)} %get-tuple-element.23), channel_id=1, source_target_pairs={{0,8},{4,12},{8,0},{12,4},{16,24},{20,28},{24,16},{28,20},{1,9},{5... | collective-permute-start | bytes 319496 | tf_op jit(solution)/shard_map/ppermute | solution.py:240
  26.4 1.5 %collective-permute-start.8 = (bf16[208,256]{1,0:T(8,128)(2,1)S(1)}, bf16[208,256]{1,0:T(8,128)(2,1)S(1)}, u32[]{:S(2)}, u32[]{:S(2)}) collective-permute-start(bf16[208,256]{1,0:T(8,128)(2,1)S(1)} %get-tuple-element.24), channel_id=1, source_target_pairs={{0,24},{4,28},{8,16},{12,20},{16,8},{20,12},{24,0},{28,4},{1,25},{... | collective-permute-start | bytes 319496 | tf_op jit(solution)/shard_map/ppermute | solution.py:240
  29.2 1.5 %collective-permute-done.6 = bf16[208,256]{1,0:T(8,128)(2,1)S(1)} collective-permute-done((bf16[208,256]{1,0:T(8,128)(2,1)S(1)}, bf16[208,256]{1,0:T(8,128)(2,1)S(1)}, u32[]{:S(2)}, u32[]{:S(2)}) %collective-permute-start.6) | collective-permute-done | bytes 106528 | tf_op jit(solution)/shard_map/ppermute | solution.py:240
  35.5 5.1 %collective-permute-start.9 = (bf16[26,1,256]{2,1,0:T(2,128)(2,1)S(1)}, bf16[26,1,256]{2,1,0:T(2,128)(2,1)S(1)}, u32[]{:S(2)}, u32[]{:S(2)}) collective-permute-start(bf16[26,1,256]{2,1,0:T(2,128)(2,1)S(1)} %get-tuple-element.44), channel_id=1, source_target_pairs={{0,1},{1,2},{2,3},{4,5},{5,6},{6,7},{8,9},{9,10},{10,11},{12,13},{... | collective-permute-start | bytes 39944 | tf_op jit(solution)/shard_map/ppermute | solution.py:253
  42.8 3.6 %weights.1 = (bf16[1152,256]{1,0:T(8,128)(2,1)}, f32[1152,256]{1,0:T(8,128)}) custom-call(bf16[4,50,256]{2,1,0:T(8,128)(2,1)} %copy-done, bf16[1,50,256]{2,1,0:T(8,128)(2,1)} %get-tuple-element.46.gtop, bf16[1,50,256]{2,1,0:T(8,128)(2,1)} %get-tuple-element.45.gbot, bf16[208,256]{1,0:T(8,128)(2,1)} %copy-done.1, bf16[26,1,256]{2,1,0:T(2,128)(2,1)} %copy-done.3, ...), custom_call_target="tpu_custom_call" | custom-call | tf_op jit(solution)/shard_map/weights/pallas_call | solution.py:263
  46.4 2.2 %collective-permute-done.11 = bf16[1152,256]{1,0:T(8,128)(2,1)S(1)} collective-permute-done((bf16[1152,256]{1,0:T(8,128)(2,1)}, bf16[1152,256]{1,0:T(8,128)(2,1)S(1)}, u32[]{:S(2)}, u32[]{:S(2)}) %collective-permute-start.11) | collective-permute-done | bytes 589856 | tf_op jit(solution)/shard_map/ppermute | solution.py:278
  50.1 1.5 %collective-permute-start.12 = (bf16[288,256]{1,0:T(8,128)(2,1)S(1)}, bf16[288,256]{1,0:T(8,128)(2,1)S(1)}, u32[]{:S(2)}, u32[]{:S(2)}) collective-permute-start(bf16[288,256]{1,0:T(8,128)(2,1)S(1)} %get-tuple-element.28), channel_id=1, source_target_pairs={{0,8},{4,12},{8,0},{12,4},{16,24},{20,28},{24,16},{28,20},{1,9},{5... | collective-permute-start | bytes 442376 | tf_op jit(solution)/shard_map/ppermute | solution.py:280
  53.7 3.2 %collective-permute-done.12 = bf16[288,256]{1,0:T(8,128)(2,1)S(1)} collective-permute-done((bf16[288,256]{1,0:T(8,128)(2,1)S(1)}, bf16[288,256]{1,0:T(8,128)(2,1)S(1)}, u32[]{:S(2)}, u32[]{:S(2)}) %collective-permute-start.12) | collective-permute-done | bytes 147488 | tf_op jit(solution)/shard_map/ppermute | solution.py:280
  56.9 2.9 %collective-permute-done.14 = bf16[288,256]{1,0:T(8,128)(2,1)S(1)} collective-permute-done((bf16[288,256]{1,0:T(8,128)(2,1)S(1)}, bf16[288,256]{1,0:T(8,128)(2,1)S(1)}, u32[]{:S(2)}, u32[]{:S(2)}) %collective-permute-start.14) | collective-permute-done | bytes 147488 | tf_op jit(solution)/shard_map/ppermute | solution.py:280
  61.2 2.4 %collective-permute-start.15 = (bf16[72,256]{1,0:T(8,128)(2,1)S(1)}, bf16[72,256]{1,0:T(8,128)(2,1)S(1)}, u32[]{:S(2)}, u32[]{:S(2)}) collective-permute-start(bf16[72,256]{1,0:T(8,128)(2,1)S(1)} %get-tuple-element.34), channel_id=1, source_target_pairs={{0,1},{1,0},{2,3},{3,2},{4,5},{5,4},{6,7},{7,6},{8,9},{9,8},{10,11... | collective-permute-start | bytes 110600 | tf_op jit(solution)/shard_map/ppermute | solution.py:283
  63.6 2.9 %collective-permute-start.17 = (bf16[72,256]{1,0:T(8,128)(2,1)S(1)}, bf16[72,256]{1,0:T(8,128)(2,1)S(1)}, u32[]{:S(2)}, u32[]{:S(2)}) collective-permute-start(bf16[72,256]{1,0:T(8,128)(2,1)S(1)} %get-tuple-element.35), channel_id=1, source_target_pairs={{0,3},{1,2},{2,1},{3,0},{4,7},{5,6},{6,5},{7,4},{8,11},{9,10},{10,... | collective-permute-start | bytes 110600 | tf_op jit(solution)/shard_map/ppermute | solution.py:283
  66.6 2.7 %collective-permute-done.17 = bf16[72,256]{1,0:T(8,128)(2,1)S(1)} collective-permute-done((bf16[72,256]{1,0:T(8,128)(2,1)S(1)}, bf16[72,256]{1,0:T(8,128)(2,1)S(1)}, u32[]{:S(2)}, u32[]{:S(2)}) %collective-permute-start.17) | collective-permute-done | bytes 36896 | tf_op jit(solution)/shard_map/ppermute | solution.py:283
  69.3 2.4 %collective-permute-done.16 = bf16[72,256]{1,0:T(8,128)(2,1)S(1)} collective-permute-done((bf16[72,256]{1,0:T(8,128)(2,1)S(1)}, bf16[72,256]{1,0:T(8,128)(2,1)S(1)}, u32[]{:S(2)}, u32[]{:S(2)}) %collective-permute-start.16) | collective-permute-done | bytes 36896 | tf_op jit(solution)/shard_map/ppermute | solution.py:283
  72.2 1.5 %collective-permute-start.19 = (bf16[72,256]{1,0:T(8,128)(2,1)S(1)}, bf16[72,256]{1,0:T(8,128)(2,1)S(1)}, u32[]{:S(2)}, u32[]{:S(2)}) collective-permute-start(bf16[72,256]{1,0:T(8,128)(2,1)S(1)} %fusion.13), channel_id=1, source_target_pairs={{0,2},{1,3},{2,0},{3,1},{4,6},{5,7},{6,4},{7,5},{8,10},{9,11},{10,... | collective-permute-start | bytes 110600 | tf_op jit(solution)/shard_map/ppermute | solution.py:286
  73.7 2.5 %collective-permute-start.18 = (bf16[72,256]{1,0:T(8,128)(2,1)S(1)}, bf16[72,256]{1,0:T(8,128)(2,1)S(1)}, u32[]{:S(2)}, u32[]{:S(2)}) collective-permute-start(bf16[72,256]{1,0:T(8,128)(2,1)S(1)} %fusion.13), channel_id=1, source_target_pairs={{0,3},{1,2},{2,1},{3,0},{4,7},{5,6},{6,5},{7,4},{8,11},{9,10},{10,... | collective-permute-start | bytes 110600 | tf_op jit(solution)/shard_map/ppermute | solution.py:286
  77.1 2.4 %collective-permute-done.18 = bf16[72,256]{1,0:T(8,128)(2,1)S(1)} collective-permute-done((bf16[72,256]{1,0:T(8,128)(2,1)S(1)}, bf16[72,256]{1,0:T(8,128)(2,1)S(1)}, u32[]{:S(2)}, u32[]{:S(2)}) %collective-permute-start.18) | collective-permute-done | bytes 36896 | tf_op jit(solution)/shard_map/ppermute | solution.py:286
  83.0 1.7 %collective-permute-done.23 = bf16[288,256]{1,0:T(8,128)(2,1)S(1)} collective-permute-done((bf16[288,256]{1,0:T(8,128)(2,1)S(1)}, bf16[288,256]{1,0:T(8,128)(2,1)S(1)}, u32[]{:S(2)}, u32[]{:S(2)}) %collective-permute-start.23) | collective-permute-done | bytes 147488 | tf_op jit(solution)/shard_map/ppermute | solution.py:289
  85.8 2.4 %collective-permute-done.21 = bf16[288,256]{1,0:T(8,128)(2,1)S(1)} collective-permute-done((bf16[288,256]{1,0:T(8,128)(2,1)S(1)}, bf16[288,256]{1,0:T(8,128)(2,1)S(1)}, u32[]{:S(2)}, u32[]{:S(2)}) %collective-permute-start.21) | collective-permute-done | bytes 147488 | tf_op jit(solution)/shard_map/ppermute | solution.py:289
  88.5 2.8 %images.1 = (bf16[192,256]{1,0:T(8,128)(2,1)}, bf16[192,256]{1,0:T(8,128)(2,1)}) custom-call(bf16[4,50,256]{2,1,0:T(8,128)(2,1)} %copy-done, bf16[1,50,256]{2,1,0:T(8,128)(2,1)} %get-tuple-element.46.gtop, bf16[1,50,256]{2,1,0:T(8,128)(2,1)} %get-tuple-element.45.gbot, bf16[208,256]{1,0:T(8,128)(2,1)} %copy-done.1, bf16[26,1,256]{2,1,0:T(2,128)(2,1)} %copy-done.3, ...), custom_call_target="tpu_custom_call" | custom-call | tf_op jit(solution)/shard_map/images/pallas_call | solution.py:270
  91.6 1.6 %convert.1 = f32[3,3,256,256]{3,2,1,0:T(8,128)} convert(bf16[3,3,256,256]{3,2,1,0:T(8,128)(2,1)S(1)} %bitcast.55) | non-fusion elementwise | flops 589824 | bytes 3538944 | tf_op jit(solution)/shard_map/convert_element_type | solution.py:292
  (56 shorter events, 23.9 us)
Async XLA Ops:
  7.4 16.2 %collective-permute-start.5 = (bf16[4,208,256]{2,1,0:T(8,128)(2,1)}, bf16[4,208,256]{2,1,0:T(8,128)(2,1)S(1)}, u32[]{:S(2)}, u32[]{:S(2)}) collective-permute-start(bf16[4,208,256]{2,1,0:T(8,128)(2,1)} %get-tuple-element.18), channel_id=1, source_target_pairs={{0,4},{4,0},{8,12},{12,8},{16,20},{20,16},{24,28},{28,24},{1,5},{5... | collective-permute-start | bytes 1277960 | tf_op jit(solution)/shard_map/ppermute | solution.py:237
  7.9 6.6 %collective-permute-start = (bf16[4,50,256]{2,1,0:T(8,128)(2,1)}, bf16[4,50,256]{2,1,0:T(8,128)(2,1)S(1)}, u32[]{:S(2)}, u32[]{:S(2)}) collective-permute-start(bf16[4,50,256]{2,1,0:T(8,128)(2,1)} %get-tuple-element.14), channel_id=1, source_target_pairs={{0,1},{1,0},{2,3},{3,2},{4,5},{5,4},{6,7},{7,6},{8,9},{9,8},{10,11... | collective-permute-start | bytes 307208 | tf_op jit(solution)/shard_map/ppermute | solution.py:238
  10.6 12.0 %collective-permute-start.1 = (bf16[4,50,256]{2,1,0:T(8,128)(2,1)}, bf16[4,50,256]{2,1,0:T(8,128)(2,1)S(1)}, u32[]{:S(2)}, u32[]{:S(2)}) collective-permute-start(bf16[4,50,256]{2,1,0:T(8,128)(2,1)} %get-tuple-element.15), channel_id=1, source_target_pairs={{0,2},{1,3},{2,0},{3,1},{4,6},{5,7},{6,4},{7,5},{8,10},{9,11},{10,... | collective-permute-start | bytes 307208 | tf_op jit(solution)/shard_map/ppermute | solution.py:238
  13.2 9.5 %collective-permute-start.2 = (bf16[4,50,256]{2,1,0:T(8,128)(2,1)}, bf16[4,50,256]{2,1,0:T(8,128)(2,1)S(1)}, u32[]{:S(2)}, u32[]{:S(2)}) collective-permute-start(bf16[4,50,256]{2,1,0:T(8,128)(2,1)} %get-tuple-element.16), channel_id=1, source_target_pairs={{0,3},{1,2},{2,1},{3,0},{4,7},{5,6},{6,5},{7,4},{8,11},{9,10},{10,... | collective-permute-start | bytes 307208 | tf_op jit(solution)/shard_map/ppermute | solution.py:238
  24.8 5.8 %collective-permute-start.6 = (bf16[208,256]{1,0:T(8,128)(2,1)S(1)}, bf16[208,256]{1,0:T(8,128)(2,1)S(1)}, u32[]{:S(2)}, u32[]{:S(2)}) collective-permute-start(bf16[208,256]{1,0:T(8,128)(2,1)S(1)} %get-tuple-element.23), channel_id=1, source_target_pairs={{0,8},{4,12},{8,0},{12,4},{16,24},{20,28},{24,16},{28,20},{1,9},{5... | collective-permute-start | bytes 319496 | tf_op jit(solution)/shard_map/ppermute | solution.py:240
  26.4 5.7 %collective-permute-start.8 = (bf16[208,256]{1,0:T(8,128)(2,1)S(1)}, bf16[208,256]{1,0:T(8,128)(2,1)S(1)}, u32[]{:S(2)}, u32[]{:S(2)}) collective-permute-start(bf16[208,256]{1,0:T(8,128)(2,1)S(1)} %get-tuple-element.24), channel_id=1, source_target_pairs={{0,24},{4,28},{8,16},{12,20},{16,8},{20,12},{24,0},{28,4},{1,25},{... | collective-permute-start | bytes 319496 | tf_op jit(solution)/shard_map/ppermute | solution.py:240
  27.9 5.3 %collective-permute-start.7 = (bf16[208,256]{1,0:T(8,128)(2,1)S(1)}, bf16[208,256]{1,0:T(8,128)(2,1)S(1)}, u32[]{:S(2)}, u32[]{:S(2)}) collective-permute-start(bf16[208,256]{1,0:T(8,128)(2,1)S(1)} %get-tuple-element.25), channel_id=1, source_target_pairs={{0,16},{4,20},{8,24},{12,28},{16,0},{20,4},{24,8},{28,12},{1,17},{... | collective-permute-start | bytes 319496 | tf_op jit(solution)/shard_map/ppermute | solution.py:240
  28.4 12.3 %collective-permute-start.4 = (bf16[1,50,256]{2,1,0:T(8,128)(2,1)S(1)}, bf16[1,50,256]{2,1,0:T(8,128)(2,1)S(1)}, u32[]{:S(2)}, u32[]{:S(2)}) collective-permute-start(bf16[1,50,256]{2,1,0:T(8,128)(2,1)S(1)} %get-tuple-element.41), channel_id=1, source_target_pairs={{0,4},{4,0},{8,12},{12,8},{16,20},{20,16},{24,28},{28,24},{1,5},{5... | collective-permute-start | bytes 76808 | tf_op jit(solution)/shard_map/ppermute | solution.py:246
  28.5 12.2 %collective-permute-start.3 = (bf16[1,50,256]{2,1,0:T(8,128)(2,1)S(1)}, bf16[1,50,256]{2,1,0:T(8,128)(2,1)S(1)}, u32[]{:S(2)}, u32[]{:S(2)}) collective-permute-start(bf16[1,50,256]{2,1,0:T(8,128)(2,1)S(1)} %get-tuple-element.42), channel_id=1, source_target_pairs={{4,8},{12,16},{20,24},{8,4},{16,12},{24,20},{5,9},{13,17},{21,25},... | collective-permute-start | bytes 76808 | tf_op jit(solution)/shard_map/ppermute | solution.py:248
  34.2 7.1 %collective-permute-start.10 = (bf16[26,1,256]{2,1,0:T(2,128)(2,1)S(1)}, bf16[26,1,256]{2,1,0:T(2,128)(2,1)S(1)}, u32[]{:S(2)}, u32[]{:S(2)}) collective-permute-start(bf16[26,1,256]{2,1,0:T(2,128)(2,1)S(1)} %get-tuple-element.43), channel_id=1, source_target_pairs={{1,0},{2,1},{3,2},{5,4},{6,5},{7,6},{9,8},{10,9},{11,10},{13,12},{... | collective-permute-start | bytes 39944 | tf_op jit(solution)/shard_map/ppermute | solution.py:254
  35.5 6.7 %collective-permute-start.9 = (bf16[26,1,256]{2,1,0:T(2,128)(2,1)S(1)}, bf16[26,1,256]{2,1,0:T(2,128)(2,1)S(1)}, u32[]{:S(2)}, u32[]{:S(2)}) collective-permute-start(bf16[26,1,256]{2,1,0:T(2,128)(2,1)S(1)} %get-tuple-element.44), channel_id=1, source_target_pairs={{0,1},{1,2},{2,3},{4,5},{5,6},{6,7},{8,9},{9,10},{10,11},{12,13},{... | collective-permute-start | bytes 39944 | tf_op jit(solution)/shard_map/ppermute | solution.py:253
  50.1 6.8 %collective-permute-start.12 = (bf16[288,256]{1,0:T(8,128)(2,1)S(1)}, bf16[288,256]{1,0:T(8,128)(2,1)S(1)}, u32[]{:S(2)}, u32[]{:S(2)}) collective-permute-start(bf16[288,256]{1,0:T(8,128)(2,1)S(1)} %get-tuple-element.28), channel_id=1, source_target_pairs={{0,8},{4,12},{8,0},{12,4},{16,24},{20,28},{24,16},{28,20},{1,9},{5... | collective-permute-start | bytes 442376 | tf_op jit(solution)/shard_map/ppermute | solution.py:280
  51.6 8.1 %collective-permute-start.14 = (bf16[288,256]{1,0:T(8,128)(2,1)S(1)}, bf16[288,256]{1,0:T(8,128)(2,1)S(1)}, u32[]{:S(2)}, u32[]{:S(2)}) collective-permute-start(bf16[288,256]{1,0:T(8,128)(2,1)S(1)} %get-tuple-element.29), channel_id=1, source_target_pairs={{0,24},{4,28},{8,16},{12,20},{16,8},{20,12},{24,0},{28,4},{1,25},{... | collective-permute-start | bytes 442376 | tf_op jit(solution)/shard_map/ppermute | solution.py:280
  52.6 8.5 %collective-permute-start.13 = (bf16[288,256]{1,0:T(8,128)(2,1)S(1)}, bf16[288,256]{1,0:T(8,128)(2,1)S(1)}, u32[]{:S(2)}, u32[]{:S(2)}) collective-permute-start(bf16[288,256]{1,0:T(8,128)(2,1)S(1)} %get-tuple-element.30), channel_id=1, source_target_pairs={{0,16},{4,20},{8,24},{12,28},{16,0},{20,4},{24,8},{28,12},{1,17},{... | collective-permute-start | bytes 442376 | tf_op jit(solution)/shard_map/ppermute | solution.py:280
  61.2 5.4 %collective-permute-start.15 = (bf16[72,256]{1,0:T(8,128)(2,1)S(1)}, bf16[72,256]{1,0:T(8,128)(2,1)S(1)}, u32[]{:S(2)}, u32[]{:S(2)}) collective-permute-start(bf16[72,256]{1,0:T(8,128)(2,1)S(1)} %get-tuple-element.34), channel_id=1, source_target_pairs={{0,1},{1,0},{2,3},{3,2},{4,5},{5,4},{6,7},{7,6},{8,9},{9,8},{10,11... | collective-permute-start | bytes 110600 | tf_op jit(solution)/shard_map/ppermute | solution.py:283
  63.6 5.8 %collective-permute-start.17 = (bf16[72,256]{1,0:T(8,128)(2,1)S(1)}, bf16[72,256]{1,0:T(8,128)(2,1)S(1)}, u32[]{:S(2)}, u32[]{:S(2)}) collective-permute-start(bf16[72,256]{1,0:T(8,128)(2,1)S(1)} %get-tuple-element.35), channel_id=1, source_target_pairs={{0,3},{1,2},{2,1},{3,0},{4,7},{5,6},{6,5},{7,4},{8,11},{9,10},{10,... | collective-permute-start | bytes 110600 | tf_op jit(solution)/shard_map/ppermute | solution.py:283
  66.5 5.3 %collective-permute-start.16 = (bf16[72,256]{1,0:T(8,128)(2,1)S(1)}, bf16[72,256]{1,0:T(8,128)(2,1)S(1)}, u32[]{:S(2)}, u32[]{:S(2)}) collective-permute-start(bf16[72,256]{1,0:T(8,128)(2,1)S(1)} %get-tuple-element.36), channel_id=1, source_target_pairs={{0,2},{1,3},{2,0},{3,1},{4,6},{5,7},{6,4},{7,5},{8,10},{9,11},{10,... | collective-permute-start | bytes 110600 | tf_op jit(solution)/shard_map/ppermute | solution.py:283
  71.8 4.5 %collective-permute-start.20 = (bf16[72,256]{1,0:T(8,128)(2,1)S(1)}, bf16[72,256]{1,0:T(8,128)(2,1)S(1)}, u32[]{:S(2)}, u32[]{:S(2)}) collective-permute-start(bf16[72,256]{1,0:T(8,128)(2,1)S(1)} %fusion.13), channel_id=1, source_target_pairs={{0,1},{1,0},{2,3},{3,2},{4,5},{5,4},{6,7},{7,6},{8,9},{9,8},{10,11... | collective-permute-start | bytes 110600 | tf_op jit(solution)/shard_map/ppermute | solution.py:286
  72.2 4.9 %collective-permute-start.19 = (bf16[72,256]{1,0:T(8,128)(2,1)S(1)}, bf16[72,256]{1,0:T(8,128)(2,1)S(1)}, u32[]{:S(2)}, u32[]{:S(2)}) collective-permute-start(bf16[72,256]{1,0:T(8,128)(2,1)S(1)} %fusion.13), channel_id=1, source_target_pairs={{0,2},{1,3},{2,0},{3,1},{4,6},{5,7},{6,4},{7,5},{8,10},{9,11},{10,... | collective-permute-start | bytes 110600 | tf_op jit(solution)/shard_map/ppermute | solution.py:286
  73.7 5.8 %collective-permute-start.18 = (bf16[72,256]{1,0:T(8,128)(2,1)S(1)}, bf16[72,256]{1,0:T(8,128)(2,1)S(1)}, u32[]{:S(2)}, u32[]{:S(2)}) collective-permute-start(bf16[72,256]{1,0:T(8,128)(2,1)S(1)} %fusion.13), channel_id=1, source_target_pairs={{0,3},{1,2},{2,1},{3,0},{4,7},{5,6},{6,5},{7,4},{8,11},{9,10},{10,... | collective-permute-start | bytes 110600 | tf_op jit(solution)/shard_map/ppermute | solution.py:286
  79.5 5.2 %collective-permute-start.23 = (bf16[288,256]{1,0:T(8,128)(2,1)S(1)}, bf16[288,256]{1,0:T(8,128)(2,1)S(1)}, u32[]{:S(2)}, u32[]{:S(2)}) collective-permute-start(bf16[288,256]{1,0:T(8,128)(2,1)S(1)} %pad_maximum_fusion.2), channel_id=1, source_target_pairs={{0,8},{4,12},{8,0},{12,4},{16,24},{20,28},{24,16},{28,20},{1,9},{5... | collective-permute-start | bytes 442376 | tf_op jit(solution)/shard_map/ppermute | solution.py:289
  80.6 5.1 %collective-permute-start.22 = (bf16[288,256]{1,0:T(8,128)(2,1)S(1)}, bf16[288,256]{1,0:T(8,128)(2,1)S(1)}, u32[]{:S(2)}, u32[]{:S(2)}) collective-permute-start(bf16[288,256]{1,0:T(8,128)(2,1)S(1)} %pad_maximum_fusion.2), channel_id=1, source_target_pairs={{0,16},{4,20},{8,24},{12,28},{16,0},{20,4},{24,8},{28,12},{1,17},{... | collective-permute-start | bytes 442376 | tf_op jit(solution)/shard_map/ppermute | solution.py:289
  82.1 6.0 %collective-permute-start.21 = (bf16[288,256]{1,0:T(8,128)(2,1)S(1)}, bf16[288,256]{1,0:T(8,128)(2,1)S(1)}, u32[]{:S(2)}, u32[]{:S(2)}) collective-permute-start(bf16[288,256]{1,0:T(8,128)(2,1)S(1)} %pad_maximum_fusion.2), channel_id=1, source_target_pairs={{0,24},{4,28},{8,16},{12,20},{16,8},{20,12},{24,0},{28,4},{1,25},{... | collective-permute-start | bytes 442376 | tf_op jit(solution)/shard_map/ppermute | solution.py:289
  88.4 2.9 %collective-permute-start.24 = (bf16[1152,256]{1,0:T(8,128)(2,1)S(1)}, bf16[1152,256]{1,0:T(8,128)(2,1)S(1)}, u32[]{:S(2)}, u32[]{:S(2)}) collective-permute-start(bf16[1152,256]{1,0:T(8,128)(2,1)S(1)} %pad_maximum_fusion.1), channel_id=1, source_target_pairs={{0,4},{4,0},{8,12},{12,8},{16,20},{20,16},{24,28},{28,24},{1,5},{5... | collective-permute-start | bytes 1769480 | tf_op jit(solution)/shard_map/ppermute | solution.py:291
  (5 other events, 29.5 us)

commit v2 on v0

v2 whole, which is shorter than its diff:
```python
import functools

import jax
import jax.numpy as jnp
from jax import lax
from jax.experimental import pallas as pl
from jax.experimental.pallas import tpu as pltpu
from jax.sharding import PartitionSpec as P

LEVELS = 4
F32 = jnp.float32
BF16 = jnp.bfloat16
SMALL_BYTES = 16 * 2**20


def flip(count, mask):
    return [(i, i ^ mask) for i in range(count)]


def ordered(parts, index):
    count = len(parts)
    bit = 1
    while bit < count:
        swap = (index & bit) != 0
        parts = [jnp.where(swap, parts[a ^ bit], parts[a]) for a in range(count)]
        bit *= 2
    return parts


def put(ref, rows, value):
    for lane in range(ref.shape[0]):
        ref[lane, rows, :] = value[:, lane * 128 : (lane + 1) * 128]


def get(ref, rows):
    return jnp.concatenate([ref[lane, rows, :] for lane in range(ref.shape[0])], axis=1)


def up16(count):
    return -(-count // 16) * 16


def joins(mask):
    return (mask & (mask + 1)) == 0


def place():
    pb = lax.axis_index("pb")
    return pb // 2, pb % 2, lax.axis_index("ka")


def carried(parts, index, step):
    total = None
    for mask, row in parts:
        row = jnp.where((index ^ mask) == index + step, row, 0.0)
        total = row if total is None else total + row
    return total


def corr_kernel(dims, a_hbm, q_hbm, key_hbm, qi_hbm, ki_hbm, *rest):
    width, key_rows, tile_q, tile_k, n_ka, n_quad, chunk = dims
    q_outs = rest[:n_ka]
    send_ref, keep_ref = rest[n_ka : n_ka + 2]
    a_ref, q_ref, key_ref, cells_ref, coarse_ref, keyf_ref, tmp_ref, kpad_ref, qpad_ref, stage_ref, qi_ref, ki_ref, sems = rest[n_ka + 2 :]
    count, channels = q_ref.shape
    rows = count // width
    scale = channels ** (-0.5)
    quad, core, z = place()

    copies = [pltpu.make_async_copy(key_hbm, key_ref, sems.at[0])]
    for i in range(count // chunk):
        lanes = pl.ds(i * chunk, chunk)
        copies.append(pltpu.make_async_copy(a_hbm.at[:, lanes], a_ref.at[:, lanes], sems.at[i + 2]))
    copies.append(pltpu.make_async_copy(q_hbm, q_ref, sems.at[1]))
    copies.append(pltpu.make_async_copy(qi_hbm, qi_ref, sems.at[count // chunk + 2]))
    copies.append(pltpu.make_async_copy(ki_hbm, ki_ref, sems.at[count // chunk + 3]))
    for copy in copies:
        copy.start()

    qpad_ref[...] = jnp.zeros_like(qpad_ref)
    edge = jnp.zeros((key_rows, channels), F32)
    put(kpad_ref, slice(0, key_rows), edge)
    put(kpad_ref, slice((width + 1) * key_rows, (width + 2) * key_rows), edge)

    copies[0].wait()
    put(keyf_ref, slice(None), key_ref[...].astype(F32))
    lines = [get(keyf_ref, pl.ds(r, width, stride=key_rows)) for r in range(key_rows)]
    offset = 0
    for level in range(LEVELS):
        w = width >> level
        if level:
            pairs = []
            for i in range(len(lines) // 2):
                put(tmp_ref, slice(0, 2 * w), lines[2 * i] + lines[2 * i + 1])
                pairs.append(get(tmp_ref, pl.ds(0, w, stride=2)) + get(tmp_ref, pl.ds(1, w, stride=2)))
            lines = pairs
        for line in lines:
            cells_ref[offset : offset + w, :] = line * (4.0**-level)
            offset += w
    cells = cells_ref[...].astype(BF16)
    for copy in copies[1:]:
        copy.wait()

    last_row = ki_ref[...].astype(F32)
    first_row, last_row = last_row[:, 0], last_row[:, key_rows - 1]
    for s in range(1, n_ka):
        if joins(s):
            q_outs[s][rows, 0:tile_k] = jnp.where((z ^ s) == z + 1, last_row, first_row).astype(BF16)
    base = n_quad * (tile_k + 2) * key_rows
    send_ref[base : base + tile_q, :] = qi_ref[0]
    send_ref[base + up16(tile_q) : base + up16(tile_q) + tile_q, :] = qi_ref[rows - 1]
    query = lax.dot_general(cells, a_ref[...], (((0,), (0,)), ((), ())), preferred_element_type=F32).T * scale
    coarse_ref[...] = jnp.dot(a_ref[...], q_ref[...], preferred_element_type=F32)
    for row in range(rows):
        qpad_ref[8 : 8 + width, :] = query[row * width : (row + 1) * width]
        for k in range(n_ka):
            stage_ref[z ^ k, 0 : tile_q + 2, :] = qpad_ref[7 + tile_q * k : 9 + tile_q * (k + 1), :]
        for s in range(n_ka):
            q_outs[s][row] = stage_ref[s, 0 : tile_q + 2, :].astype(BF16)

    offsets = [0]
    for level in range(LEVELS):
        offsets.append(offsets[-1] + (key_rows >> level) * (width >> level))
    finer = None
    for level in reversed(range(LEVELS)):
        w = width >> level
        here = []
        for r in range(key_rows >> level):
            start = offsets[level] + r * w
            value = coarse_ref[start : start + w, :] * (scale * 4.0**-level)
            if finer is not None:
                value = value + finer[r // 2]
            here.append(value)
        if level:
            finer = []
            for value in here:
                put(tmp_ref, pl.ds(0, w, stride=2), value)
                put(tmp_ref, pl.ds(1, w, stride=2), value)
                finer.append(get(tmp_ref, slice(0, 2 * w)))
    for r in range(key_rows):
        put(kpad_ref, pl.ds(key_rows + r, width, stride=key_rows), here[r])
    size = (tile_k + 2) * key_rows
    for s in range(n_quad):
        first = (quad ^ s) * 2 * tile_k * key_rows
        mine = pl.multiple_of(first + core * tile_k * key_rows, 8)
        other = pl.multiple_of(first + (1 - core) * tile_k * key_rows, 8)
        keep_ref[s] = get(kpad_ref, pl.ds(mine, size))
        send_ref[s * size : (s + 1) * size, :] = get(kpad_ref, pl.ds(other, size)).astype(BF16)


def correlate(grads, queries, keys, query_image, key_image, width, key_rows, n_ka, n_quad):
    cells, count = grads.shape
    channels = queries.shape[1]
    rows = count // width
    tile_q = width // n_ka
    tile_k = width // (2 * n_quad)
    size = (tile_k + 2) * key_rows
    chunk = 256
    hbm = pl.BlockSpec(memory_space=pltpu.HBM)
    vmem = pl.BlockSpec(memory_space=pltpu.VMEM)
    dims = (width, key_rows, tile_q, tile_k, n_ka, n_quad, chunk)
    lanes = channels // 128
    return pl.pallas_call(
        functools.partial(corr_kernel, dims),
        in_specs=[hbm] * 5,
        out_specs=[vmem] * (n_ka + 2),
        out_shape=[jax.ShapeDtypeStruct((rows + (s > 0 and joins(s)), tile_q + 2, channels), BF16) for s in range(n_ka)]
        + [
            jax.ShapeDtypeStruct((n_quad * size + 2 * up16(tile_q), channels), BF16),
            jax.ShapeDtypeStruct((n_quad, size, channels), F32),
        ],
        scratch_shapes=[
            pltpu.VMEM((cells, count), BF16),
            pltpu.VMEM((count, channels), BF16),
            pltpu.VMEM((width * key_rows, channels), BF16),
            pltpu.VMEM((cells, channels), F32),
            pltpu.VMEM((cells, channels), F32),
            pltpu.VMEM((lanes, width * key_rows, 128), F32),
            pltpu.VMEM((lanes, width, 128), F32),
            pltpu.VMEM((lanes, (width + 2) * key_rows, 128), F32),
            pltpu.VMEM((width + 16, channels), F32),
            pltpu.VMEM((n_ka, tile_q + 8, channels), F32),
            pltpu.VMEM(query_image.shape, BF16),
            pltpu.VMEM(key_image.shape, BF16),
            pltpu.SemaphoreType.DMA((count // chunk + 4,)),
        ],
        compiler_params=pltpu.CompilerParams(vmem_limit_bytes=cells * (count * 4 + channels * 24)),
        name="correlate",
    )(*[pltpu.with_memory_space_constraint(x, pltpu.HBM) for x in (grads, queries, keys, query_image, key_image)])


def pair_kernel(size, tile, keep_ref, recv_ref, own_ref, near_ref, *sends):
    quad, core, _ = place()
    n_quad = len(sends) + 1
    base = n_quad * size
    first = recv_ref[base : base + tile, :].astype(F32)
    last = recv_ref[base + up16(tile) : base + up16(tile) + tile, :].astype(F32)
    near_ref[...] = jnp.where(core == 0, first, last).astype(BF16)
    onward = jnp.where(core == 0, last, first).astype(BF16)
    own_ref[...] = keep_ref[0] + recv_ref[0:size, :].astype(F32)
    for s, send in enumerate(sends, 1):
        send[0:size, :] = (keep_ref[s] + recv_ref[s * size : (s + 1) * size, :].astype(F32)).astype(BF16)
        if joins(s):
            send[size : size + tile, :] = onward


def both_sides(refs, near_ref, size, quad, core):
    tile = near_ref.shape[0]
    parts = [(s, ref[size : size + tile, :].astype(F32)) for s, ref in enumerate(refs, 1) if joins(s)]
    near = near_ref[...].astype(F32)
    far = carried(parts, quad, 2 * core - 1)
    return jnp.where(core == 0, far, near), jnp.where(core == 0, near, far)


def weight_kernel(n_ka, n_quad, *refs):
    q_refs = refs[:n_ka]
    k_refs = refs[n_ka : n_ka + n_quad]
    near_ref, qi_ref, ki_ref = refs[n_ka + n_quad : n_ka + n_quad + 3]
    send_ref, keep_ref, gq_ref, gk_ref, acc_ref, sum_ref, ext_ref = refs[n_ka + n_quad + 3 :]
    rows, wide, channels = gq_ref.shape
    size = gk_ref.shape[0]
    tile_k, key_rows, cin = ki_ref.shape
    tile_q = wide - 2
    quad, core, z = place()
    top, bottom = both_sides(k_refs[1:], near_ref, size, quad, core)
    lines = [(s, ref[rows, 0:tile_k].astype(F32)) for s, ref in enumerate(q_refs) if s and joins(s)]
    ext_ref[:, 8 : 8 + key_rows, :] = ki_ref[...].astype(F32)
    ext_ref[:, 7, :] = carried(lines, z, -1)
    ext_ref[:, 8 + key_rows, :] = carried(lines, z, 1)
    query = jnp.concatenate([top[None], qi_ref[...].astype(F32), bottom[None]], axis=0)
    image = []
    for a in (-1, 0, 1):
        first = query[1 + a : 1 + a + rows].reshape(rows * tile_q, cin)
        second = ext_ref[:, 8 + a : 8 + a + key_rows, :].reshape(tile_k * key_rows, cin)
        image.append(jnp.concatenate([first, second], axis=0).T.astype(BF16))
    image = jnp.concatenate(image, axis=0)
    query = q_refs[0][...].astype(F32)
    for ref in q_refs[1:]:
        query = query + ref[0:rows].astype(F32)
    gq = query.astype(BF16)
    gq_ref[...] = gq
    sum_ref[:, 0:wide, :] = gq.astype(F32)
    key = k_refs[0][...]
    for ref in k_refs[1:]:
        key = key + ref[0:size, :].astype(F32)
    gk = key.astype(BF16)
    gk_ref[...] = gk
    count = tile_k * key_rows
    for b in (-1, 0, 1):
        first = sum_ref[:, 1 - b : 1 - b + tile_q, :].reshape(rows * tile_q, channels).astype(BF16)
        grad = jnp.concatenate([first, gk[(1 - b) * key_rows : (1 - b) * key_rows + count]], axis=0)
        part = jnp.dot(image, grad, preferred_element_type=F32)
        for a in range(3):
            tap = a * 3 + b + 1
            acc_ref[tap * cin : (tap + 1) * cin, :] = part[a * cin : (a + 1) * cin]
    half = keep_ref.shape[0]
    keep_ref[...] = acc_ref[pl.ds(pl.multiple_of(core * half, 16), half), :]
    send_ref[0:half, :] = acc_ref[pl.ds(pl.multiple_of((1 - core) * half, 16), half), :].astype(BF16)
    send_ref[half : half + wide, :] = gq[0]
    send_ref[half + up16(wide) : half + up16(wide) + wide, :] = gq[rows - 1]


def piece_kernel(keep_ref, recv_ref, own_ref, near_ref, *rest):
    *sends, sum_ref = rest
    quad, core, _ = place()
    half = keep_ref.shape[0]
    size = own_ref.shape[0]
    tile = near_ref.shape[0]
    first = recv_ref[half : half + tile, :].astype(F32)
    last = recv_ref[half + up16(tile) : half + up16(tile) + tile, :].astype(F32)
    near_ref[...] = jnp.where(core == 0, first, last).astype(BF16)
    onward = jnp.where(core == 0, last, first).astype(BF16)
    sum_ref[...] = keep_ref[...] + recv_ref[0:half, :].astype(F32)
    own_ref[...] = sum_ref[pl.ds(pl.multiple_of(quad * size, 16), size), :]
    for s, send in enumerate(sends, 1):
        send[0:size, :] = sum_ref[pl.ds(pl.multiple_of((quad ^ s) * size, 16), size), :].astype(BF16)
        if joins(s):
            send[size : size + tile, :] = onward


def layer_kernel(n_quad, n_ka, *refs):
    own_ref, *got = refs[:n_quad]
    near_ref, gk_ref, out_ref, top_ref, bottom_ref = refs[n_quad : n_quad + 5]
    sends = refs[n_quad + 5 : n_quad + 4 + n_ka]
    stage_ref, ext_ref = refs[n_quad + 4 + n_ka :]
    quad, core, z = place()
    size = own_ref.shape[0]
    piece = size // n_ka
    top, bottom = both_sides(got, near_ref, size, quad, core)
    top_ref[...] = top.astype(BF16)
    bottom_ref[...] = bottom.astype(BF16)
    total = own_ref[...]
    for ref in got:
        total = total + ref[0:size, :].astype(F32)
    for k in range(n_ka):
        stage_ref[z ^ k, 0:piece, :] = total[k * piece : (k + 1) * piece]
    out_ref[...] = stage_ref[0, 0:piece, :]
    tall, key_rows, _ = ext_ref.shape
    ext_ref[...] = gk_ref[...].astype(F32).reshape(ext_ref.shape)
    first, last = ext_ref[:, 0, :], ext_ref[:, key_rows - 1, :]
    for s, send in enumerate(sends, 1):
        send[0:piece, :] = stage_ref[s, 0:piece, :].astype(BF16)
        if joins(s):
            send[piece : piece + tall, :] = jnp.where((z ^ s) == z + 1, last, first).astype(BF16)


def image_kernel(piece, gq_ref, top_ref, bottom_ref, gk_ref, w_ref, *rest):
    *got, qo_ref, ko_ref, qext_ref, kext_ref = rest
    rows, wide, channels = gq_ref.shape
    tall = kext_ref.shape[0]
    key_rows = gk_ref.shape[0] // tall
    tile_q = wide - 2
    tile_k = tall - 2
    _, _, z = place()
    lines = [(s, ref[piece : piece + tall, :].astype(F32)) for s, ref in enumerate(got, 1) if joins(s)]
    qext_ref[0, 0:wide, :] = top_ref[...].astype(F32)
    qext_ref[1 : rows + 1, 0:wide, :] = gq_ref[...].astype(F32)
    qext_ref[rows + 1, 0:wide, :] = bottom_ref[...].astype(F32)
    kext_ref[:, 8 : 8 + key_rows, :] = gk_ref[...].astype(F32).reshape(tall, key_rows, channels)
    kext_ref[:, 7, :] = carried(lines, z, -1)
    kext_ref[:, 8 + key_rows, :] = carried(lines, z, 1)
    total = None
    for tap in range(9):
        a, b = tap // 3 - 1, tap % 3 - 1
        first = qext_ref[1 - a : 1 - a + rows, 1 - b : 1 - b + tile_q, :].reshape(rows * tile_q, channels)
        second = kext_ref[1 - b : 1 - b + tile_k, 8 - a : 8 - a + key_rows, :].reshape(tile_k * key_rows, channels)
        grad = jnp.concatenate([first.astype(BF16), second.astype(BF16)], axis=0)
        part = lax.dot_general(grad, w_ref[tap], (((1,), (1,)), ((), ())), preferred_element_type=F32)
        total = part if total is None else total + part
    count = qo_ref.shape[0]
    qo_ref[...] = total[:count].astype(BF16)
    ko_ref[...] = total[count:].astype(BF16)


def call(kernel, name, outs, args, scratch=()):
    return pl.pallas_call(
        kernel,
        in_specs=[pl.BlockSpec(memory_space=pltpu.VMEM)] * len(args),
        out_shape=[jax.ShapeDtypeStruct(shape, dtype) for shape, dtype in outs],
        scratch_shapes=[pltpu.VMEM(shape, F32) for shape in scratch],
        compiler_params=pltpu.CompilerParams(vmem_limit_bytes=SMALL_BYTES),
        name=name,
    )(*args)


def body(query_features, key_features, pyramid_grad, query_image, key_image, conv_weight):
    n_pb = lax.axis_size("pb")
    n_ka = lax.axis_size("ka")
    n_quad = n_pb // 2
    quad, core, z = place()
    strip_rows, width, channels = query_features.shape
    key_rows = key_features.shape[1]
    cin = conv_weight.shape[2]
    tile_q = width // n_ka
    tile_k = width // n_pb
    wide = tile_q + 2
    tall = tile_k + 2
    size = tall * key_rows
    taps = 9
    half = taps * cin // 2
    quarter = half // n_quad
    piece = quarter // n_ka

    def to_core(x):
        return lax.ppermute(x, "pb", flip(n_pb, 1))

    def to_quad(parts):
        return [lax.ppermute(x, "pb", flip(n_pb, 2 * s)) for s, x in enumerate(parts, 1)]

    def to_layers(parts):
        return [lax.ppermute(x, "ka", flip(n_ka, s)) for s, x in enumerate(parts, 1)]

    def extra(count, mask, more):
        return count + (more if joins(mask) else 0)

    grads = jnp.transpose(pyramid_grad.reshape(pyramid_grad.shape[0], pyramid_grad.shape[2]))
    *q_parts, k_send, k_keep = correlate(
        grads,
        query_features.reshape(strip_rows * width, channels),
        key_features.reshape(width * key_rows, channels),
        query_image,
        key_image,
        width,
        key_rows,
        n_ka,
        n_quad,
    )
    k_recv = to_core(k_send)
    q_recv = to_layers(q_parts[1:])
    outs = [((size, channels), F32), ((tile_q, cin), BF16)]
    outs += [((extra(size, s, tile_q), channels), BF16) for s in range(1, n_quad)]
    k_own, near, *k_pair = call(functools.partial(pair_kernel, size, tile_q), "pairs", outs, (k_keep, k_recv))
    k_more = to_quad(k_pair)
    outs = [
        ((half + 2 * up16(wide), channels), BF16),
        ((half, channels), F32),
        ((strip_rows, wide, channels), BF16),
        ((size, channels), BF16),
    ]
    w_send, w_keep, gq, gk = call(
        functools.partial(weight_kernel, n_ka, n_quad),
        "weights",
        outs,
        (q_parts[0], *q_recv, k_own, *k_more, near, query_image, key_image),
        [(taps * cin, channels), (strip_rows, up16(wide), channels), (tile_k, key_rows + 16, cin)],
    )

    w_recv = to_core(w_send)
    outs = [((quarter, channels), F32), ((wide, channels), BF16)]
    outs += [((extra(quarter, s, wide), channels), BF16) for s in range(1, n_quad)]
    own, near, *sends = call(piece_kernel, "pieces", outs, (w_keep, w_recv), [(half, channels)])
    got = to_quad(sends)
    outs = [((piece, channels), F32)] + [((wide, channels), BF16)] * 2
    outs += [((extra(piece, s, tall), channels), BF16) for s in range(1, n_ka)]
    own, top, bottom, *sends = call(
        functools.partial(layer_kernel, n_quad, n_ka),
        "layers",
        outs,
        (own, *got, near, gk),
        [(n_ka, up16(piece), channels), (tall, key_rows, channels)],
    )
    got = to_layers(sends)
    part = sum([x[:piece].astype(F32) for x in got], own).astype(BF16)
    q_out, k_out = call(
        functools.partial(image_kernel, piece),
        "images",
        [((strip_rows * tile_q, cin), BF16), ((tile_k * key_rows, cin), BF16)],
        (gq, top, bottom, gk, conv_weight.reshape(taps, cin, channels), *got),
        [(strip_rows + 2, up16(wide), channels), (tall, key_rows + 16, channels)],
    )
    part = jnp.concatenate(ordered([part] + to_layers([part] * (n_ka - 1)), z), axis=0)
    part = jnp.concatenate(ordered([part] + to_quad([part] * (n_quad - 1)), quad), axis=0)
    whole = jnp.concatenate(ordered([part, to_core(part)], core), axis=0)
    return (
        q_out.reshape(query_image.shape),
        k_out.reshape(key_image.shape),
        whole.astype(F32).reshape(conv_weight.shape),
    )


def solution(mesh):
    placed = (
        P("pb", None, None),
        P(None, "ka", None),
        P("pb", "ka", None),
        P("pb", "ka", None),
        P("pb", "ka", None),
        P(),
    )
    return jax.shard_map(
        body,
        mesh=mesh,
        in_specs=placed,
        out_specs=(P("pb", "ka", None), P("pb", "ka", None), P()),
        check_vma=False,
    )
```

time: 263 us -> 68.2 us (0.26)
  waiting for transfers between devices: 146 us -> 27.2 us
  matrix products: 24.1 us -> 0 us
  local copies, waits for them, and re-layouts: 19.6 us -> 1 us
  other arithmetic: 16.6 us -> 2.25 us
  between operations: 14.4 us -> 0.79 us
  starting transfers between devices: 40.9 us -> 28.8 us
  Pallas kernels: 0 us -> 7.93 us
    psum x1 -> x0, waiting for transfers between devices: 128 us -> none  [body(): weight_grad = lax.psum(local_weight, ('pb', 'ka'))]
    ppermute x16 -> x21, waiting for transfers between devices: 3.34 us -> 27.2 us  [the longest x9 12.8 us: to_quad(): lax.ppermute(x, 'pb', flip(n_pb, 2 * s))]
    dot_general x43 -> x0, matrix products: 22.2 us -> none  [the longest x4 8.37 us: body(): jnp.dot(grad_block, ordered, preferred_element_type=jnp.float32)]
    reduce_scatter x2 -> x0, waiting for transfers between devices: 14.3 us -> none  [the longest x1 14.2 us: body(): lax.psum_scatter((fine_term + coarse_sum) * norm_scale, 'pb', scatter_dim...]
    ppermute x16 -> x21, starting transfers between devices: 40.8 us -> 28.8 us  [the longest x9 16.1 us: to_layers(): lax.ppermute(x, 'ka', flip(n_ka, s))]
    pallas_call x0 -> x6, Pallas kernels: none -> 7.93 us  [the longest x1 4.81 us: correlate(): pl.pallas_call(functools.partial(corr_kernel, dims), in_specs=[hbm] * 5,...]
    unnamed x29 -> x6, local copies, waits for them, and re-layouts: 6.82 us -> 1 us
    reduce_sum x4 -> x0, other arithmetic: 5.52 us -> none  [pool_levels(): pooled = strip_float.reshape(cell_cols // factor, factor, key_rows // fac...]
  transfers between devices with their start and end apart: 19 -> 21, of which waited for: 5 -> 10; matrix products, arithmetic and copies ran while one was open for 19% -> 0% of each run, Pallas kernels for 0% -> 2%
where the time goes in v2:
time: 68.2 us; the launch traced here: 68 us
  starting transfers between devices  28.8 us (42%)
  waiting for transfers between devices  27.2 us (40%)
  Pallas kernels  7.93 us (12%)
  other arithmetic  2.25 us (3%)
  local copies, waits for them, and re-layouts  1 us (1%)
  between operations  0.79 us (1%)
    ppermute x9, starting transfers between devices, to_layers(): lax.ppermute(x, 'ka', flip(n_ka, s))  16.1 us
    ppermute x9, waiting for transfers between devices, to_quad(): lax.ppermute(x, 'pb', flip(n_pb, 2 * s))  12.8 us
    ppermute x9, waiting for transfers between devices, to_layers(): lax.ppermute(x, 'ka', flip(n_ka, s))  12.3 us
    ppermute x9, starting transfers between devices, to_quad(): lax.ppermute(x, 'pb', flip(n_pb, 2 * s))  12 us
    pallas_call x1, Pallas kernels, correlate(): pl.pallas_call(functools.partial(corr_kernel, dims), in_specs=[hbm] * 5,...  4.81 us
    pallas_call x5, Pallas kernels, call(): pl.pallas_call(kernel, in_specs=[pl.BlockSpec(memory_space=pltpu.VMEM)] *...  3.13 us
    ppermute x3, waiting for transfers between devices, to_core(): return lax.ppermute(x, 'pb', flip(n_pb, 1))  2.09 us
    convert_element_type x1, other arithmetic, body(): whole.astype(F32).reshape(conv_weight.shape)  1.63 us
  transfers between devices with their start and end apart: 21, of which 10 were waited for; matrix products, arithmetic and copies ran while one was open for 0% of the time, Pallas kernels for 2%

profile of v2, /device:TPU:0, one launch (start us, length us, event | category | flops | bytes accessed | tf_op | source)
XLA Modules:
  0.0 68.0 jit_solution(5064591044189190036)
XLA Ops:
  0.6 4.8 %correlate.1 = (bf16[4,50,256]{2,1,0:T(8,128)(2,1)S(1)}, bf16[5,50,256]{2,1,0:T(8,128)(2,1)S(1)}, bf16[4,50,256]{2,1,0:T(8,128)(2,1)S(1)}, bf16[5,50,256]{2,1,0:...) custom-call(bf16[2040,768]{1,0:T(8,128)(2,1)} %bitcast.12, bf16[768,256]{1,0:T(8,128)(2,1)} %bitcast.14, ...), custom_call_target="tpu_custom_call" | custom-call | tf_op jit(solution)/shard_map/correlate/pallas_call | solution.py:163
  6.0 3.7 %collective-permute-start.1 = (bf16[4,50,256]{2,1,0:T(8,128)(2,1)S(1)}, bf16[4,50,256]{2,1,0:T(8,128)(2,1)S(1)}, u32[]{:S(2)}, u32[]{:S(2)}) collective-permute-start(bf16[4,50,256]{2,1,0:T(8,128)(2,1)S(1)} %get-tuple-element.33), channel_id=1, source_target_pairs={{0,2},{1,3},{2,0},{3,1},{4,6},{5,7},{6,4},{7,5},{8,10},{9,11},{10,... | collective-permute-start | bytes 307208 | tf_op jit(solution)/shard_map/ppermute | solution.py:371
  9.7 1.6 %collective-permute-start.4 = (bf16[256,256]{1,0:T(8,128)(2,1)S(1)}, bf16[256,256]{1,0:T(8,128)(2,1)S(1)}, u32[]{:S(2)}, u32[]{:S(2)}) collective-permute-start(bf16[256,256]{1,0:T(8,128)(2,1)S(1)} %get-tuple-element.38), channel_id=1, source_target_pairs={{0,8},{4,12},{8,0},{12,4},{16,24},{20,28},{24,16},{28,20},{1,9},{5... | collective-permute-start | bytes 393224 | tf_op jit(solution)/shard_map/ppermute | solution.py:368
  11.3 1.5 %collective-permute-start.6 = (bf16[256,256]{1,0:T(8,128)(2,1)S(1)}, bf16[256,256]{1,0:T(8,128)(2,1)S(1)}, u32[]{:S(2)}, u32[]{:S(2)}) collective-permute-start(bf16[256,256]{1,0:T(8,128)(2,1)S(1)} %get-tuple-element.40), channel_id=1, source_target_pairs={{0,24},{4,28},{8,16},{12,20},{16,8},{20,12},{24,0},{28,4},{1,25},{... | collective-permute-start | bytes 393224 | tf_op jit(solution)/shard_map/ppermute | solution.py:368
  12.8 1.6 %collective-permute-start = (bf16[5,50,256]{2,1,0:T(8,128)(2,1)S(1)}, bf16[5,50,256]{2,1,0:T(8,128)(2,1)S(1)}, u32[]{:S(2)}, u32[]{:S(2)}) collective-permute-start(bf16[5,50,256]{2,1,0:T(8,128)(2,1)S(1)} %get-tuple-element.32), channel_id=1, source_target_pairs={{0,1},{1,0},{2,3},{3,2},{4,5},{5,4},{6,7},{7,6},{8,9},{9,8},{10,11... | collective-permute-start | bytes 384008 | tf_op jit(solution)/shard_map/ppermute | solution.py:371
  14.4 1.6 %collective-permute-start.2 = (bf16[5,50,256]{2,1,0:T(8,128)(2,1)S(1)}, bf16[5,50,256]{2,1,0:T(8,128)(2,1)S(1)}, u32[]{:S(2)}, u32[]{:S(2)}) collective-permute-start(bf16[5,50,256]{2,1,0:T(8,128)(2,1)S(1)} %get-tuple-element.34), channel_id=1, source_target_pairs={{0,3},{1,2},{2,1},{3,0},{4,7},{5,6},{6,5},{7,4},{8,11},{9,10},{10,... | collective-permute-start | bytes 384008 | tf_op jit(solution)/shard_map/ppermute | solution.py:371
  16.0 1.9 %collective-permute-start.5 = (bf16[208,256]{1,0:T(8,128)(2,1)S(1)}, bf16[208,256]{1,0:T(8,128)(2,1)S(1)}, u32[]{:S(2)}, u32[]{:S(2)}) collective-permute-start(bf16[208,256]{1,0:T(8,128)(2,1)S(1)} %get-tuple-element.39), channel_id=1, source_target_pairs={{0,16},{4,20},{8,24},{12,28},{16,0},{20,4},{24,8},{28,12},{1,17},{... | collective-permute-start | bytes 319496 | tf_op jit(solution)/shard_map/ppermute | solution.py:368
  17.9 1.9 %collective-permute-done.refs_1_ = bf16[5,50,256]{2,1,0:T(8,128)(2,1)S(1)} collective-permute-done((bf16[5,50,256]{2,1,0:T(8,128)(2,1)S(1)}, bf16[5,50,256]{2,1,0:T(8,128)(2,1)S(1)}, u32[]{:S(2)}, u32[]{:S(2)}) %collective-permute-start) | collective-permute-done | bytes 128032 | tf_op jit(solution)/shard_map/ppermute | solution.py:371
  19.8 2.5 %collective-permute-done.2.refs_3_ = bf16[5,50,256]{2,1,0:T(8,128)(2,1)S(1)} collective-permute-done((bf16[5,50,256]{2,1,0:T(8,128)(2,1)S(1)}, bf16[5,50,256]{2,1,0:T(8,128)(2,1)S(1)}, u32[]{:S(2)}, u32[]{:S(2)}) %collective-permute-start.2) | collective-permute-done | bytes 128032 | tf_op jit(solution)/shard_map/ppermute | solution.py:371
  23.7 2.1 %collective-permute-done.7.recv_ref = bf16[1280,256]{1,0:T(8,128)(2,1)S(1)} collective-permute-done((bf16[1280,256]{1,0:T(8,128)(2,1)S(1)}, bf16[1280,256]{1,0:T(8,128)(2,1)S(1)}, u32[]{:S(2)}, u32[]{:S(2)}) %collective-permute-start.7) | collective-permute-done | bytes 655392 | tf_op jit(solution)/shard_map/ppermute | solution.py:365
  26.0 1.6 %collective-permute-start.8 = (bf16[338,256]{1,0:T(8,128)(2,1)S(1)}, bf16[338,256]{1,0:T(8,128)(2,1)S(1)}, u32[]{:S(2)}, u32[]{:S(2)}) collective-permute-start(bf16[338,256]{1,0:T(8,128)(2,1)S(1)} %get-tuple-element.46), channel_id=1, source_target_pairs={{0,8},{4,12},{8,0},{12,4},{16,24},{20,28},{24,16},{28,20},{1,9},{5... | collective-permute-start | bytes 519176 | tf_op jit(solution)/shard_map/ppermute | solution.py:368
  28.2 1.4 %collective-permute-start.9 = (bf16[288,256]{1,0:T(8,128)(2,1)S(1)}, bf16[288,256]{1,0:T(8,128)(2,1)S(1)}, u32[]{:S(2)}, u32[]{:S(2)}) collective-permute-start(bf16[288,256]{1,0:T(8,128)(2,1)S(1)} %get-tuple-element.47), channel_id=1, source_target_pairs={{0,16},{4,20},{8,24},{12,28},{16,0},{20,4},{24,8},{28,12},{1,17},{... | collective-permute-start | bytes 442376 | tf_op jit(solution)/shard_map/ppermute | solution.py:368
  29.6 7.7 %collective-permute-done.9.refs_2_ = bf16[288,256]{1,0:T(8,128)(2,1)S(1)} collective-permute-done((bf16[288,256]{1,0:T(8,128)(2,1)S(1)}, bf16[288,256]{1,0:T(8,128)(2,1)S(1)}, u32[]{:S(2)}, u32[]{:S(2)}) %collective-permute-start.9) | collective-permute-done | bytes 147488 | tf_op jit(solution)/shard_map/ppermute | solution.py:368
  37.5 1.4 %collective-permute-start.11 = (bf16[98,256]{1,0:T(8,128)(2,1)S(1)}, bf16[98,256]{1,0:T(8,128)(2,1)S(1)}, u32[]{:S(2)}, u32[]{:S(2)}) collective-permute-start(bf16[98,256]{1,0:T(8,128)(2,1)S(1)} %get-tuple-element.53), channel_id=1, source_target_pairs={{0,1},{1,0},{2,3},{3,2},{4,5},{5,4},{6,7},{7,6},{8,9},{9,8},{10,11... | collective-permute-start | bytes 150536 | tf_op jit(solution)/shard_map/ppermute | solution.py:371
  38.9 3.4 %collective-permute-start.13 = (bf16[98,256]{1,0:T(8,128)(2,1)S(1)}, bf16[98,256]{1,0:T(8,128)(2,1)S(1)}, u32[]{:S(2)}, u32[]{:S(2)}) collective-permute-start(bf16[98,256]{1,0:T(8,128)(2,1)S(1)} %get-tuple-element.55), channel_id=1, source_target_pairs={{0,3},{1,2},{2,1},{3,0},{4,7},{5,6},{6,5},{7,4},{8,11},{9,10},{10,... | collective-permute-start | bytes 150536 | tf_op jit(solution)/shard_map/ppermute | solution.py:371
  42.3 4.9 %collective-permute-done.12.rest_1_ = bf16[72,256]{1,0:T(8,128)(2,1)S(1)} collective-permute-done((bf16[72,256]{1,0:T(8,128)(2,1)S(1)}, bf16[72,256]{1,0:T(8,128)(2,1)S(1)}, u32[]{:S(2)}, u32[]{:S(2)}) %collective-permute-start.12) | collective-permute-done | bytes 36896 | tf_op jit(solution)/shard_map/ppermute | solution.py:371
  47.4 1.4 %collective-permute-start.15 = (bf16[72,256]{1,0:T(8,128)(2,1)S(1)}, bf16[72,256]{1,0:T(8,128)(2,1)S(1)}, u32[]{:S(2)}, u32[]{:S(2)}) collective-permute-start(bf16[72,256]{1,0:T(8,128)(2,1)S(1)} %add_convert_fusion), channel_id=1, source_target_pairs={{0,2},{1,3},{2,0},{3,1},{4,6},{5,7},{6,4},{7,5},{8,10},{9,11},{10,... | collective-permute-start | bytes 110600 | tf_op jit(solution)/shard_map/ppermute | solution.py:371
  48.9 2.8 %collective-permute-start.14 = (bf16[72,256]{1,0:T(8,128)(2,1)S(1)}, bf16[72,256]{1,0:T(8,128)(2,1)S(1)}, u32[]{:S(2)}, u32[]{:S(2)}) collective-permute-start(bf16[72,256]{1,0:T(8,128)(2,1)S(1)} %add_convert_fusion), channel_id=1, source_target_pairs={{0,3},{1,2},{2,1},{3,0},{4,7},{5,6},{6,5},{7,4},{8,11},{9,10},{10,... | collective-permute-start | bytes 110600 | tf_op jit(solution)/shard_map/ppermute | solution.py:371
  52.3 2.3 %collective-permute-done.14 = bf16[72,256]{1,0:T(8,128)(2,1)S(1)} collective-permute-done((bf16[72,256]{1,0:T(8,128)(2,1)S(1)}, bf16[72,256]{1,0:T(8,128)(2,1)S(1)}, u32[]{:S(2)}, u32[]{:S(2)}) %collective-permute-start.14) | collective-permute-done | bytes 36896 | tf_op jit(solution)/shard_map/ppermute | solution.py:371
  54.7 1.6 %collective-permute-start.19 = (bf16[288,256]{1,0:T(8,128)(2,1)S(1)}, bf16[288,256]{1,0:T(8,128)(2,1)S(1)}, u32[]{:S(2)}, u32[]{:S(2)}) collective-permute-start(bf16[288,256]{1,0:T(8,128)(2,1)S(1)} %pad_maximum_fusion.2), channel_id=1, source_target_pairs={{0,8},{4,12},{8,0},{12,4},{16,24},{20,28},{24,16},{28,20},{1,9},{5... | collective-permute-start | bytes 442376 | tf_op jit(solution)/shard_map/ppermute | solution.py:368
  58.2 1.7 %collective-permute-done.19 = bf16[288,256]{1,0:T(8,128)(2,1)S(1)} collective-permute-done((bf16[288,256]{1,0:T(8,128)(2,1)S(1)}, bf16[288,256]{1,0:T(8,128)(2,1)S(1)}, u32[]{:S(2)}, u32[]{:S(2)}) %collective-permute-start.19) | collective-permute-done | bytes 147488 | tf_op jit(solution)/shard_map/ppermute | solution.py:368
  59.9 1.5 %collective-permute-done.18 = bf16[288,256]{1,0:T(8,128)(2,1)S(1)} collective-permute-done((bf16[288,256]{1,0:T(8,128)(2,1)S(1)}, bf16[288,256]{1,0:T(8,128)(2,1)S(1)}, u32[]{:S(2)}, u32[]{:S(2)}) %collective-permute-start.18) | collective-permute-done | bytes 147488 | tf_op jit(solution)/shard_map/ppermute | solution.py:368
  61.4 1.9 %collective-permute-done.17 = bf16[288,256]{1,0:T(8,128)(2,1)S(1)} collective-permute-done((bf16[288,256]{1,0:T(8,128)(2,1)S(1)}, bf16[288,256]{1,0:T(8,128)(2,1)S(1)}, u32[]{:S(2)}, u32[]{:S(2)}) %collective-permute-start.17) | collective-permute-done | bytes 147488 | tf_op jit(solution)/shard_map/ppermute | solution.py:368
  66.4 1.6 %convert.1 = f32[3,3,256,256]{3,2,1,0:T(8,128)} convert(bf16[3,3,256,256]{3,2,1,0:T(8,128)(2,1)S(1)} %bitcast.11) | non-fusion elementwise | flops 589824 | bytes 3538944 | tf_op jit(solution)/shard_map/convert_element_type | solution.py:437
  (39 shorter events, 8.9 us)
Async XLA Ops:
  5.4 16.9 %copy-start.1 = (bf16[4,48,256]{2,1,0:T(8,128)(2,1)S(1)}, bf16[4,48,256]{2,1,0:T(8,128)(2,1)}, u32[]{:S(2)}) copy-start(bf16[4,48,256]{2,1,0:T(8,128)(2,1)} %refs_9_.1) | copy-start | bytes 294916
  5.5 16.9 %copy-start.2 = (bf16[24,8,256]{2,1,0:T(8,128)(2,1)S(1)}, bf16[24,8,256]{2,1,0:T(8,128)(2,1)}, u32[]{:S(2)}) copy-start(bf16[24,8,256]{2,1,0:T(8,128)(2,1)} %refs_10_.1) | copy-start | bytes 294916
  5.5 4.2 %collective-permute-start.3 = (bf16[928,256]{1,0:T(8,128)(2,1)S(1)}, bf16[928,256]{1,0:T(8,128)(2,1)S(1)}, u32[]{:S(2)}, u32[]{:S(2)}) collective-permute-start(bf16[928,256]{1,0:T(8,128)(2,1)S(1)} %get-tuple-element.36), channel_id=1, source_target_pairs={{0,4},{4,0},{8,12},{12,8},{16,20},{20,16},{24,28},{28,24},{1,5},{5... | collective-permute-start | bytes 1425416 | tf_op jit(solution)/shard_map/ppermute | solution.py:365
  6.0 10.0 %collective-permute-start.1 = (bf16[4,50,256]{2,1,0:T(8,128)(2,1)S(1)}, bf16[4,50,256]{2,1,0:T(8,128)(2,1)S(1)}, u32[]{:S(2)}, u32[]{:S(2)}) collective-permute-start(bf16[4,50,256]{2,1,0:T(8,128)(2,1)S(1)} %get-tuple-element.33), channel_id=1, source_target_pairs={{0,2},{1,3},{2,0},{3,1},{4,6},{5,7},{6,4},{7,5},{8,10},{9,11},{10,... | collective-permute-start | bytes 307208 | tf_op jit(solution)/shard_map/ppermute | solution.py:371
  9.7 12.6 %collective-permute-start.4 = (bf16[256,256]{1,0:T(8,128)(2,1)S(1)}, bf16[256,256]{1,0:T(8,128)(2,1)S(1)}, u32[]{:S(2)}, u32[]{:S(2)}) collective-permute-start(bf16[256,256]{1,0:T(8,128)(2,1)S(1)} %get-tuple-element.38), channel_id=1, source_target_pairs={{0,8},{4,12},{8,0},{12,4},{16,24},{20,28},{24,16},{28,20},{1,9},{5... | collective-permute-start | bytes 393224 | tf_op jit(solution)/shard_map/ppermute | solution.py:368
  11.3 11.1 %collective-permute-start.6 = (bf16[256,256]{1,0:T(8,128)(2,1)S(1)}, bf16[256,256]{1,0:T(8,128)(2,1)S(1)}, u32[]{:S(2)}, u32[]{:S(2)}) collective-permute-start(bf16[256,256]{1,0:T(8,128)(2,1)S(1)} %get-tuple-element.40), channel_id=1, source_target_pairs={{0,24},{4,28},{8,16},{12,20},{16,8},{20,12},{24,0},{28,4},{1,25},{... | collective-permute-start | bytes 393224 | tf_op jit(solution)/shard_map/ppermute | solution.py:368
  12.8 7.0 %collective-permute-start = (bf16[5,50,256]{2,1,0:T(8,128)(2,1)S(1)}, bf16[5,50,256]{2,1,0:T(8,128)(2,1)S(1)}, u32[]{:S(2)}, u32[]{:S(2)}) collective-permute-start(bf16[5,50,256]{2,1,0:T(8,128)(2,1)S(1)} %get-tuple-element.32), channel_id=1, source_target_pairs={{0,1},{1,0},{2,3},{3,2},{4,5},{5,4},{6,7},{7,6},{8,9},{9,8},{10,11... | collective-permute-start | bytes 384008 | tf_op jit(solution)/shard_map/ppermute | solution.py:371
  14.4 8.0 %collective-permute-start.2 = (bf16[5,50,256]{2,1,0:T(8,128)(2,1)S(1)}, bf16[5,50,256]{2,1,0:T(8,128)(2,1)S(1)}, u32[]{:S(2)}, u32[]{:S(2)}) collective-permute-start(bf16[5,50,256]{2,1,0:T(8,128)(2,1)S(1)} %get-tuple-element.34), channel_id=1, source_target_pairs={{0,3},{1,2},{2,1},{3,0},{4,7},{5,6},{6,5},{7,4},{8,11},{9,10},{10,... | collective-permute-start | bytes 384008 | tf_op jit(solution)/shard_map/ppermute | solution.py:371
  16.0 6.3 %collective-permute-start.5 = (bf16[208,256]{1,0:T(8,128)(2,1)S(1)}, bf16[208,256]{1,0:T(8,128)(2,1)S(1)}, u32[]{:S(2)}, u32[]{:S(2)}) collective-permute-start(bf16[208,256]{1,0:T(8,128)(2,1)S(1)} %get-tuple-element.39), channel_id=1, source_target_pairs={{0,16},{4,20},{8,24},{12,28},{16,0},{20,4},{24,8},{28,12},{1,17},{... | collective-permute-start | bytes 319496 | tf_op jit(solution)/shard_map/ppermute | solution.py:368
  23.7 2.2 %collective-permute-start.7 = (bf16[1280,256]{1,0:T(8,128)(2,1)S(1)}, bf16[1280,256]{1,0:T(8,128)(2,1)S(1)}, u32[]{:S(2)}, u32[]{:S(2)}) collective-permute-start(bf16[1280,256]{1,0:T(8,128)(2,1)S(1)} %get-tuple-element.44), channel_id=1, source_target_pairs={{0,4},{4,0},{8,12},{12,8},{16,20},{20,16},{24,28},{28,24},{1,5},{5... | collective-permute-start | bytes 1966088 | tf_op jit(solution)/shard_map/ppermute | solution.py:365
  26.0 11.3 %collective-permute-start.8 = (bf16[338,256]{1,0:T(8,128)(2,1)S(1)}, bf16[338,256]{1,0:T(8,128)(2,1)S(1)}, u32[]{:S(2)}, u32[]{:S(2)}) collective-permute-start(bf16[338,256]{1,0:T(8,128)(2,1)S(1)} %get-tuple-element.46), channel_id=1, source_target_pairs={{0,8},{4,12},{8,0},{12,4},{16,24},{20,28},{24,16},{28,20},{1,9},{5... | collective-permute-start | bytes 519176 | tf_op jit(solution)/shard_map/ppermute | solution.py:368
  27.6 9.7 %collective-permute-start.10 = (bf16[338,256]{1,0:T(8,128)(2,1)S(1)}, bf16[338,256]{1,0:T(8,128)(2,1)S(1)}, u32[]{:S(2)}, u32[]{:S(2)}) collective-permute-start(bf16[338,256]{1,0:T(8,128)(2,1)S(1)} %get-tuple-element.48), channel_id=1, source_target_pairs={{0,24},{4,28},{8,16},{12,20},{16,8},{20,12},{24,0},{28,4},{1,25},{... | collective-permute-start | bytes 519176 | tf_op jit(solution)/shard_map/ppermute | solution.py:368
  28.2 9.1 %collective-permute-start.9 = (bf16[288,256]{1,0:T(8,128)(2,1)S(1)}, bf16[288,256]{1,0:T(8,128)(2,1)S(1)}, u32[]{:S(2)}, u32[]{:S(2)}) collective-permute-start(bf16[288,256]{1,0:T(8,128)(2,1)S(1)} %get-tuple-element.47), channel_id=1, source_target_pairs={{0,16},{4,20},{8,24},{12,28},{16,0},{20,4},{24,8},{28,12},{1,17},{... | collective-permute-start | bytes 442376 | tf_op jit(solution)/shard_map/ppermute | solution.py:368
  37.5 9.6 %collective-permute-start.11 = (bf16[98,256]{1,0:T(8,128)(2,1)S(1)}, bf16[98,256]{1,0:T(8,128)(2,1)S(1)}, u32[]{:S(2)}, u32[]{:S(2)}) collective-permute-start(bf16[98,256]{1,0:T(8,128)(2,1)S(1)} %get-tuple-element.53), channel_id=1, source_target_pairs={{0,1},{1,0},{2,3},{3,2},{4,5},{5,4},{6,7},{7,6},{8,9},{9,8},{10,11... | collective-permute-start | bytes 150536 | tf_op jit(solution)/shard_map/ppermute | solution.py:371
  38.9 8.3 %collective-permute-start.13 = (bf16[98,256]{1,0:T(8,128)(2,1)S(1)}, bf16[98,256]{1,0:T(8,128)(2,1)S(1)}, u32[]{:S(2)}, u32[]{:S(2)}) collective-permute-start(bf16[98,256]{1,0:T(8,128)(2,1)S(1)} %get-tuple-element.55), channel_id=1, source_target_pairs={{0,3},{1,2},{2,1},{3,0},{4,7},{5,6},{6,5},{7,4},{8,11},{9,10},{10,... | collective-permute-start | bytes 150536 | tf_op jit(solution)/shard_map/ppermute | solution.py:371
  42.3 4.9 %collective-permute-start.12 = (bf16[72,256]{1,0:T(8,128)(2,1)S(1)}, bf16[72,256]{1,0:T(8,128)(2,1)S(1)}, u32[]{:S(2)}, u32[]{:S(2)}) collective-permute-start(bf16[72,256]{1,0:T(8,128)(2,1)S(1)} %get-tuple-element.54), channel_id=1, source_target_pairs={{0,2},{1,3},{2,0},{3,1},{4,6},{5,7},{6,4},{7,5},{8,10},{9,11},{10,... | collective-permute-start | bytes 110600 | tf_op jit(solution)/shard_map/ppermute | solution.py:371
  47.2 4.5 %collective-permute-start.16 = (bf16[72,256]{1,0:T(8,128)(2,1)S(1)}, bf16[72,256]{1,0:T(8,128)(2,1)S(1)}, u32[]{:S(2)}, u32[]{:S(2)}) collective-permute-start(bf16[72,256]{1,0:T(8,128)(2,1)S(1)} %add_convert_fusion), channel_id=1, source_target_pairs={{0,1},{1,0},{2,3},{3,2},{4,5},{5,4},{6,7},{7,6},{8,9},{9,8},{10,11... | collective-permute-start | bytes 110600 | tf_op jit(solution)/shard_map/ppermute | solution.py:371
  47.4 4.9 %collective-permute-start.15 = (bf16[72,256]{1,0:T(8,128)(2,1)S(1)}, bf16[72,256]{1,0:T(8,128)(2,1)S(1)}, u32[]{:S(2)}, u32[]{:S(2)}) collective-permute-start(bf16[72,256]{1,0:T(8,128)(2,1)S(1)} %add_convert_fusion), channel_id=1, source_target_pairs={{0,2},{1,3},{2,0},{3,1},{4,6},{5,7},{6,4},{7,5},{8,10},{9,11},{10,... | collective-permute-start | bytes 110600 | tf_op jit(solution)/shard_map/ppermute | solution.py:371
  48.9 5.8 %collective-permute-start.14 = (bf16[72,256]{1,0:T(8,128)(2,1)S(1)}, bf16[72,256]{1,0:T(8,128)(2,1)S(1)}, u32[]{:S(2)}, u32[]{:S(2)}) collective-permute-start(bf16[72,256]{1,0:T(8,128)(2,1)S(1)} %add_convert_fusion), channel_id=1, source_target_pairs={{0,3},{1,2},{2,1},{3,0},{4,7},{5,6},{6,5},{7,4},{8,11},{9,10},{10,... | collective-permute-start | bytes 110600 | tf_op jit(solution)/shard_map/ppermute | solution.py:371
  54.7 5.2 %collective-permute-start.19 = (bf16[288,256]{1,0:T(8,128)(2,1)S(1)}, bf16[288,256]{1,0:T(8,128)(2,1)S(1)}, u32[]{:S(2)}, u32[]{:S(2)}) collective-permute-start(bf16[288,256]{1,0:T(8,128)(2,1)S(1)} %pad_maximum_fusion.2), channel_id=1, source_target_pairs={{0,8},{4,12},{8,0},{12,4},{16,24},{20,28},{24,16},{28,20},{1,9},{5... | collective-permute-start | bytes 442376 | tf_op jit(solution)/shard_map/ppermute | solution.py:368
  56.3 5.1 %collective-permute-start.18 = (bf16[288,256]{1,0:T(8,128)(2,1)S(1)}, bf16[288,256]{1,0:T(8,128)(2,1)S(1)}, u32[]{:S(2)}, u32[]{:S(2)}) collective-permute-start(bf16[288,256]{1,0:T(8,128)(2,1)S(1)} %pad_maximum_fusion.2), channel_id=1, source_target_pairs={{0,16},{4,20},{8,24},{12,28},{16,0},{20,4},{24,8},{28,12},{1,17},{... | collective-permute-start | bytes 442376 | tf_op jit(solution)/shard_map/ppermute | solution.py:368
  57.3 6.0 %collective-permute-start.17 = (bf16[288,256]{1,0:T(8,128)(2,1)S(1)}, bf16[288,256]{1,0:T(8,128)(2,1)S(1)}, u32[]{:S(2)}, u32[]{:S(2)}) collective-permute-start(bf16[288,256]{1,0:T(8,128)(2,1)S(1)} %pad_maximum_fusion.2), channel_id=1, source_target_pairs={{0,24},{4,28},{8,16},{12,20},{16,8},{20,12},{24,0},{28,4},{1,25},{... | collective-permute-start | bytes 442376 | tf_op jit(solution)/shard_map/ppermute | solution.py:368
  63.4 1.3 %copy-start = (bf16[3,3,256,256]{3,2,1,0:T(8,128)(2,1)S(1)}, bf16[3,3,256,256]{3,2,1,0:T(8,128)(2,1)}, u32[]{:S(2)}) copy-start(bf16[3,3,256,256]{3,2,1,0:T(8,128)(2,1)} %param.11) | copy-start | bytes 3538948
  63.6 2.4 %collective-permute-start.20 = (bf16[1152,256]{1,0:T(8,128)(2,1)S(1)}, bf16[1152,256]{1,0:T(8,128)(2,1)S(1)}, u32[]{:S(2)}, u32[]{:S(2)}) collective-permute-start(bf16[1152,256]{1,0:T(8,128)(2,1)S(1)} %pad_maximum_fusion.1), channel_id=1, source_target_pairs={{0,4},{4,0},{8,12},{12,8},{16,20},{20,16},{24,28},{28,24},{1,5},{5... | collective-permute-start | bytes 1769480 | tf_op jit(solution)/shard_map/ppermute | solution.py:365

commit v3 on v2

--- a/solution.py
+++ b/solution.py
@@ -15,16 +15,6 @@
 
 def flip(count, mask):
     return [(i, i ^ mask) for i in range(count)]
-
-
-def ordered(parts, index):
-    count = len(parts)
-    bit = 1
-    while bit < count:
-        swap = (index & bit) != 0
-        parts = [jnp.where(swap, parts[a ^ bit], parts[a]) for a in range(count)]
-        bit *= 2
-    return parts
 
 
 def put(ref, rows, value):
@@ -100,23 +90,24 @@
     cells = cells_ref[...].astype(BF16)
     for copy in copies[1:]:
         copy.wait()
+    query = lax.dot_general(cells, a_ref[...], (((0,), (0,)), ((), ())), preferred_element_type=F32).T * scale
 
     last_row = ki_ref[...].astype(F32)
     first_row, last_row = last_row[:, 0], last_row[:, key_rows - 1]
+    wide = tile_q + 2
     for s in range(1, n_ka):
         if joins(s):
-            q_outs[s][rows, 0:tile_k] = jnp.where((z ^ s) == z + 1, last_row, first_row).astype(BF16)
+            stage_ref[s, rows * wide : rows * wide + tile_k, :] = jnp.where((z ^ s) == z + 1, last_row, first_row)
     base = n_quad * (tile_k + 2) * key_rows
     send_ref[base : base + tile_q, :] = qi_ref[0]
     send_ref[base + up16(tile_q) : base + up16(tile_q) + tile_q, :] = qi_ref[rows - 1]
-    query = lax.dot_general(cells, a_ref[...], (((0,), (0,)), ((), ())), preferred_element_type=F32).T * scale
     coarse_ref[...] = jnp.dot(a_ref[...], q_ref[...], preferred_element_type=F32)
     for row in range(rows):
         qpad_ref[8 : 8 + width, :] = query[row * width : (row + 1) * width]
         for k in range(n_ka):
-            stage_ref[z ^ k, 0 : tile_q + 2, :] = qpad_ref[7 + tile_q * k : 9 + tile_q * (k + 1), :]
-        for s in range(n_ka):
-            q_outs[s][row] = stage_ref[s, 0 : tile_q + 2, :].astype(BF16)
+            stage_ref[z ^ k, row * wide : (row + 1) * wide, :] = qpad_ref[7 + tile_q * k : 9 + tile_q * (k + 1), :]
+    for s in range(n_ka):
+        q_outs[s][...] = stage_ref[s, 0 : q_outs[s].shape[0], :].astype(BF16)
 
     offsets = [0]
     for level in range(LEVELS):
@@ -155,6 +146,7 @@
     tile_q = width // n_ka
     tile_k = width // (2 * n_quad)
     size = (tile_k + 2) * key_rows
+    counts = [rows * (tile_q + 2) + (tile_k if s and joins(s) else 0) for s in range(n_ka)]
     chunk = 256
     hbm = pl.BlockSpec(memory_space=pltpu.HBM)
     vmem = pl.BlockSpec(memory_space=pltpu.VMEM)
@@ -164,7 +156,9 @@
         functools.partial(corr_kernel, dims),
         in_specs=[hbm] * 5,
         out_specs=[vmem] * (n_ka + 2),
-        out_shape=[jax.ShapeDtypeStruct((rows + (s > 0 and joins(s)), tile_q + 2, channels), BF16) for s in range(n_ka)]
+        out_shape=[
+            jax.ShapeDtypeStruct((count, channels), BF16) for count in counts
+        ]
         + [
             jax.ShapeDtypeStruct((n_quad * size + 2 * up16(tile_q), channels), BF16),
             jax.ShapeDtypeStruct((n_quad, size, channels), F32),
@@ -179,7 +173,7 @@
             pltpu.VMEM((lanes, width, 128), F32),
             pltpu.VMEM((lanes, (width + 2) * key_rows, 128), F32),
             pltpu.VMEM((width + 16, channels), F32),
-            pltpu.VMEM((n_ka, tile_q + 8, channels), F32),
+            pltpu.VMEM((n_ka, up16(max(counts)), channels), F32),
             pltpu.VMEM(query_image.shape, BF16),
             pltpu.VMEM(key_image.shape, BF16),
             pltpu.SemaphoreType.DMA((count // chunk + 4,)),
@@ -217,13 +211,13 @@
     k_refs = refs[n_ka : n_ka + n_quad]
     near_ref, qi_ref, ki_ref = refs[n_ka + n_quad : n_ka + n_quad + 3]
     send_ref, keep_ref, gq_ref, gk_ref, acc_ref, sum_ref, ext_ref = refs[n_ka + n_quad + 3 :]
-    rows, wide, channels = gq_ref.shape
-    size = gk_ref.shape[0]
+    size, channels = gk_ref.shape
     tile_k, key_rows, cin = ki_ref.shape
-    tile_q = wide - 2
+    rows, tile_q, _ = qi_ref.shape
+    wide = tile_q + 2
     quad, core, z = place()
     top, bottom = both_sides(k_refs[1:], near_ref, size, quad, core)
-    lines = [(s, ref[rows, 0:tile_k].astype(F32)) for s, ref in enumerate(q_refs) if s and joins(s)]
+    lines = [(s, ref[rows * wide : rows * wide + tile_k, :].astype(F32)) for s, ref in enumerate(q_refs) if s and joins(s)]
     ext_ref[:, 8 : 8 + key_rows, :] = ki_ref[...].astype(F32)
     ext_ref[:, 7, :] = carried(lines, z, -1)
     ext_ref[:, 8 + key_rows, :] = carried(lines, z, 1)
@@ -236,10 +230,10 @@
     image = jnp.concatenate(image, axis=0)
     query = q_refs[0][...].astype(F32)
     for ref in q_refs[1:]:
-        query = query + ref[0:rows].astype(F32)
+        query = query + ref[0 : rows * wide, :].astype(F32)
     gq = query.astype(BF16)
     gq_ref[...] = gq
-    sum_ref[:, 0:wide, :] = gq.astype(F32)
+    sum_ref[...] = gq.astype(F32)
     key = k_refs[0][...]
     for ref in k_refs[1:]:
         key = key + ref[0:size, :].astype(F32)
@@ -247,7 +241,8 @@
     gk_ref[...] = gk
     count = tile_k * key_rows
     for b in (-1, 0, 1):
-        first = sum_ref[:, 1 - b : 1 - b + tile_q, :].reshape(rows * tile_q, channels).astype(BF16)
+        starts = [row * wide + 1 - b for row in range(rows)]
+        first = jnp.concatenate([sum_ref[start : start + tile_q, :] for start in starts], axis=0).astype(BF16)
         grad = jnp.concatenate([first, gk[(1 - b) * key_rows : (1 - b) * key_rows + count]], axis=0)
         part = jnp.dot(image, grad, preferred_element_type=F32)
         for a in range(3):
@@ -256,8 +251,8 @@
     half = keep_ref.shape[0]
     keep_ref[...] = acc_ref[pl.ds(pl.multiple_of(core * half, 16), half), :]
     send_ref[0:half, :] = acc_ref[pl.ds(pl.multiple_of((1 - core) * half, 16), half), :].astype(BF16)
-    send_ref[half : half + wide, :] = gq[0]
-    send_ref[half + up16(wide) : half + up16(wide) + wide, :] = gq[rows - 1]
+    first, last = sum_ref[0:wide, :], sum_ref[(rows - 1) * wide : rows * wide, :]
+    send_ref[half : half + wide, :] = jnp.where(core == 0, last, first).astype(BF16)
 
 
 def piece_kernel(keep_ref, recv_ref, own_ref, near_ref, *rest):
@@ -266,56 +261,67 @@
     half = keep_ref.shape[0]
     size = own_ref.shape[0]
     tile = near_ref.shape[0]
-    first = recv_ref[half : half + tile, :].astype(F32)
-    last = recv_ref[half + up16(tile) : half + up16(tile) + tile, :].astype(F32)
-    near_ref[...] = jnp.where(core == 0, first, last).astype(BF16)
-    onward = jnp.where(core == 0, last, first).astype(BF16)
+    near_ref[...] = recv_ref[half : half + tile, :]
     sum_ref[...] = keep_ref[...] + recv_ref[0:half, :].astype(F32)
     own_ref[...] = sum_ref[pl.ds(pl.multiple_of(quad * size, 16), size), :]
     for s, send in enumerate(sends, 1):
-        send[0:size, :] = sum_ref[pl.ds(pl.multiple_of((quad ^ s) * size, 16), size), :].astype(BF16)
-        if joins(s):
-            send[size : size + tile, :] = onward
-
-
-def layer_kernel(n_quad, n_ka, *refs):
+        send[...] = sum_ref[pl.ds(pl.multiple_of((quad ^ s) * size, 16), size), :].astype(BF16)
+
+
+def layer_kernel(n_quad, rows, *refs):
     own_ref, *got = refs[:n_quad]
-    near_ref, gk_ref, out_ref, top_ref, bottom_ref = refs[n_quad : n_quad + 5]
-    sends = refs[n_quad + 5 : n_quad + 4 + n_ka]
-    stage_ref, ext_ref = refs[n_quad + 4 + n_ka :]
-    quad, core, z = place()
+    gq_ref, out_ref, far_ref, *sends, stage_ref = refs[n_quad:]
+    _, core, z = place()
+    n_ka = len(sends) + 1
     size = own_ref.shape[0]
     piece = size // n_ka
-    top, bottom = both_sides(got, near_ref, size, quad, core)
-    top_ref[...] = top.astype(BF16)
-    bottom_ref[...] = bottom.astype(BF16)
     total = own_ref[...]
     for ref in got:
-        total = total + ref[0:size, :].astype(F32)
+        total = total + ref[...].astype(F32)
     for k in range(n_ka):
         stage_ref[z ^ k, 0:piece, :] = total[k * piece : (k + 1) * piece]
     out_ref[...] = stage_ref[0, 0:piece, :]
+    for s, send in enumerate(sends, 1):
+        send[...] = stage_ref[s, 0:piece, :].astype(BF16)
+    query = gq_ref[...].astype(F32)
+    wide = query.shape[0] // rows
+    far_ref[...] = jnp.where(core == 0, query[0:wide], query[(rows - 1) * wide :]).astype(BF16)
+
+
+def combine_kernel(n_ka, *refs):
+    own_ref, *got = refs[:n_ka]
+    gk_ref, out_ref, *sends, ext_ref = refs[n_ka:]
+    _, _, z = place()
+    piece = own_ref.shape[0]
+    total = own_ref[...]
+    for ref in got:
+        total = total + ref[...].astype(F32)
+    total = total.astype(BF16)
+    out_ref[...] = total
     tall, key_rows, _ = ext_ref.shape
     ext_ref[...] = gk_ref[...].astype(F32).reshape(ext_ref.shape)
     first, last = ext_ref[:, 0, :], ext_ref[:, key_rows - 1, :]
     for s, send in enumerate(sends, 1):
-        send[0:piece, :] = stage_ref[s, 0:piece, :].astype(BF16)
+        send[0:piece, :] = total
         if joins(s):
             send[piece : piece + tall, :] = jnp.where((z ^ s) == z + 1, last, first).astype(BF16)
 
 
-def image_kernel(piece, gq_ref, top_ref, bottom_ref, gk_ref, w_ref, *rest):
-    *got, qo_ref, ko_ref, qext_ref, kext_ref = rest
-    rows, wide, channels = gq_ref.shape
+def image_kernel(piece, rows, gq_ref, near_ref, far_ref, gk_ref, w_ref, *rest):
+    *got, qo_ref, ko_ref, end_ref, qext_ref, kext_ref = rest
+    wide, channels = near_ref.shape
     tall = kext_ref.shape[0]
     key_rows = gk_ref.shape[0] // tall
     tile_q = wide - 2
     tile_k = tall - 2
-    _, _, z = place()
+    _, core, z = place()
+    near, far = near_ref[...].astype(F32), far_ref[...].astype(F32)
     lines = [(s, ref[piece : piece + tall, :].astype(F32)) for s, ref in enumerate(got, 1) if joins(s)]
-    qext_ref[0, 0:wide, :] = top_ref[...].astype(F32)
-    qext_ref[1 : rows + 1, 0:wide, :] = gq_ref[...].astype(F32)
-    qext_ref[rows + 1, 0:wide, :] = bottom_ref[...].astype(F32)
+    qext_ref[0, 0:wide, :] = jnp.where(core == 0, far, near)
+    query = gq_ref[...].astype(F32)
+    for row in range(rows):
+        qext_ref[row + 1, 0:wide, :] = query[row * wide : (row + 1) * wide]
+    qext_ref[rows + 1, 0:wide, :] = jnp.where(core == 0, near, far)
     kext_ref[:, 8 : 8 + key_rows, :] = gk_ref[...].astype(F32).reshape(tall, key_rows, channels)
     kext_ref[:, 7, :] = carried(lines, z, -1)
     kext_ref[:, 8 + key_rows, :] = carried(lines, z, 1)
@@ -330,17 +336,62 @@
     count = qo_ref.shape[0]
     qo_ref[...] = total[:count].astype(BF16)
     ko_ref[...] = total[count:].astype(BF16)
-
-
-def call(kernel, name, outs, args, scratch=()):
+    end_ref[...] = jnp.zeros_like(end_ref)
+
+
+def gather_kernel(count, axis, *refs):
+    z = place()[axis]
+    *_, out_ref, stage_ref = refs
+    piece = refs[0].shape[0]
+    for s in range(count):
+        stage_ref[z ^ s, 0:piece, :] = refs[s][0:piece, :].astype(F32)
+    for k in range(count):
+        out_ref[k * piece : (k + 1) * piece, :] = stage_ref[k, 0:piece, :].astype(BF16)
+
+
+def widen_kernel(other, *refs):
+    half_ref, out_hbm, wide_ref, sems = refs[0], *refs[-3:]
+    _, core, _ = place()
+    half = half_ref.shape[0]
+    count = sems.shape[0]
+    size = half // count
+    base = (1 - core if other else core) * half
+    copies = []
+    for i in range(count):
+        wide_ref[i * size : (i + 1) * size, :] = half_ref[i * size : (i + 1) * size, :].astype(F32)
+        rows = pl.ds(pl.multiple_of(base + i * size, 8), size)
+        copies.append(pltpu.make_async_copy(wide_ref.at[pl.ds(i * size, size)], out_hbm.at[rows], sems.at[i]))
+        copies[-1].start()
+    for copy in copies:
+        copy.wait()
+
+
+def widen(half, whole=None):
+    rows, channels = half.shape
+    hbm = pl.BlockSpec(memory_space=pltpu.HBM)
+    vmem = pl.BlockSpec(memory_space=pltpu.VMEM)
+    more = [] if whole is None else [pltpu.with_memory_space_constraint(whole, pltpu.HBM)]
+    return pl.pallas_call(
+        functools.partial(widen_kernel, whole is not None),
+        in_specs=[vmem] + [hbm] * len(more),
+        out_specs=hbm,
+        out_shape=jax.ShapeDtypeStruct((2 * rows, channels), F32),
+        scratch_shapes=[pltpu.VMEM((rows, channels), F32), pltpu.SemaphoreType.DMA((4,))],
+        input_output_aliases={1: 0} if more else {},
+        compiler_params=pltpu.CompilerParams(vmem_limit_bytes=SMALL_BYTES),
+        name="widen",
+    )(half, *more)
+
+
+def call(kernel, name, outs, args, scratch=(), after=()):
     return pl.pallas_call(
         kernel,
-        in_specs=[pl.BlockSpec(memory_space=pltpu.VMEM)] * len(args),
+        in_specs=[pl.BlockSpec(memory_space=pltpu.VMEM)] * len(args) + [pl.BlockSpec(memory_space=pl.ANY)] * len(after),
         out_shape=[jax.ShapeDtypeStruct(shape, dtype) for shape, dtype in outs],
         scratch_shapes=[pltpu.VMEM(shape, F32) for shape in scratch],
         compiler_params=pltpu.CompilerParams(vmem_limit_bytes=SMALL_BYTES),
         name=name,
-    )(*args)
+    )(*args, *after)
 
 
 def body(query_features, key_features, pyramid_grad, query_image, key_image, conv_weight):
@@ -367,6 +418,10 @@
     def to_quad(parts):
         return [lax.ppermute(x, "pb", flip(n_pb, 2 * s)) for s, x in enumerate(parts, 1)]
 
+    def to_chip(x):
+        links = [(i, i + 1) for i in range(1, n_pb - 1, 2)]
+        return lax.ppermute(x, "pb", links + [(d, s) for s, d in links])
+
     def to_layers(parts):
         return [lax.ppermute(x, "ka", flip(n_ka, s)) for s, x in enumerate(parts, 1)]
 
@@ -392,9 +447,9 @@
     k_own, near, *k_pair = call(functools.partial(pair_kernel, size, tile_q), "pairs", outs, (k_keep, k_recv))
     k_more = to_quad(k_pair)
     outs = [
-        ((half + 2 * up16(wide), channels), BF16),
+        ((half + wide, channels), BF16),
         ((half, channels), F32),
-        ((strip_rows, wide, channels), BF16),
+        ((strip_rows * wide, channels), BF16),
         ((size, channels), BF16),
     ]
     w_send, w_keep, gq, gk = call(
@@ -402,39 +457,58 @@
         "weights",
         outs,
         (q_parts[0], *q_recv, k_own, *k_more, near, query_image, key_image),
-        [(taps * cin, channels), (strip_rows, up16(wide), channels), (tile_k, key_rows + 16, cin)],
+        [(taps * cin, channels), (strip_rows * wide, channels), (tile_k, key_rows + 16, cin)],
     )
 
     w_recv = to_core(w_send)
     outs = [((quarter, channels), F32), ((wide, channels), BF16)]
-    outs += [((extra(quarter, s, wide), channels), BF16) for s in range(1, n_quad)]
+    outs += [((quarter, channels), BF16)] * (n_quad - 1)
     own, near, *sends = call(piece_kernel, "pieces", outs, (w_keep, w_recv), [(half, channels)])
     got = to_quad(sends)
-    outs = [((piece, channels), F32)] + [((wide, channels), BF16)] * 2
-    outs += [((extra(piece, s, tall), channels), BF16) for s in range(1, n_ka)]
-    own, top, bottom, *sends = call(
-        functools.partial(layer_kernel, n_quad, n_ka),
+    own, far, *sends = call(
+        functools.partial(layer_kernel, n_quad, strip_rows),
         "layers",
-        outs,
-        (own, *got, near, gk),
-        [(n_ka, up16(piece), channels), (tall, key_rows, channels)],
+        [((piece, channels), F32), ((wide, channels), BF16)] + [((piece, channels), BF16)] * (n_ka - 1),
+        (own, *got, gq),
+        [(n_ka, up16(piece), channels)],
     )
     got = to_layers(sends)
-    part = sum([x[:piece].astype(F32) for x in got], own).astype(BF16)
-    q_out, k_out = call(
-        functools.partial(image_kernel, piece),
+    far = to_chip(far)
+    part, *sends = call(
+        functools.partial(combine_kernel, n_ka),
+        "combine",
+        [((piece, channels), BF16)] + [((extra(piece, s, tall), channels), BF16) for s in range(1, n_ka)],
+        (own, *got, gk),
+        [(tall, key_rows, channels)],
+    )
+    got = to_layers(sends)
+    (part,) = call(
+        functools.partial(gather_kernel, n_ka, 2),
+        "gather",
+        [((quarter, channels), BF16)],
+        (part, *got),
+        [(n_ka, up16(piece), channels)],
+    )
+    q_out, k_out, end = call(
+        functools.partial(image_kernel, piece, strip_rows),
         "images",
-        [((strip_rows * tile_q, cin), BF16), ((tile_k * key_rows, cin), BF16)],
-        (gq, top, bottom, gk, conv_weight.reshape(taps, cin, channels), *got),
+        [((strip_rows * tile_q, cin), BF16), ((tile_k * key_rows, cin), BF16), ((8, 128), F32)],
+        (gq, near, far, gk, conv_weight.reshape(taps, cin, channels), *got),
         [(strip_rows + 2, up16(wide), channels), (tall, key_rows + 16, channels)],
     )
-    part = jnp.concatenate(ordered([part] + to_layers([part] * (n_ka - 1)), z), axis=0)
-    part = jnp.concatenate(ordered([part] + to_quad([part] * (n_quad - 1)), quad), axis=0)
-    whole = jnp.concatenate(ordered([part, to_core(part)], core), axis=0)
+    (part,) = call(
+        functools.partial(gather_kernel, n_quad, 0),
+        "gather",
+        [((half, channels), BF16)],
+        (part, *to_quad([part] * (n_quad - 1))),
+        [(n_quad, up16(quarter), channels)],
+        after=(end,),
+    )
+    weight_grad = widen(to_core(part), widen(part))
     return (
         q_out.reshape(query_image.shape),
         k_out.reshape(key_image.shape),
-        whole.astype(F32).reshape(conv_weight.shape),
+        weight_grad.reshape(conv_weight.shape),
     )
 
 

time: 68.2 us -> 65.2 us (0.956)
  waiting for transfers between devices: 27.2 us -> 24.5 us
  Pallas kernels: 7.93 us -> 10.3 us
  other arithmetic: 2.25 us -> 0 us
  local copies, waits for them, and re-layouts: 1 us -> 0.01 us
    ppermute x9, waiting for transfers between devices: 12.8 us -> 9.03 us  [to_quad(): lax.ppermute(x, 'pb', flip(n_pb, 2 * s))]
    pallas_call x0 -> x2, Pallas kernels: none -> 2.12 us  [widen(): pl.pallas_call(functools.partial(widen_kernel, whole is not None), in_spe...]
    ppermute x3, starting transfers between devices: 0.66 us -> 2.47 us  [to_core(): return lax.ppermute(x, 'pb', flip(n_pb, 1))]
    convert_element_type x2 -> x0, other arithmetic: 1.66 us -> none  [the longest x1 1.63 us: body(): whole.astype(F32).reshape(conv_weight.shape)]
    ppermute x9, starting transfers between devices: 16.1 us -> 14.9 us  [to_layers(): lax.ppermute(x, 'ka', flip(n_ka, s))]
    unnamed x6, local copies, waits for them, and re-layouts: 1 us -> 0.01 us
    ppermute x9, starting transfers between devices: 12 us -> 11.2 us  [to_quad(): lax.ppermute(x, 'pb', flip(n_pb, 2 * s))]
    pallas_call x5 -> x8, Pallas kernels: 3.13 us -> 3.39 us  [call(): pl.pallas_call(kernel, in_specs=[pl.BlockSpec(memory_space=pltpu.VMEM)] *...]
  transfers between devices with their start and end apart: 21 -> 22, of which waited for: 10 -> 12; matrix products, arithmetic and copies ran while one was open for 0% -> 0% of each run, Pallas kernels for 2% -> 4%
where the time goes in v3:
time: 65.2 us; the launch traced here: 64.7 us
  starting transfers between devices  29.2 us (45%)
  waiting for transfers between devices  24.5 us (38%)
  Pallas kernels  10.3 us (16%)
  between operations  0.78 us (1%)
    ppermute x9, starting transfers between devices, to_layers(): lax.ppermute(x, 'ka', flip(n_ka, s))  14.9 us
    ppermute x9, waiting for transfers between devices, to_layers(): lax.ppermute(x, 'ka', flip(n_ka, s))  12.8 us
    ppermute x9, starting transfers between devices, to_quad(): lax.ppermute(x, 'pb', flip(n_pb, 2 * s))  11.2 us
    ppermute x9, waiting for transfers between devices, to_quad(): lax.ppermute(x, 'pb', flip(n_pb, 2 * s))  9.03 us
    pallas_call x1, Pallas kernels, correlate(): pl.pallas_call(functools.partial(corr_kernel, dims), in_specs=[hbm] * 5,...  4.8 us
    pallas_call x8, Pallas kernels, call(): pl.pallas_call(kernel, in_specs=[pl.BlockSpec(memory_space=pltpu.VMEM)] *...  3.39 us
    ppermute x3, waiting for transfers between devices, to_core(): return lax.ppermute(x, 'pb', flip(n_pb, 1))  2.6 us
    ppermute x3, starting transfers between devices, to_core(): return lax.ppermute(x, 'pb', flip(n_pb, 1))  2.47 us
  transfers between devices with their start and end apart: 22, of which 12 were waited for; matrix products, arithmetic and copies ran while one was open for 0% of the time, Pallas kernels for 4%

profile of v3, /device:TPU:0, one launch (start us, length us, event | category | flops | bytes accessed | tf_op | source)
XLA Modules:
  0.0 64.7 jit_solution(7584533466241751585)
XLA Ops:
  0.7 4.8 %correlate.1 = (bf16[200,256]{1,0:T(8,128)(2,1)S(1)}, bf16[224,256]{1,0:T(8,128)(2,1)S(1)}, bf16[200,256]{1,0:T(8,128)(2,1)S(1)}, bf16[224,256]{1,0:T(8,128)(2,1...) custom-call(bf16[2040,768]{1,0:T(8,128)(2,1)} %bitcast.11, bf16[768,256]{1,0:T(8,128)(2,1)} %bitcast.13, ...), custom_call_target="tpu_custom_call" | custom-call | tf_op jit(solution)/shard_map/correlate/pallas_call | solution.py:155
  6.0 3.7 %collective-permute-start.1 = (bf16[200,256]{1,0:T(8,128)(2,1)S(1)}, bf16[200,256]{1,0:T(8,128)(2,1)S(1)}, u32[]{:S(2)}, u32[]{:S(2)}) collective-permute-start(bf16[200,256]{1,0:T(8,128)(2,1)S(1)} %get-tuple-element.37), channel_id=1, source_target_pairs={{0,2},{1,3},{2,0},{3,1},{4,6},{5,7},{6,4},{7,5},{8,10},{9,11},{10,... | collective-permute-start | bytes 307208 | tf_op jit(solution)/shard_map/ppermute | solution.py:426
  9.7 1.6 %collective-permute-start.4 = (bf16[256,256]{1,0:T(8,128)(2,1)S(1)}, bf16[256,256]{1,0:T(8,128)(2,1)S(1)}, u32[]{:S(2)}, u32[]{:S(2)}) collective-permute-start(bf16[256,256]{1,0:T(8,128)(2,1)S(1)} %get-tuple-element.42), channel_id=1, source_target_pairs={{0,8},{4,12},{8,0},{12,4},{16,24},{20,28},{24,16},{28,20},{1,9},{5... | collective-permute-start | bytes 393224 | tf_op jit(solution)/shard_map/ppermute | solution.py:419
  11.3 1.5 %collective-permute-start.6 = (bf16[256,256]{1,0:T(8,128)(2,1)S(1)}, bf16[256,256]{1,0:T(8,128)(2,1)S(1)}, u32[]{:S(2)}, u32[]{:S(2)}) collective-permute-start(bf16[256,256]{1,0:T(8,128)(2,1)S(1)} %get-tuple-element.44), channel_id=1, source_target_pairs={{0,24},{4,28},{8,16},{12,20},{16,8},{20,12},{24,0},{28,4},{1,25},{... | collective-permute-start | bytes 393224 | tf_op jit(solution)/shard_map/ppermute | solution.py:419
  12.8 1.6 %collective-permute-start = (bf16[224,256]{1,0:T(8,128)(2,1)S(1)}, bf16[224,256]{1,0:T(8,128)(2,1)S(1)}, u32[]{:S(2)}, u32[]{:S(2)}) collective-permute-start(bf16[224,256]{1,0:T(8,128)(2,1)S(1)} %get-tuple-element.36), channel_id=1, source_target_pairs={{0,1},{1,0},{2,3},{3,2},{4,5},{5,4},{6,7},{7,6},{8,9},{9,8},{10,11... | collective-permute-start | bytes 344072 | tf_op jit(solution)/shard_map/ppermute | solution.py:426
  14.4 1.6 %collective-permute-start.2 = (bf16[224,256]{1,0:T(8,128)(2,1)S(1)}, bf16[224,256]{1,0:T(8,128)(2,1)S(1)}, u32[]{:S(2)}, u32[]{:S(2)}) collective-permute-start(bf16[224,256]{1,0:T(8,128)(2,1)S(1)} %get-tuple-element.38), channel_id=1, source_target_pairs={{0,3},{1,2},{2,1},{3,0},{4,7},{5,6},{6,5},{7,4},{8,11},{9,10},{10,... | collective-permute-start | bytes 344072 | tf_op jit(solution)/shard_map/ppermute | solution.py:426
  17.9 3.4 %collective-permute-done.2.refs_3_ = bf16[224,256]{1,0:T(8,128)(2,1)S(1)} collective-permute-done((bf16[224,256]{1,0:T(8,128)(2,1)S(1)}, bf16[224,256]{1,0:T(8,128)(2,1)S(1)}, u32[]{:S(2)}, u32[]{:S(2)}) %collective-permute-start.2) | collective-permute-done | bytes 114720 | tf_op jit(solution)/shard_map/ppermute | solution.py:426
  21.4 1.3 %weights.1 = (bf16[1202,256]{1,0:T(8,128)(2,1)S(1)}, f32[1152,256]{1,0:T(8,128)S(1)}, bf16[200,256]{1,0:T(8,128)(2,1)S(1)}, bf16[208,256]{1,0:T(8,128)(2,1)S(1)}) custom-call(bf16[200,256]{1,0:T(8,128)(2,1)S(1)} %get-tuple-element.35.refs_0_, bf16[224,256]{1,0:T(8,128)(2,1)S(1)} %collective-permute-done.refs_1_, ...), custom_call_target="tpu_custom_call" | custom-call | tf_op jit(solution)/shard_map/weights/pallas_call | solution.py:387
  22.9 2.0 %collective-permute-done.7.recv_ref = bf16[1202,256]{1,0:T(8,128)(2,1)S(1)} collective-permute-done((bf16[1202,256]{1,0:T(8,128)(2,1)S(1)}, bf16[1202,256]{1,0:T(8,128)(2,1)S(1)}, u32[]{:S(2)}, u32[]{:S(2)}) %collective-permute-start.7) | collective-permute-done | bytes 615456 | tf_op jit(solution)/shard_map/ppermute | solution.py:416
  25.1 1.6 %collective-permute-start.8 = (bf16[288,256]{1,0:T(8,128)(2,1)S(1)}, bf16[288,256]{1,0:T(8,128)(2,1)S(1)}, u32[]{:S(2)}, u32[]{:S(2)}) collective-permute-start(bf16[288,256]{1,0:T(8,128)(2,1)S(1)} %get-tuple-element.51), channel_id=1, source_target_pairs={{0,8},{4,12},{8,0},{12,4},{16,24},{20,28},{24,16},{28,20},{1,9},{5... | collective-permute-start | bytes 442376 | tf_op jit(solution)/shard_map/ppermute | solution.py:419
  27.2 1.5 %collective-permute-start.10 = (bf16[288,256]{1,0:T(8,128)(2,1)S(1)}, bf16[288,256]{1,0:T(8,128)(2,1)S(1)}, u32[]{:S(2)}, u32[]{:S(2)}) collective-permute-start(bf16[288,256]{1,0:T(8,128)(2,1)S(1)} %get-tuple-element.53), channel_id=1, source_target_pairs={{0,24},{4,28},{8,16},{12,20},{16,8},{20,12},{24,0},{28,4},{1,25},{... | collective-permute-start | bytes 442376 | tf_op jit(solution)/shard_map/ppermute | solution.py:419
  28.7 3.1 %collective-permute-done.8.refs_1_ = bf16[288,256]{1,0:T(8,128)(2,1)S(1)} collective-permute-done((bf16[288,256]{1,0:T(8,128)(2,1)S(1)}, bf16[288,256]{1,0:T(8,128)(2,1)S(1)}, u32[]{:S(2)}, u32[]{:S(2)}) %collective-permute-start.8) | collective-permute-done | bytes 147488 | tf_op jit(solution)/shard_map/ppermute | solution.py:419
  31.8 3.7 %collective-permute-done.9.refs_2_ = bf16[288,256]{1,0:T(8,128)(2,1)S(1)} collective-permute-done((bf16[288,256]{1,0:T(8,128)(2,1)S(1)}, bf16[288,256]{1,0:T(8,128)(2,1)S(1)}, u32[]{:S(2)}, u32[]{:S(2)}) %collective-permute-start.9) | collective-permute-done | bytes 147488 | tf_op jit(solution)/shard_map/ppermute | solution.py:419
  35.5 1.6 %collective-permute-start.12 = (bf16[72,256]{1,0:T(8,128)(2,1)S(1)}, bf16[72,256]{1,0:T(8,128)(2,1)S(1)}, u32[]{:S(2)}, u32[]{:S(2)}) collective-permute-start(bf16[72,256]{1,0:T(8,128)(2,1)S(1)} %get-tuple-element.57), channel_id=1, source_target_pairs={{0,1},{1,0},{2,3},{3,2},{4,5},{5,4},{6,7},{7,6},{8,9},{9,8},{10,11... | collective-permute-start | bytes 110600 | tf_op jit(solution)/shard_map/ppermute | solution.py:426
  37.2 1.7 %collective-permute-start.13 = (bf16[72,256]{1,0:T(8,128)(2,1)S(1)}, bf16[72,256]{1,0:T(8,128)(2,1)S(1)}, u32[]{:S(2)}, u32[]{:S(2)}) collective-permute-start(bf16[72,256]{1,0:T(8,128)(2,1)S(1)} %get-tuple-element.58), channel_id=1, source_target_pairs={{0,2},{1,3},{2,0},{3,1},{4,6},{5,7},{6,4},{7,5},{8,10},{9,11},{10,... | collective-permute-start | bytes 110600 | tf_op jit(solution)/shard_map/ppermute | solution.py:426
  40.0 2.7 %collective-permute-done.13.refs_2_ = bf16[72,256]{1,0:T(8,128)(2,1)S(1)} collective-permute-done((bf16[72,256]{1,0:T(8,128)(2,1)S(1)}, bf16[72,256]{1,0:T(8,128)(2,1)S(1)}, u32[]{:S(2)}, u32[]{:S(2)}) %collective-permute-start.13) | collective-permute-done | bytes 36896 | tf_op jit(solution)/shard_map/ppermute | solution.py:426
  42.7 2.3 %collective-permute-done.14.refs_3_ = bf16[72,256]{1,0:T(8,128)(2,1)S(1)} collective-permute-done((bf16[72,256]{1,0:T(8,128)(2,1)S(1)}, bf16[72,256]{1,0:T(8,128)(2,1)S(1)}, u32[]{:S(2)}, u32[]{:S(2)}) %collective-permute-start.14) | collective-permute-done | bytes 36896 | tf_op jit(solution)/shard_map/ppermute | solution.py:426
  46.0 2.7 %collective-permute-start.16 = (bf16[72,256]{1,0:T(8,128)(2,1)S(1)}, bf16[72,256]{1,0:T(8,128)(2,1)S(1)}, u32[]{:S(2)}, u32[]{:S(2)}) collective-permute-start(bf16[72,256]{1,0:T(8,128)(2,1)S(1)} %get-tuple-element.61), channel_id=1, source_target_pairs={{0,2},{1,3},{2,0},{3,1},{4,6},{5,7},{6,4},{7,5},{8,10},{9,11},{10,... | collective-permute-start | bytes 110600 | tf_op jit(solution)/shard_map/ppermute | solution.py:426
  48.8 3.5 %collective-permute-done.16.rest_1_.refs_2_ = bf16[72,256]{1,0:T(8,128)(2,1)S(1)} collective-permute-done((bf16[72,256]{1,0:T(8,128)(2,1)S(1)}, bf16[72,256]{1,0:T(8,128)(2,1)S(1)}, u32[]{:S(2)}, u32[]{:S(2)}) %collective-permute-start.16) | collective-permute-done | bytes 36896 | tf_op jit(solution)/shard_map/ppermute | solution.py:426
  52.3 1.4 %collective-permute-start.20 = (bf16[288,256]{1,0:T(8,128)(2,1)S(1)}, bf16[288,256]{1,0:T(8,128)(2,1)S(1)}, u32[]{:S(2)}, u32[]{:S(2)}) collective-permute-start(bf16[288,256]{1,0:T(8,128)(2,1)S(1)} %gather.2.refs_0_), channel_id=1, source_target_pairs={{0,24},{4,28},{8,16},{12,20},{16,8},{20,12},{24,0},{28,4},{1,25},{... | collective-permute-start | bytes 442376 | tf_op jit(solution)/shard_map/ppermute | solution.py:419
  53.7 1.1 %collective-permute-start.19 = (bf16[288,256]{1,0:T(8,128)(2,1)S(1)}, bf16[288,256]{1,0:T(8,128)(2,1)S(1)}, u32[]{:S(2)}, u32[]{:S(2)}) collective-permute-start(bf16[288,256]{1,0:T(8,128)(2,1)S(1)} %gather.2.refs_0_), channel_id=1, source_target_pairs={{0,16},{4,20},{8,24},{12,28},{16,0},{20,4},{24,8},{28,12},{1,17},{... | collective-permute-start | bytes 442376 | tf_op jit(solution)/shard_map/ppermute | solution.py:419
  56.5 1.3 %images.1 = (bf16[192,256]{1,0:T(8,128)(2,1)}, bf16[192,256]{1,0:T(8,128)(2,1)}, f32[8,128]{1,0:T(8,128)S(1)}) custom-call(bf16[200,256]{1,0:T(8,128)(2,1)S(1)} %get-tuple-element.46.refs_4_.gq_ref, bf16[50,256]{1,0:T(8,128)(2,1)S(1)} %get-tuple-element.49.near_ref, bf16[50,256]{1,0:T(8,128)(2,1)S(1)} %collective-permute-done.11.far_ref, ...), custom_call_target="tpu_custom_call" | custom-call | tf_op jit(solution)/shard_map/images/pallas_call | solution.py:387
  58.5 1.5 %collective-permute-done.19.refs_2_ = bf16[288,256]{1,0:T(8,128)(2,1)S(1)} collective-permute-done((bf16[288,256]{1,0:T(8,128)(2,1)S(1)}, bf16[288,256]{1,0:T(8,128)(2,1)S(1)}, u32[]{:S(2)}, u32[]{:S(2)}) %collective-permute-start.19) | collective-permute-done | bytes 147488 | tf_op jit(solution)/shard_map/ppermute | solution.py:419
  60.1 1.9 %collective-permute-start.21 = (bf16[1152,256]{1,0:T(8,128)(2,1)S(1)}, bf16[1152,256]{1,0:T(8,128)(2,1)S(1)}, u32[]{:S(2)}, u32[]{:S(2)}) collective-permute-start(bf16[1152,256]{1,0:T(8,128)(2,1)S(1)} %gather.3.refs_0_), channel_id=1, source_target_pairs={{0,4},{4,0},{8,12},{12,8},{16,20},{20,16},{24,28},{28,24},{1,5},{5... | collective-permute-start | bytes 1769480 | tf_op jit(solution)/shard_map/ppermute | solution.py:416
  (37 shorter events, 10.7 us)
Async XLA Ops:
  0.6 20.8 %copy-start.1 = (bf16[4,48,256]{2,1,0:T(8,128)(2,1)S(1)}, bf16[4,48,256]{2,1,0:T(8,128)(2,1)}, u32[]{:S(2)}) copy-start(bf16[4,48,256]{2,1,0:T(8,128)(2,1)} %refs_9_.1) | copy-start | bytes 294916
  5.5 4.2 %collective-permute-start.3 = (bf16[928,256]{1,0:T(8,128)(2,1)S(1)}, bf16[928,256]{1,0:T(8,128)(2,1)S(1)}, u32[]{:S(2)}, u32[]{:S(2)}) collective-permute-start(bf16[928,256]{1,0:T(8,128)(2,1)S(1)} %get-tuple-element.40), channel_id=1, source_target_pairs={{0,4},{4,0},{8,12},{12,8},{16,20},{20,16},{24,28},{28,24},{1,5},{5... | collective-permute-start | bytes 1425416 | tf_op jit(solution)/shard_map/ppermute | solution.py:416
  6.0 10.0 %collective-permute-start.1 = (bf16[200,256]{1,0:T(8,128)(2,1)S(1)}, bf16[200,256]{1,0:T(8,128)(2,1)S(1)}, u32[]{:S(2)}, u32[]{:S(2)}) collective-permute-start(bf16[200,256]{1,0:T(8,128)(2,1)S(1)} %get-tuple-element.37), channel_id=1, source_target_pairs={{0,2},{1,3},{2,0},{3,1},{4,6},{5,7},{6,4},{7,5},{8,10},{9,11},{10,... | collective-permute-start | bytes 307208 | tf_op jit(solution)/shard_map/ppermute | solution.py:426
  9.7 46.8 %copy-start = (bf16[3,3,256,256]{3,2,1,0:T(8,128)(2,1)S(1)}, bf16[3,3,256,256]{3,2,1,0:T(8,128)(2,1)}, u32[]{:S(2)}) copy-start(bf16[3,3,256,256]{3,2,1,0:T(8,128)(2,1)} %param.11) | copy-start | bytes 3538948
  9.7 11.7 %collective-permute-start.4 = (bf16[256,256]{1,0:T(8,128)(2,1)S(1)}, bf16[256,256]{1,0:T(8,128)(2,1)S(1)}, u32[]{:S(2)}, u32[]{:S(2)}) collective-permute-start(bf16[256,256]{1,0:T(8,128)(2,1)S(1)} %get-tuple-element.42), channel_id=1, source_target_pairs={{0,8},{4,12},{8,0},{12,4},{16,24},{20,28},{24,16},{28,20},{1,9},{5... | collective-permute-start | bytes 393224 | tf_op jit(solution)/shard_map/ppermute | solution.py:419
  11.3 10.1 %collective-permute-start.6 = (bf16[256,256]{1,0:T(8,128)(2,1)S(1)}, bf16[256,256]{1,0:T(8,128)(2,1)S(1)}, u32[]{:S(2)}, u32[]{:S(2)}) collective-permute-start(bf16[256,256]{1,0:T(8,128)(2,1)S(1)} %get-tuple-element.44), channel_id=1, source_target_pairs={{0,24},{4,28},{8,16},{12,20},{16,8},{20,12},{24,0},{28,4},{1,25},{... | collective-permute-start | bytes 393224 | tf_op jit(solution)/shard_map/ppermute | solution.py:419
  12.8 5.1 %collective-permute-start = (bf16[224,256]{1,0:T(8,128)(2,1)S(1)}, bf16[224,256]{1,0:T(8,128)(2,1)S(1)}, u32[]{:S(2)}, u32[]{:S(2)}) collective-permute-start(bf16[224,256]{1,0:T(8,128)(2,1)S(1)} %get-tuple-element.36), channel_id=1, source_target_pairs={{0,1},{1,0},{2,3},{3,2},{4,5},{5,4},{6,7},{7,6},{8,9},{9,8},{10,11... | collective-permute-start | bytes 344072 | tf_op jit(solution)/shard_map/ppermute | solution.py:426
  14.4 6.9 %collective-permute-start.2 = (bf16[224,256]{1,0:T(8,128)(2,1)S(1)}, bf16[224,256]{1,0:T(8,128)(2,1)S(1)}, u32[]{:S(2)}, u32[]{:S(2)}) collective-permute-start(bf16[224,256]{1,0:T(8,128)(2,1)S(1)} %get-tuple-element.38), channel_id=1, source_target_pairs={{0,3},{1,2},{2,1},{3,0},{4,7},{5,6},{6,5},{7,4},{8,11},{9,10},{10,... | collective-permute-start | bytes 344072 | tf_op jit(solution)/shard_map/ppermute | solution.py:426
  16.0 5.4 %collective-permute-start.5 = (bf16[208,256]{1,0:T(8,128)(2,1)S(1)}, bf16[208,256]{1,0:T(8,128)(2,1)S(1)}, u32[]{:S(2)}, u32[]{:S(2)}) collective-permute-start(bf16[208,256]{1,0:T(8,128)(2,1)S(1)} %get-tuple-element.43), channel_id=1, source_target_pairs={{0,16},{4,20},{8,24},{12,28},{16,0},{20,4},{24,8},{28,12},{1,17},{... | collective-permute-start | bytes 319496 | tf_op jit(solution)/shard_map/ppermute | solution.py:419
  22.8 2.1 %collective-permute-start.7 = (bf16[1202,256]{1,0:T(8,128)(2,1)S(1)}, bf16[1202,256]{1,0:T(8,128)(2,1)S(1)}, u32[]{:S(2)}, u32[]{:S(2)}) collective-permute-start(bf16[1202,256]{1,0:T(8,128)(2,1)S(1)} %get-tuple-element.48), channel_id=1, source_target_pairs={{0,4},{4,0},{8,12},{12,8},{16,20},{20,16},{24,28},{28,24},{1,5},{5... | collective-permute-start | bytes 1846280 | tf_op jit(solution)/shard_map/ppermute | solution.py:416
  25.1 6.7 %collective-permute-start.8 = (bf16[288,256]{1,0:T(8,128)(2,1)S(1)}, bf16[288,256]{1,0:T(8,128)(2,1)S(1)}, u32[]{:S(2)}, u32[]{:S(2)}) collective-permute-start(bf16[288,256]{1,0:T(8,128)(2,1)S(1)} %get-tuple-element.51), channel_id=1, source_target_pairs={{0,8},{4,12},{8,0},{12,4},{16,24},{20,28},{24,16},{28,20},{1,9},{5... | collective-permute-start | bytes 442376 | tf_op jit(solution)/shard_map/ppermute | solution.py:419
  26.7 8.8 %collective-permute-start.9 = (bf16[288,256]{1,0:T(8,128)(2,1)S(1)}, bf16[288,256]{1,0:T(8,128)(2,1)S(1)}, u32[]{:S(2)}, u32[]{:S(2)}) collective-permute-start(bf16[288,256]{1,0:T(8,128)(2,1)S(1)} %get-tuple-element.52), channel_id=1, source_target_pairs={{0,16},{4,20},{8,24},{12,28},{16,0},{20,4},{24,8},{28,12},{1,17},{... | collective-permute-start | bytes 442376 | tf_op jit(solution)/shard_map/ppermute | solution.py:419
  27.2 8.3 %collective-permute-start.10 = (bf16[288,256]{1,0:T(8,128)(2,1)S(1)}, bf16[288,256]{1,0:T(8,128)(2,1)S(1)}, u32[]{:S(2)}, u32[]{:S(2)}) collective-permute-start(bf16[288,256]{1,0:T(8,128)(2,1)S(1)} %get-tuple-element.53), channel_id=1, source_target_pairs={{0,24},{4,28},{8,16},{12,20},{16,8},{20,12},{24,0},{28,4},{1,25},{... | collective-permute-start | bytes 442376 | tf_op jit(solution)/shard_map/ppermute | solution.py:419
  35.5 4.5 %collective-permute-start.12 = (bf16[72,256]{1,0:T(8,128)(2,1)S(1)}, bf16[72,256]{1,0:T(8,128)(2,1)S(1)}, u32[]{:S(2)}, u32[]{:S(2)}) collective-permute-start(bf16[72,256]{1,0:T(8,128)(2,1)S(1)} %get-tuple-element.57), channel_id=1, source_target_pairs={{0,1},{1,0},{2,3},{3,2},{4,5},{5,4},{6,7},{7,6},{8,9},{9,8},{10,11... | collective-permute-start | bytes 110600 | tf_op jit(solution)/shard_map/ppermute | solution.py:426
  37.2 5.5 %collective-permute-start.13 = (bf16[72,256]{1,0:T(8,128)(2,1)S(1)}, bf16[72,256]{1,0:T(8,128)(2,1)S(1)}, u32[]{:S(2)}, u32[]{:S(2)}) collective-permute-start(bf16[72,256]{1,0:T(8,128)(2,1)S(1)} %get-tuple-element.58), channel_id=1, source_target_pairs={{0,2},{1,3},{2,0},{3,1},{4,6},{5,7},{6,4},{7,5},{8,10},{9,11},{10,... | collective-permute-start | bytes 110600 | tf_op jit(solution)/shard_map/ppermute | solution.py:426
  38.9 6.1 %collective-permute-start.14 = (bf16[72,256]{1,0:T(8,128)(2,1)S(1)}, bf16[72,256]{1,0:T(8,128)(2,1)S(1)}, u32[]{:S(2)}, u32[]{:S(2)}) collective-permute-start(bf16[72,256]{1,0:T(8,128)(2,1)S(1)} %get-tuple-element.59), channel_id=1, source_target_pairs={{0,3},{1,2},{2,1},{3,0},{4,7},{5,6},{6,5},{7,4},{8,11},{9,10},{10,... | collective-permute-start | bytes 110600 | tf_op jit(solution)/shard_map/ppermute | solution.py:426
  45.2 7.0 %collective-permute-start.15 = (bf16[98,256]{1,0:T(8,128)(2,1)S(1)}, bf16[98,256]{1,0:T(8,128)(2,1)S(1)}, u32[]{:S(2)}, u32[]{:S(2)}) collective-permute-start(bf16[98,256]{1,0:T(8,128)(2,1)S(1)} %get-tuple-element.60), channel_id=1, source_target_pairs={{0,1},{1,0},{2,3},{3,2},{4,5},{5,4},{6,7},{7,6},{8,9},{9,8},{10,11... | collective-permute-start | bytes 150536 | tf_op jit(solution)/shard_map/ppermute | solution.py:426
  45.3 7.0 %collective-permute-start.17 = (bf16[98,256]{1,0:T(8,128)(2,1)S(1)}, bf16[98,256]{1,0:T(8,128)(2,1)S(1)}, u32[]{:S(2)}, u32[]{:S(2)}) collective-permute-start(bf16[98,256]{1,0:T(8,128)(2,1)S(1)} %get-tuple-element.62), channel_id=1, source_target_pairs={{0,3},{1,2},{2,1},{3,0},{4,7},{5,6},{6,5},{7,4},{8,11},{9,10},{10,... | collective-permute-start | bytes 150536 | tf_op jit(solution)/shard_map/ppermute | solution.py:426
  46.0 6.2 %collective-permute-start.16 = (bf16[72,256]{1,0:T(8,128)(2,1)S(1)}, bf16[72,256]{1,0:T(8,128)(2,1)S(1)}, u32[]{:S(2)}, u32[]{:S(2)}) collective-permute-start(bf16[72,256]{1,0:T(8,128)(2,1)S(1)} %get-tuple-element.61), channel_id=1, source_target_pairs={{0,2},{1,3},{2,0},{3,1},{4,6},{5,7},{6,4},{7,5},{8,10},{9,11},{10,... | collective-permute-start | bytes 110600 | tf_op jit(solution)/shard_map/ppermute | solution.py:426
  52.3 6.2 %collective-permute-start.20 = (bf16[288,256]{1,0:T(8,128)(2,1)S(1)}, bf16[288,256]{1,0:T(8,128)(2,1)S(1)}, u32[]{:S(2)}, u32[]{:S(2)}) collective-permute-start(bf16[288,256]{1,0:T(8,128)(2,1)S(1)} %gather.2.refs_0_), channel_id=1, source_target_pairs={{0,24},{4,28},{8,16},{12,20},{16,8},{20,12},{24,0},{28,4},{1,25},{... | collective-permute-start | bytes 442376 | tf_op jit(solution)/shard_map/ppermute | solution.py:419
  53.7 6.2 %collective-permute-start.19 = (bf16[288,256]{1,0:T(8,128)(2,1)S(1)}, bf16[288,256]{1,0:T(8,128)(2,1)S(1)}, u32[]{:S(2)}, u32[]{:S(2)}) collective-permute-start(bf16[288,256]{1,0:T(8,128)(2,1)S(1)} %gather.2.refs_0_), channel_id=1, source_target_pairs={{0,16},{4,20},{8,24},{12,28},{16,0},{20,4},{24,8},{28,12},{1,17},{... | collective-permute-start | bytes 442376 | tf_op jit(solution)/shard_map/ppermute | solution.py:419
  54.8 5.1 %collective-permute-start.18 = (bf16[288,256]{1,0:T(8,128)(2,1)S(1)}, bf16[288,256]{1,0:T(8,128)(2,1)S(1)}, u32[]{:S(2)}, u32[]{:S(2)}) collective-permute-start(bf16[288,256]{1,0:T(8,128)(2,1)S(1)} %gather.2.refs_0_), channel_id=1, source_target_pairs={{0,8},{4,12},{8,0},{12,4},{16,24},{20,28},{24,16},{28,20},{1,9},{5... | collective-permute-start | bytes 442376 | tf_op jit(solution)/shard_map/ppermute | solution.py:419
  55.8 0.7 %collective-permute-start.11 = (bf16[50,256]{1,0:T(8,128)(2,1)S(1)}, bf16[50,256]{1,0:T(8,128)(2,1)S(1)}, u32[]{:S(2)}, u32[]{:S(2)}) collective-permute-start(bf16[50,256]{1,0:T(8,128)(2,1)S(1)} %get-tuple-element.54), channel_id=1, source_target_pairs={{4,8},{12,16},{20,24},{8,4},{16,12},{24,20},{5,9},{13,17},{21,25},... | collective-permute-start | bytes 76808 | tf_op jit(solution)/shard_map/ppermute | solution.py:423
  60.1 3.5 %collective-permute-start.21 = (bf16[1152,256]{1,0:T(8,128)(2,1)S(1)}, bf16[1152,256]{1,0:T(8,128)(2,1)S(1)}, u32[]{:S(2)}, u32[]{:S(2)}) collective-permute-start(bf16[1152,256]{1,0:T(8,128)(2,1)S(1)} %gather.3.refs_0_), channel_id=1, source_target_pairs={{0,4},{4,0},{8,12},{12,8},{16,20},{20,16},{24,28},{28,24},{1,5},{5... | collective-permute-start | bytes 1769480 | tf_op jit(solution)/shard_map/ppermute | solution.py:416
  (1 other events, 20.8 us)

commit v4 on v3

--- a/solution.py
+++ b/solution.py
@@ -251,27 +251,30 @@
     half = keep_ref.shape[0]
     keep_ref[...] = acc_ref[pl.ds(pl.multiple_of(core * half, 16), half), :]
     send_ref[0:half, :] = acc_ref[pl.ds(pl.multiple_of((1 - core) * half, 16), half), :].astype(BF16)
-    first, last = sum_ref[0:wide, :], sum_ref[(rows - 1) * wide : rows * wide, :]
-    send_ref[half : half + wide, :] = jnp.where(core == 0, last, first).astype(BF16)
-
-
-def piece_kernel(keep_ref, recv_ref, own_ref, near_ref, *rest):
+    send_ref[half : half + wide, :] = sum_ref[0:wide, :].astype(BF16)
+    send_ref[half + up16(wide) : half + up16(wide) + wide, :] = sum_ref[(rows - 1) * wide : rows * wide, :].astype(BF16)
+
+
+def piece_kernel(keep_ref, recv_ref, own_ref, near_ref, onward_ref, *rest):
     *sends, sum_ref = rest
     quad, core, _ = place()
     half = keep_ref.shape[0]
     size = own_ref.shape[0]
     tile = near_ref.shape[0]
-    near_ref[...] = recv_ref[half : half + tile, :]
+    first = recv_ref[half : half + tile, :].astype(F32)
+    last = recv_ref[half + up16(tile) : half + up16(tile) + tile, :].astype(F32)
+    near_ref[...] = jnp.where(core == 0, first, last).astype(BF16)
+    onward_ref[...] = jnp.where(core == 0, last, first).astype(BF16)
     sum_ref[...] = keep_ref[...] + recv_ref[0:half, :].astype(F32)
     own_ref[...] = sum_ref[pl.ds(pl.multiple_of(quad * size, 16), size), :]
     for s, send in enumerate(sends, 1):
         send[...] = sum_ref[pl.ds(pl.multiple_of((quad ^ s) * size, 16), size), :].astype(BF16)
 
 
-def layer_kernel(n_quad, rows, *refs):
+def layer_kernel(n_quad, *refs):
     own_ref, *got = refs[:n_quad]
-    gq_ref, out_ref, far_ref, *sends, stage_ref = refs[n_quad:]
-    _, core, z = place()
+    out_ref, *sends, stage_ref = refs[n_quad + 1 :]
+    _, _, z = place()
     n_ka = len(sends) + 1
     size = own_ref.shape[0]
     piece = size // n_ka
@@ -281,11 +284,8 @@
     for k in range(n_ka):
         stage_ref[z ^ k, 0:piece, :] = total[k * piece : (k + 1) * piece]
     out_ref[...] = stage_ref[0, 0:piece, :]
-    for s, send in enumerate(sends, 1):
+    for s, send in enumerate(reversed(sends), 1):
         send[...] = stage_ref[s, 0:piece, :].astype(BF16)
-    query = gq_ref[...].astype(F32)
-    wide = query.shape[0] // rows
-    far_ref[...] = jnp.where(core == 0, query[0:wide], query[(rows - 1) * wide :]).astype(BF16)
 
 
 def combine_kernel(n_ka, *refs):
@@ -301,10 +301,9 @@
     tall, key_rows, _ = ext_ref.shape
     ext_ref[...] = gk_ref[...].astype(F32).reshape(ext_ref.shape)
     first, last = ext_ref[:, 0, :], ext_ref[:, key_rows - 1, :]
-    for s, send in enumerate(sends, 1):
+    for s, send in enumerate(reversed(sends), 1):
         send[0:piece, :] = total
-        if joins(s):
-            send[piece : piece + tall, :] = jnp.where((z ^ s) == z + 1, last, first).astype(BF16)
+        send[piece : piece + tall, :] = jnp.where((z ^ s) == z + 1, last, first).astype(BF16)
 
 
 def image_kernel(piece, rows, gq_ref, near_ref, far_ref, gk_ref, w_ref, *rest):
@@ -316,7 +315,7 @@
     tile_k = tall - 2
     _, core, z = place()
     near, far = near_ref[...].astype(F32), far_ref[...].astype(F32)
-    lines = [(s, ref[piece : piece + tall, :].astype(F32)) for s, ref in enumerate(got, 1) if joins(s)]
+    lines = [(s, ref[piece : piece + tall, :].astype(F32)) for s, ref in enumerate(reversed(got), 1) if joins(s)]
     qext_ref[0, 0:wide, :] = jnp.where(core == 0, far, near)
     query = gq_ref[...].astype(F32)
     for row in range(rows):
@@ -340,11 +339,11 @@
 
 
 def gather_kernel(count, axis, *refs):
-    z = place()[axis]
+    own = place()[axis]
     *_, out_ref, stage_ref = refs
     piece = refs[0].shape[0]
-    for s in range(count):
-        stage_ref[z ^ s, 0:piece, :] = refs[s][0:piece, :].astype(F32)
+    for i in range(count):
+        stage_ref[own ^ ((count - i) % count), 0:piece, :] = refs[i][0:piece, :].astype(F32)
     for k in range(count):
         out_ref[k * piece : (k + 1) * piece, :] = stage_ref[k, 0:piece, :].astype(BF16)
 
@@ -418,12 +417,11 @@
     def to_quad(parts):
         return [lax.ppermute(x, "pb", flip(n_pb, 2 * s)) for s, x in enumerate(parts, 1)]
 
-    def to_chip(x):
-        links = [(i, i + 1) for i in range(1, n_pb - 1, 2)]
-        return lax.ppermute(x, "pb", links + [(d, s) for s, d in links])
-
     def to_layers(parts):
         return [lax.ppermute(x, "ka", flip(n_ka, s)) for s, x in enumerate(parts, 1)]
+
+    def to_far_layers(parts):
+        return [lax.ppermute(x, "ka", flip(n_ka, n_ka - i)) for i, x in enumerate(parts, 1)]
 
     def extra(count, mask, more):
         return count + (more if joins(mask) else 0)
@@ -447,7 +445,7 @@
     k_own, near, *k_pair = call(functools.partial(pair_kernel, size, tile_q), "pairs", outs, (k_keep, k_recv))
     k_more = to_quad(k_pair)
     outs = [
-        ((half + wide, channels), BF16),
+        ((half + 2 * up16(wide), channels), BF16),
         ((half, channels), F32),
         ((strip_rows * wide, channels), BF16),
         ((size, channels), BF16),
@@ -461,27 +459,28 @@
     )
 
     w_recv = to_core(w_send)
-    outs = [((quarter, channels), F32), ((wide, channels), BF16)]
-    outs += [((quarter, channels), BF16)] * (n_quad - 1)
-    own, near, *sends = call(piece_kernel, "pieces", outs, (w_keep, w_recv), [(half, channels)])
+    outs = [((quarter, channels), F32)] + [((wide, channels), BF16)] * 2 + [((quarter, channels), BF16)] * (n_quad - 1)
+    own, near, far, *sends = call(piece_kernel, "pieces", outs, (w_keep, w_recv), [(half, channels)])
     got = to_quad(sends)
-    own, far, *sends = call(
-        functools.partial(layer_kernel, n_quad, strip_rows),
+    firsts = range(0, n_pb - 2, 2)
+    far = lax.ppermute(far, "pb", [(i, i + 2) for i in firsts] + [(i + 3, i + 1) for i in firsts])
+    own, *sends = call(
+        functools.partial(layer_kernel, n_quad),
         "layers",
-        [((piece, channels), F32), ((wide, channels), BF16)] + [((piece, channels), BF16)] * (n_ka - 1),
-        (own, *got, gq),
+        [((piece, channels), F32)] + [((piece, channels), BF16)] * (n_ka - 1),
+        (own, *got),
         [(n_ka, up16(piece), channels)],
-    )
-    got = to_layers(sends)
-    far = to_chip(far)
+        after=(far,),
+    )
+    got = to_far_layers(sends)
     part, *sends = call(
         functools.partial(combine_kernel, n_ka),
         "combine",
-        [((piece, channels), BF16)] + [((extra(piece, s, tall), channels), BF16) for s in range(1, n_ka)],
+        [((piece, channels), BF16)] + [((piece + tall, channels), BF16)] * (n_ka - 1),
         (own, *got, gk),
         [(tall, key_rows, channels)],
     )
-    got = to_layers(sends)
+    got = to_far_layers(sends)
     (part,) = call(
         functools.partial(gather_kernel, n_ka, 2),
         "gather",
@@ -500,7 +499,7 @@
         functools.partial(gather_kernel, n_quad, 0),
         "gather",
         [((half, channels), BF16)],
-        (part, *to_quad([part] * (n_quad - 1))),
+        (part, *reversed(to_quad([part] * (n_quad - 1)))),
         [(n_quad, up16(quarter), channels)],
         after=(end,),
     )

time: 65.2 us -> 62.5 us (0.959)
  waiting for transfers between devices: 24.5 us -> 20.2 us
  starting transfers between devices: 29.2 us -> 31 us
    ppermute x1 -> x7, starting transfers between devices: 0.65 us -> 12.3 us  [the longest x6 8.91 us: to_far_layers(): lax.ppermute(x, 'ka', flip(n_ka, n_ka - i))]
    ppermute x9 -> x3, waiting for transfers between devices: 12.8 us -> 4.28 us  [to_layers(): lax.ppermute(x, 'ka', flip(n_ka, s))]
    ppermute x9 -> x3, starting transfers between devices: 14.9 us -> 6.88 us  [to_layers(): lax.ppermute(x, 'ka', flip(n_ka, s))]
    ppermute x1 -> x7, waiting for transfers between devices: 0.01 us -> 7.79 us  [the longest x6 6.25 us: to_far_layers(): lax.ppermute(x, 'ka', flip(n_ka, n_ka - i))]
    ppermute x9, waiting for transfers between devices: 9.03 us -> 5.13 us  [to_quad(): lax.ppermute(x, 'pb', flip(n_pb, 2 * s))]
    ppermute x3, starting transfers between devices: 2.47 us -> 0.66 us  [to_core(): return lax.ppermute(x, 'pb', flip(n_pb, 1))]
  transfers between devices with their start and end apart: 22 -> 22, of which waited for: 12 -> 14; matrix products, arithmetic and copies ran while one was open for 0% -> 0% of each run, Pallas kernels for 4% -> 4%
where the time goes in v4:
time: 62.5 us; the launch traced here: 62.4 us
  starting transfers between devices  31 us (50%)
  waiting for transfers between devices  20.2 us (32%)
  Pallas kernels  10.4 us (17%)
  between operations  0.76 us (1%)
    ppermute x9, starting transfers between devices, to_quad(): lax.ppermute(x, 'pb', flip(n_pb, 2 * s))  11.2 us
    ppermute x6, starting transfers between devices, to_far_layers(): lax.ppermute(x, 'ka', flip(n_ka, n_ka - i))  8.91 us
    ppermute x3, starting transfers between devices, to_layers(): lax.ppermute(x, 'ka', flip(n_ka, s))  6.88 us
    ppermute x6, waiting for transfers between devices, to_far_layers(): lax.ppermute(x, 'ka', flip(n_ka, n_ka - i))  6.25 us
    ppermute x9, waiting for transfers between devices, to_quad(): lax.ppermute(x, 'pb', flip(n_pb, 2 * s))  5.13 us
    pallas_call x1, Pallas kernels, correlate(): pl.pallas_call(functools.partial(corr_kernel, dims), in_specs=[hbm] * 5,...  4.8 us
    ppermute x3, waiting for transfers between devices, to_layers(): lax.ppermute(x, 'ka', flip(n_ka, s))  4.28 us
    pallas_call x8, Pallas kernels, call(): pl.pallas_call(kernel, in_specs=[pl.BlockSpec(memory_space=pltpu.VMEM)] *...  3.45 us
  transfers between devices with their start and end apart: 22, of which 14 were waited for; matrix products, arithmetic and copies ran while one was open for 0% of the time, Pallas kernels for 4%

profile of v4, /device:TPU:0, one launch (start us, length us, event | category | flops | bytes accessed | tf_op | source)
XLA Modules:
  0.0 62.4 jit_solution(7299841098240676793)
XLA Ops:
  0.7 4.8 %correlate.1 = (bf16[200,256]{1,0:T(8,128)(2,1)S(1)}, bf16[224,256]{1,0:T(8,128)(2,1)S(1)}, bf16[200,256]{1,0:T(8,128)(2,1)S(1)}, bf16[224,256]{1,0:T(8,128)(2,1...) custom-call(bf16[2040,768]{1,0:T(8,128)(2,1)} %bitcast.11, bf16[768,256]{1,0:T(8,128)(2,1)} %bitcast.13, ...), custom_call_target="tpu_custom_call" | custom-call | tf_op jit(solution)/shard_map/correlate/pallas_call | solution.py:155
  6.0 3.7 %collective-permute-start.1 = (bf16[200,256]{1,0:T(8,128)(2,1)S(1)}, bf16[200,256]{1,0:T(8,128)(2,1)S(1)}, u32[]{:S(2)}, u32[]{:S(2)}) collective-permute-start(bf16[200,256]{1,0:T(8,128)(2,1)S(1)} %get-tuple-element.37), channel_id=1, source_target_pairs={{0,2},{1,3},{2,0},{3,1},{4,6},{5,7},{6,4},{7,5},{8,10},{9,11},{10,... | collective-permute-start | bytes 307208 | tf_op jit(solution)/shard_map/ppermute | solution.py:421
  9.7 1.6 %collective-permute-start.4 = (bf16[256,256]{1,0:T(8,128)(2,1)S(1)}, bf16[256,256]{1,0:T(8,128)(2,1)S(1)}, u32[]{:S(2)}, u32[]{:S(2)}) collective-permute-start(bf16[256,256]{1,0:T(8,128)(2,1)S(1)} %get-tuple-element.42), channel_id=1, source_target_pairs={{0,8},{4,12},{8,0},{12,4},{16,24},{20,28},{24,16},{28,20},{1,9},{5... | collective-permute-start | bytes 393224 | tf_op jit(solution)/shard_map/ppermute | solution.py:418
  11.3 1.5 %collective-permute-start.6 = (bf16[256,256]{1,0:T(8,128)(2,1)S(1)}, bf16[256,256]{1,0:T(8,128)(2,1)S(1)}, u32[]{:S(2)}, u32[]{:S(2)}) collective-permute-start(bf16[256,256]{1,0:T(8,128)(2,1)S(1)} %get-tuple-element.44), channel_id=1, source_target_pairs={{0,24},{4,28},{8,16},{12,20},{16,8},{20,12},{24,0},{28,4},{1,25},{... | collective-permute-start | bytes 393224 | tf_op jit(solution)/shard_map/ppermute | solution.py:418
  12.8 1.6 %collective-permute-start = (bf16[224,256]{1,0:T(8,128)(2,1)S(1)}, bf16[224,256]{1,0:T(8,128)(2,1)S(1)}, u32[]{:S(2)}, u32[]{:S(2)}) collective-permute-start(bf16[224,256]{1,0:T(8,128)(2,1)S(1)} %get-tuple-element.36), channel_id=1, source_target_pairs={{0,1},{1,0},{2,3},{3,2},{4,5},{5,4},{6,7},{7,6},{8,9},{9,8},{10,11... | collective-permute-start | bytes 344072 | tf_op jit(solution)/shard_map/ppermute | solution.py:421
  14.4 1.6 %collective-permute-start.2 = (bf16[224,256]{1,0:T(8,128)(2,1)S(1)}, bf16[224,256]{1,0:T(8,128)(2,1)S(1)}, u32[]{:S(2)}, u32[]{:S(2)}) collective-permute-start(bf16[224,256]{1,0:T(8,128)(2,1)S(1)} %get-tuple-element.38), channel_id=1, source_target_pairs={{0,3},{1,2},{2,1},{3,0},{4,7},{5,6},{6,5},{7,4},{8,11},{9,10},{10,... | collective-permute-start | bytes 344072 | tf_op jit(solution)/shard_map/ppermute | solution.py:421
  17.9 3.4 %collective-permute-done.2.refs_3_ = bf16[224,256]{1,0:T(8,128)(2,1)S(1)} collective-permute-done((bf16[224,256]{1,0:T(8,128)(2,1)S(1)}, bf16[224,256]{1,0:T(8,128)(2,1)S(1)}, u32[]{:S(2)}, u32[]{:S(2)}) %collective-permute-start.2) | collective-permute-done | bytes 114720 | tf_op jit(solution)/shard_map/ppermute | solution.py:421
  22.9 2.1 %collective-permute-done.7.recv_ref = bf16[1280,256]{1,0:T(8,128)(2,1)S(1)} collective-permute-done((bf16[1280,256]{1,0:T(8,128)(2,1)S(1)}, bf16[1280,256]{1,0:T(8,128)(2,1)S(1)}, u32[]{:S(2)}, u32[]{:S(2)}) %collective-permute-start.7) | collective-permute-done | bytes 655392 | tf_op jit(solution)/shard_map/ppermute | solution.py:415
  25.2 1.6 %collective-permute-start.9 = (bf16[288,256]{1,0:T(8,128)(2,1)S(1)}, bf16[288,256]{1,0:T(8,128)(2,1)S(1)}, u32[]{:S(2)}, u32[]{:S(2)}) collective-permute-start(bf16[288,256]{1,0:T(8,128)(2,1)S(1)} %get-tuple-element.53), channel_id=1, source_target_pairs={{0,8},{4,12},{8,0},{12,4},{16,24},{20,28},{24,16},{28,20},{1,9},{5... | collective-permute-start | bytes 442376 | tf_op jit(solution)/shard_map/ppermute | solution.py:418
  27.2 1.5 %collective-permute-start.11 = (bf16[288,256]{1,0:T(8,128)(2,1)S(1)}, bf16[288,256]{1,0:T(8,128)(2,1)S(1)}, u32[]{:S(2)}, u32[]{:S(2)}) collective-permute-start(bf16[288,256]{1,0:T(8,128)(2,1)S(1)} %get-tuple-element.55), channel_id=1, source_target_pairs={{0,24},{4,28},{8,16},{12,20},{16,8},{20,12},{24,0},{28,4},{1,25},{... | collective-permute-start | bytes 442376 | tf_op jit(solution)/shard_map/ppermute | solution.py:418
  28.7 3.4 %collective-permute-start.8 = (bf16[50,256]{1,0:T(8,128)(2,1)S(1)}, bf16[50,256]{1,0:T(8,128)(2,1)S(1)}, u32[]{:S(2)}, u32[]{:S(2)}) collective-permute-start(bf16[50,256]{1,0:T(8,128)(2,1)S(1)} %get-tuple-element.50), channel_id=1, source_target_pairs={{0,8},{8,16},{16,24},{12,4},{20,12},{28,20},{1,9},{9,17},{17,25},{... | collective-permute-start | bytes 76808 | tf_op jit(solution)/shard_map/ppermute | solution.py:466
  32.1 1.5 %collective-permute-done.8.refs_4_.far_ref = bf16[50,256]{1,0:T(8,128)(2,1)S(1)} collective-permute-done((bf16[50,256]{1,0:T(8,128)(2,1)S(1)}, bf16[50,256]{1,0:T(8,128)(2,1)S(1)}, u32[]{:S(2)}, u32[]{:S(2)}) %collective-permute-start.8) | collective-permute-done | bytes 25632 | tf_op jit(solution)/shard_map/ppermute | solution.py:466
  33.7 1.8 %collective-permute-done.10.refs_2_ = bf16[288,256]{1,0:T(8,128)(2,1)S(1)} collective-permute-done((bf16[288,256]{1,0:T(8,128)(2,1)S(1)}, bf16[288,256]{1,0:T(8,128)(2,1)S(1)}, u32[]{:S(2)}, u32[]{:S(2)}) %collective-permute-start.10) | collective-permute-done | bytes 147488 | tf_op jit(solution)/shard_map/ppermute | solution.py:418
  35.6 2.8 %collective-permute-start.12 = (bf16[72,256]{1,0:T(8,128)(2,1)S(1)}, bf16[72,256]{1,0:T(8,128)(2,1)S(1)}, u32[]{:S(2)}, u32[]{:S(2)}) collective-permute-start(bf16[72,256]{1,0:T(8,128)(2,1)S(1)} %get-tuple-element.57), channel_id=1, source_target_pairs={{0,3},{1,2},{2,1},{3,0},{4,7},{5,6},{6,5},{7,4},{8,11},{9,10},{10,... | collective-permute-start | bytes 110600 | tf_op jit(solution)/shard_map/ppermute | solution.py:424
  38.7 1.3 %collective-permute-start.14 = (bf16[72,256]{1,0:T(8,128)(2,1)S(1)}, bf16[72,256]{1,0:T(8,128)(2,1)S(1)}, u32[]{:S(2)}, u32[]{:S(2)}) collective-permute-start(bf16[72,256]{1,0:T(8,128)(2,1)S(1)} %get-tuple-element.59), channel_id=1, source_target_pairs={{0,1},{1,0},{2,3},{3,2},{4,5},{5,4},{6,7},{7,6},{8,9},{9,8},{10,11... | collective-permute-start | bytes 110600 | tf_op jit(solution)/shard_map/ppermute | solution.py:424
  40.1 1.4 %collective-permute-done.12.refs_1_ = bf16[72,256]{1,0:T(8,128)(2,1)S(1)} collective-permute-done((bf16[72,256]{1,0:T(8,128)(2,1)S(1)}, bf16[72,256]{1,0:T(8,128)(2,1)S(1)}, u32[]{:S(2)}, u32[]{:S(2)}) %collective-permute-start.12) | collective-permute-done | bytes 36896 | tf_op jit(solution)/shard_map/ppermute | solution.py:424
  41.5 1.8 %collective-permute-done.13.refs_2_ = bf16[72,256]{1,0:T(8,128)(2,1)S(1)} collective-permute-done((bf16[72,256]{1,0:T(8,128)(2,1)S(1)}, bf16[72,256]{1,0:T(8,128)(2,1)S(1)}, u32[]{:S(2)}, u32[]{:S(2)}) %collective-permute-start.13) | collective-permute-done | bytes 36896 | tf_op jit(solution)/shard_map/ppermute | solution.py:424
  43.4 1.9 %collective-permute-start.15 = (bf16[98,256]{1,0:T(8,128)(2,1)S(1)}, bf16[98,256]{1,0:T(8,128)(2,1)S(1)}, u32[]{:S(2)}, u32[]{:S(2)}) collective-permute-start(bf16[98,256]{1,0:T(8,128)(2,1)S(1)} %get-tuple-element.60), channel_id=1, source_target_pairs={{0,3},{1,2},{2,1},{3,0},{4,7},{5,6},{6,5},{7,4},{8,11},{9,10},{10,... | collective-permute-start | bytes 150536 | tf_op jit(solution)/shard_map/ppermute | solution.py:424
  45.7 2.2 %collective-permute-start.17 = (bf16[98,256]{1,0:T(8,128)(2,1)S(1)}, bf16[98,256]{1,0:T(8,128)(2,1)S(1)}, u32[]{:S(2)}, u32[]{:S(2)}) collective-permute-start(bf16[98,256]{1,0:T(8,128)(2,1)S(1)} %get-tuple-element.62), channel_id=1, source_target_pairs={{0,1},{1,0},{2,3},{3,2},{4,5},{5,4},{6,7},{7,6},{8,9},{9,8},{10,11... | collective-permute-start | bytes 150536 | tf_op jit(solution)/shard_map/ppermute | solution.py:424
  47.9 1.5 %collective-permute-done.15.rest_0_.refs_1_ = bf16[98,256]{1,0:T(8,128)(2,1)S(1)} collective-permute-done((bf16[98,256]{1,0:T(8,128)(2,1)S(1)}, bf16[98,256]{1,0:T(8,128)(2,1)S(1)}, u32[]{:S(2)}, u32[]{:S(2)}) %collective-permute-start.15) | collective-permute-done | bytes 50208 | tf_op jit(solution)/shard_map/ppermute | solution.py:424
  49.4 1.5 %collective-permute-done.16.rest_1_.refs_2_ = bf16[98,256]{1,0:T(8,128)(2,1)S(1)} collective-permute-done((bf16[98,256]{1,0:T(8,128)(2,1)S(1)}, bf16[98,256]{1,0:T(8,128)(2,1)S(1)}, u32[]{:S(2)}, u32[]{:S(2)}) %collective-permute-start.16) | collective-permute-done | bytes 50208 | tf_op jit(solution)/shard_map/ppermute | solution.py:424
  53.0 1.5 %collective-permute-start.18 = (bf16[288,256]{1,0:T(8,128)(2,1)S(1)}, bf16[288,256]{1,0:T(8,128)(2,1)S(1)}, u32[]{:S(2)}, u32[]{:S(2)}) collective-permute-start(bf16[288,256]{1,0:T(8,128)(2,1)S(1)} %gather.2.refs_0_), channel_id=1, source_target_pairs={{0,24},{4,28},{8,16},{12,20},{16,8},{20,12},{24,0},{28,4},{1,25},{... | collective-permute-start | bytes 442376 | tf_op jit(solution)/shard_map/ppermute | solution.py:418
  54.6 1.4 %images.1 = (bf16[192,256]{1,0:T(8,128)(2,1)}, bf16[192,256]{1,0:T(8,128)(2,1)}, f32[8,128]{1,0:T(8,128)S(1)}) custom-call(bf16[200,256]{1,0:T(8,128)(2,1)S(1)} %get-tuple-element.46.gq_ref, bf16[50,256]{1,0:T(8,128)(2,1)S(1)} %get-tuple-element.49.near_ref, bf16[50,256]{1,0:T(8,128)(2,1)S(1)} %collective-permute-done.8.refs_4_.far_ref, ...), custom_call_target="tpu_custom_call" | custom-call | tf_op jit(solution)/shard_map/images/pallas_call | solution.py:386
  57.3 1.8 %collective-permute-done.18.refs_1_ = bf16[288,256]{1,0:T(8,128)(2,1)S(1)} collective-permute-done((bf16[288,256]{1,0:T(8,128)(2,1)S(1)}, bf16[288,256]{1,0:T(8,128)(2,1)S(1)}, u32[]{:S(2)}, u32[]{:S(2)}) %collective-permute-start.18) | collective-permute-done | bytes 147488 | tf_op jit(solution)/shard_map/ppermute | solution.py:418
  (37 shorter events, 12.4 us)
Async XLA Ops:
  0.6 20.8 %copy-start.1 = (bf16[4,48,256]{2,1,0:T(8,128)(2,1)S(1)}, bf16[4,48,256]{2,1,0:T(8,128)(2,1)}, u32[]{:S(2)}) copy-start(bf16[4,48,256]{2,1,0:T(8,128)(2,1)} %refs_9_.1) | copy-start | bytes 294916
  5.5 4.2 %collective-permute-start.3 = (bf16[928,256]{1,0:T(8,128)(2,1)S(1)}, bf16[928,256]{1,0:T(8,128)(2,1)S(1)}, u32[]{:S(2)}, u32[]{:S(2)}) collective-permute-start(bf16[928,256]{1,0:T(8,128)(2,1)S(1)} %get-tuple-element.40), channel_id=1, source_target_pairs={{0,4},{4,0},{8,12},{12,8},{16,20},{20,16},{24,28},{28,24},{1,5},{5... | collective-permute-start | bytes 1425416 | tf_op jit(solution)/shard_map/ppermute | solution.py:415
  6.0 10.0 %collective-permute-start.1 = (bf16[200,256]{1,0:T(8,128)(2,1)S(1)}, bf16[200,256]{1,0:T(8,128)(2,1)S(1)}, u32[]{:S(2)}, u32[]{:S(2)}) collective-permute-start(bf16[200,256]{1,0:T(8,128)(2,1)S(1)} %get-tuple-element.37), channel_id=1, source_target_pairs={{0,2},{1,3},{2,0},{3,1},{4,6},{5,7},{6,4},{7,5},{8,10},{9,11},{10,... | collective-permute-start | bytes 307208 | tf_op jit(solution)/shard_map/ppermute | solution.py:421
  9.7 44.8 %copy-start = (bf16[3,3,256,256]{3,2,1,0:T(8,128)(2,1)S(1)}, bf16[3,3,256,256]{3,2,1,0:T(8,128)(2,1)}, u32[]{:S(2)}) copy-start(bf16[3,3,256,256]{3,2,1,0:T(8,128)(2,1)} %param.11) | copy-start | bytes 3538948
  9.7 11.7 %collective-permute-start.4 = (bf16[256,256]{1,0:T(8,128)(2,1)S(1)}, bf16[256,256]{1,0:T(8,128)(2,1)S(1)}, u32[]{:S(2)}, u32[]{:S(2)}) collective-permute-start(bf16[256,256]{1,0:T(8,128)(2,1)S(1)} %get-tuple-element.42), channel_id=1, source_target_pairs={{0,8},{4,12},{8,0},{12,4},{16,24},{20,28},{24,16},{28,20},{1,9},{5... | collective-permute-start | bytes 393224 | tf_op jit(solution)/shard_map/ppermute | solution.py:418
  11.3 10.1 %collective-permute-start.6 = (bf16[256,256]{1,0:T(8,128)(2,1)S(1)}, bf16[256,256]{1,0:T(8,128)(2,1)S(1)}, u32[]{:S(2)}, u32[]{:S(2)}) collective-permute-start(bf16[256,256]{1,0:T(8,128)(2,1)S(1)} %get-tuple-element.44), channel_id=1, source_target_pairs={{0,24},{4,28},{8,16},{12,20},{16,8},{20,12},{24,0},{28,4},{1,25},{... | collective-permute-start | bytes 393224 | tf_op jit(solution)/shard_map/ppermute | solution.py:418
  12.8 5.1 %collective-permute-start = (bf16[224,256]{1,0:T(8,128)(2,1)S(1)}, bf16[224,256]{1,0:T(8,128)(2,1)S(1)}, u32[]{:S(2)}, u32[]{:S(2)}) collective-permute-start(bf16[224,256]{1,0:T(8,128)(2,1)S(1)} %get-tuple-element.36), channel_id=1, source_target_pairs={{0,1},{1,0},{2,3},{3,2},{4,5},{5,4},{6,7},{7,6},{8,9},{9,8},{10,11... | collective-permute-start | bytes 344072 | tf_op jit(solution)/shard_map/ppermute | solution.py:421
  14.4 6.9 %collective-permute-start.2 = (bf16[224,256]{1,0:T(8,128)(2,1)S(1)}, bf16[224,256]{1,0:T(8,128)(2,1)S(1)}, u32[]{:S(2)}, u32[]{:S(2)}) collective-permute-start(bf16[224,256]{1,0:T(8,128)(2,1)S(1)} %get-tuple-element.38), channel_id=1, source_target_pairs={{0,3},{1,2},{2,1},{3,0},{4,7},{5,6},{6,5},{7,4},{8,11},{9,10},{10,... | collective-permute-start | bytes 344072 | tf_op jit(solution)/shard_map/ppermute | solution.py:421
  16.0 5.4 %collective-permute-start.5 = (bf16[208,256]{1,0:T(8,128)(2,1)S(1)}, bf16[208,256]{1,0:T(8,128)(2,1)S(1)}, u32[]{:S(2)}, u32[]{:S(2)}) collective-permute-start(bf16[208,256]{1,0:T(8,128)(2,1)S(1)} %get-tuple-element.43), channel_id=1, source_target_pairs={{0,16},{4,20},{8,24},{12,28},{16,0},{20,4},{24,8},{28,12},{1,17},{... | collective-permute-start | bytes 319496 | tf_op jit(solution)/shard_map/ppermute | solution.py:418
  22.8 2.2 %collective-permute-start.7 = (bf16[1280,256]{1,0:T(8,128)(2,1)S(1)}, bf16[1280,256]{1,0:T(8,128)(2,1)S(1)}, u32[]{:S(2)}, u32[]{:S(2)}) collective-permute-start(bf16[1280,256]{1,0:T(8,128)(2,1)S(1)} %get-tuple-element.48), channel_id=1, source_target_pairs={{0,4},{4,0},{8,12},{12,8},{16,20},{20,16},{24,28},{28,24},{1,5},{5... | collective-permute-start | bytes 1966088 | tf_op jit(solution)/shard_map/ppermute | solution.py:415
  25.2 8.5 %collective-permute-start.9 = (bf16[288,256]{1,0:T(8,128)(2,1)S(1)}, bf16[288,256]{1,0:T(8,128)(2,1)S(1)}, u32[]{:S(2)}, u32[]{:S(2)}) collective-permute-start(bf16[288,256]{1,0:T(8,128)(2,1)S(1)} %get-tuple-element.53), channel_id=1, source_target_pairs={{0,8},{4,12},{8,0},{12,4},{16,24},{20,28},{24,16},{28,20},{1,9},{5... | collective-permute-start | bytes 442376 | tf_op jit(solution)/shard_map/ppermute | solution.py:418
  26.7 8.8 %collective-permute-start.10 = (bf16[288,256]{1,0:T(8,128)(2,1)S(1)}, bf16[288,256]{1,0:T(8,128)(2,1)S(1)}, u32[]{:S(2)}, u32[]{:S(2)}) collective-permute-start(bf16[288,256]{1,0:T(8,128)(2,1)S(1)} %get-tuple-element.54), channel_id=1, source_target_pairs={{0,16},{4,20},{8,24},{12,28},{16,0},{20,4},{24,8},{28,12},{1,17},{... | collective-permute-start | bytes 442376 | tf_op jit(solution)/shard_map/ppermute | solution.py:418
  27.2 8.3 %collective-permute-start.11 = (bf16[288,256]{1,0:T(8,128)(2,1)S(1)}, bf16[288,256]{1,0:T(8,128)(2,1)S(1)}, u32[]{:S(2)}, u32[]{:S(2)}) collective-permute-start(bf16[288,256]{1,0:T(8,128)(2,1)S(1)} %get-tuple-element.55), channel_id=1, source_target_pairs={{0,24},{4,28},{8,16},{12,20},{16,8},{20,12},{24,0},{28,4},{1,25},{... | collective-permute-start | bytes 442376 | tf_op jit(solution)/shard_map/ppermute | solution.py:418
  28.7 4.9 %collective-permute-start.8 = (bf16[50,256]{1,0:T(8,128)(2,1)S(1)}, bf16[50,256]{1,0:T(8,128)(2,1)S(1)}, u32[]{:S(2)}, u32[]{:S(2)}) collective-permute-start(bf16[50,256]{1,0:T(8,128)(2,1)S(1)} %get-tuple-element.50), channel_id=1, source_target_pairs={{0,8},{8,16},{16,24},{12,4},{20,12},{28,20},{1,9},{9,17},{17,25},{... | collective-permute-start | bytes 76808 | tf_op jit(solution)/shard_map/ppermute | solution.py:466
  35.6 5.9 %collective-permute-start.12 = (bf16[72,256]{1,0:T(8,128)(2,1)S(1)}, bf16[72,256]{1,0:T(8,128)(2,1)S(1)}, u32[]{:S(2)}, u32[]{:S(2)}) collective-permute-start(bf16[72,256]{1,0:T(8,128)(2,1)S(1)} %get-tuple-element.57), channel_id=1, source_target_pairs={{0,3},{1,2},{2,1},{3,0},{4,7},{5,6},{6,5},{7,4},{8,11},{9,10},{10,... | collective-permute-start | bytes 110600 | tf_op jit(solution)/shard_map/ppermute | solution.py:424
  38.4 4.9 %collective-permute-start.13 = (bf16[72,256]{1,0:T(8,128)(2,1)S(1)}, bf16[72,256]{1,0:T(8,128)(2,1)S(1)}, u32[]{:S(2)}, u32[]{:S(2)}) collective-permute-start(bf16[72,256]{1,0:T(8,128)(2,1)S(1)} %get-tuple-element.58), channel_id=1, source_target_pairs={{0,2},{1,3},{2,0},{3,1},{4,6},{5,7},{6,4},{7,5},{8,10},{9,11},{10,... | collective-permute-start | bytes 110600 | tf_op jit(solution)/shard_map/ppermute | solution.py:424
  38.7 4.6 %collective-permute-start.14 = (bf16[72,256]{1,0:T(8,128)(2,1)S(1)}, bf16[72,256]{1,0:T(8,128)(2,1)S(1)}, u32[]{:S(2)}, u32[]{:S(2)}) collective-permute-start(bf16[72,256]{1,0:T(8,128)(2,1)S(1)} %get-tuple-element.59), channel_id=1, source_target_pairs={{0,1},{1,0},{2,3},{3,2},{4,5},{5,4},{6,7},{7,6},{8,9},{9,8},{10,11... | collective-permute-start | bytes 110600 | tf_op jit(solution)/shard_map/ppermute | solution.py:424
  43.4 6.0 %collective-permute-start.15 = (bf16[98,256]{1,0:T(8,128)(2,1)S(1)}, bf16[98,256]{1,0:T(8,128)(2,1)S(1)}, u32[]{:S(2)}, u32[]{:S(2)}) collective-permute-start(bf16[98,256]{1,0:T(8,128)(2,1)S(1)} %get-tuple-element.60), channel_id=1, source_target_pairs={{0,3},{1,2},{2,1},{3,0},{4,7},{5,6},{6,5},{7,4},{8,11},{9,10},{10,... | collective-permute-start | bytes 150536 | tf_op jit(solution)/shard_map/ppermute | solution.py:424
  45.3 5.6 %collective-permute-start.16 = (bf16[98,256]{1,0:T(8,128)(2,1)S(1)}, bf16[98,256]{1,0:T(8,128)(2,1)S(1)}, u32[]{:S(2)}, u32[]{:S(2)}) collective-permute-start(bf16[98,256]{1,0:T(8,128)(2,1)S(1)} %get-tuple-element.61), channel_id=1, source_target_pairs={{0,2},{1,3},{2,0},{3,1},{4,6},{5,7},{6,4},{7,5},{8,10},{9,11},{10,... | collective-permute-start | bytes 150536 | tf_op jit(solution)/shard_map/ppermute | solution.py:424
  45.7 5.2 %collective-permute-start.17 = (bf16[98,256]{1,0:T(8,128)(2,1)S(1)}, bf16[98,256]{1,0:T(8,128)(2,1)S(1)}, u32[]{:S(2)}, u32[]{:S(2)}) collective-permute-start(bf16[98,256]{1,0:T(8,128)(2,1)S(1)} %get-tuple-element.62), channel_id=1, source_target_pairs={{0,1},{1,0},{2,3},{3,2},{4,5},{5,4},{6,7},{7,6},{8,9},{9,8},{10,11... | collective-permute-start | bytes 150536 | tf_op jit(solution)/shard_map/ppermute | solution.py:424
  51.0 5.2 %collective-permute-start.20 = (bf16[288,256]{1,0:T(8,128)(2,1)S(1)}, bf16[288,256]{1,0:T(8,128)(2,1)S(1)}, u32[]{:S(2)}, u32[]{:S(2)}) collective-permute-start(bf16[288,256]{1,0:T(8,128)(2,1)S(1)} %gather.2.refs_0_), channel_id=1, source_target_pairs={{0,8},{4,12},{8,0},{12,4},{16,24},{20,28},{24,16},{28,20},{1,9},{5... | collective-permute-start | bytes 442376 | tf_op jit(solution)/shard_map/ppermute | solution.py:418
  52.1 5.1 %collective-permute-start.19 = (bf16[288,256]{1,0:T(8,128)(2,1)S(1)}, bf16[288,256]{1,0:T(8,128)(2,1)S(1)}, u32[]{:S(2)}, u32[]{:S(2)}) collective-permute-start(bf16[288,256]{1,0:T(8,128)(2,1)S(1)} %gather.2.refs_0_), channel_id=1, source_target_pairs={{0,16},{4,20},{8,24},{12,28},{16,0},{20,4},{24,8},{28,12},{1,17},{... | collective-permute-start | bytes 442376 | tf_op jit(solution)/shard_map/ppermute | solution.py:418
  53.0 6.0 %collective-permute-start.18 = (bf16[288,256]{1,0:T(8,128)(2,1)S(1)}, bf16[288,256]{1,0:T(8,128)(2,1)S(1)}, u32[]{:S(2)}, u32[]{:S(2)}) collective-permute-start(bf16[288,256]{1,0:T(8,128)(2,1)S(1)} %gather.2.refs_0_), channel_id=1, source_target_pairs={{0,24},{4,28},{8,16},{12,20},{16,8},{20,12},{24,0},{28,4},{1,25},{... | collective-permute-start | bytes 442376 | tf_op jit(solution)/shard_map/ppermute | solution.py:418
  59.2 2.1 %collective-permute-start.21 = (bf16[1152,256]{1,0:T(8,128)(2,1)S(1)}, bf16[1152,256]{1,0:T(8,128)(2,1)S(1)}, u32[]{:S(2)}, u32[]{:S(2)}) collective-permute-start(bf16[1152,256]{1,0:T(8,128)(2,1)S(1)} %gather.3.refs_0_), channel_id=1, source_target_pairs={{0,4},{4,0},{8,12},{12,8},{16,20},{20,16},{24,28},{28,24},{1,5},{5... | collective-permute-start | bytes 1769480 | tf_op jit(solution)/shard_map/ppermute | solution.py:415
  (1 other events, 20.8 us)

commit v5 on v4

--- a/solution.py
+++ b/solution.py
@@ -210,7 +210,7 @@
     q_refs = refs[:n_ka]
     k_refs = refs[n_ka : n_ka + n_quad]
     near_ref, qi_ref, ki_ref = refs[n_ka + n_quad : n_ka + n_quad + 3]
-    send_ref, keep_ref, gq_ref, gk_ref, acc_ref, sum_ref, ext_ref = refs[n_ka + n_quad + 3 :]
+    send_ref, late_ref, keep_ref, gq_ref, gk_ref, acc_ref, sum_ref, ext_ref = refs[n_ka + n_quad + 3 :]
     size, channels = gk_ref.shape
     tile_k, key_rows, cin = ki_ref.shape
     rows, tile_q, _ = qi_ref.shape
@@ -248,37 +248,42 @@
         for a in range(3):
             tap = a * 3 + b + 1
             acc_ref[tap * cin : (tap + 1) * cin, :] = part[a * cin : (a + 1) * cin]
-    half = keep_ref.shape[0]
-    keep_ref[...] = acc_ref[pl.ds(pl.multiple_of(core * half, 16), half), :]
-    send_ref[0:half, :] = acc_ref[pl.ds(pl.multiple_of((1 - core) * half, 16), half), :].astype(BF16)
-    send_ref[half : half + wide, :] = sum_ref[0:wide, :].astype(BF16)
-    send_ref[half + up16(wide) : half + up16(wide) + wide, :] = sum_ref[(rows - 1) * wide : rows * wide, :].astype(BF16)
-
-
-def piece_kernel(keep_ref, recv_ref, own_ref, near_ref, onward_ref, *rest):
-    *sends, sum_ref = rest
-    quad, core, _ = place()
-    half = keep_ref.shape[0]
-    size = own_ref.shape[0]
+    quarter = late_ref.shape[0]
+    half = n_quad * quarter
+    for s in range(n_quad):
+        mine = pl.multiple_of(core * half + (quad ^ s) * quarter, 16)
+        other = pl.multiple_of((1 - core) * half + (quad ^ s) * quarter, 16)
+        keep_ref[s * quarter : (s + 1) * quarter, :] = acc_ref[pl.ds(mine, quarter), :]
+        if s:
+            send_ref[(s - 1) * quarter : s * quarter, :] = acc_ref[pl.ds(other, quarter), :].astype(BF16)
+        else:
+            late_ref[...] = acc_ref[pl.ds(other, quarter), :].astype(BF16)
+    base = half - quarter
+    send_ref[base : base + wide, :] = sum_ref[0:wide, :].astype(BF16)
+    send_ref[base + up16(wide) : base + up16(wide) + wide, :] = sum_ref[(rows - 1) * wide : rows * wide, :].astype(BF16)
+
+
+def piece_kernel(keep_ref, recv_ref, near_ref, onward_ref, *sends):
+    _, core, _ = place()
+    size = sends[0].shape[0]
     tile = near_ref.shape[0]
-    first = recv_ref[half : half + tile, :].astype(F32)
-    last = recv_ref[half + up16(tile) : half + up16(tile) + tile, :].astype(F32)
+    base = len(sends) * size
+    first = recv_ref[base : base + tile, :].astype(F32)
+    last = recv_ref[base + up16(tile) : base + up16(tile) + tile, :].astype(F32)
     near_ref[...] = jnp.where(core == 0, first, last).astype(BF16)
     onward_ref[...] = jnp.where(core == 0, last, first).astype(BF16)
-    sum_ref[...] = keep_ref[...] + recv_ref[0:half, :].astype(F32)
-    own_ref[...] = sum_ref[pl.ds(pl.multiple_of(quad * size, 16), size), :]
     for s, send in enumerate(sends, 1):
-        send[...] = sum_ref[pl.ds(pl.multiple_of((quad ^ s) * size, 16), size), :].astype(BF16)
+        send[...] = (keep_ref[s * size : (s + 1) * size, :] + recv_ref[(s - 1) * size : s * size, :].astype(F32)).astype(BF16)
 
 
 def layer_kernel(n_quad, *refs):
-    own_ref, *got = refs[:n_quad]
-    out_ref, *sends, stage_ref = refs[n_quad + 1 :]
+    keep_ref, *got = refs[: n_quad + 1]
+    out_ref, *sends, stage_ref = refs[n_quad + 2 :]
     _, _, z = place()
     n_ka = len(sends) + 1
-    size = own_ref.shape[0]
+    size = got[0].shape[0]
     piece = size // n_ka
-    total = own_ref[...]
+    total = keep_ref[0:size, :]
     for ref in got:
         total = total + ref[...].astype(F32)
     for k in range(n_ka):
@@ -445,12 +450,13 @@
     k_own, near, *k_pair = call(functools.partial(pair_kernel, size, tile_q), "pairs", outs, (k_keep, k_recv))
     k_more = to_quad(k_pair)
     outs = [
-        ((half + 2 * up16(wide), channels), BF16),
+        ((half - quarter + 2 * up16(wide), channels), BF16),
+        ((quarter, channels), BF16),
         ((half, channels), F32),
         ((strip_rows * wide, channels), BF16),
         ((size, channels), BF16),
     ]
-    w_send, w_keep, gq, gk = call(
+    w_send, w_late, w_keep, gq, gk = call(
         functools.partial(weight_kernel, n_ka, n_quad),
         "weights",
         outs,
@@ -459,8 +465,9 @@
     )
 
     w_recv = to_core(w_send)
-    outs = [((quarter, channels), F32)] + [((wide, channels), BF16)] * 2 + [((quarter, channels), BF16)] * (n_quad - 1)
-    own, near, far, *sends = call(piece_kernel, "pieces", outs, (w_keep, w_recv), [(half, channels)])
+    w_late = to_core(w_late)
+    outs = [((wide, channels), BF16)] * 2 + [((quarter, channels), BF16)] * (n_quad - 1)
+    near, far, *sends = call(piece_kernel, "pieces", outs, (w_keep, w_recv))
     got = to_quad(sends)
     firsts = range(0, n_pb - 2, 2)
     far = lax.ppermute(far, "pb", [(i, i + 2) for i in firsts] + [(i + 3, i + 1) for i in firsts])
@@ -468,7 +475,7 @@
         functools.partial(layer_kernel, n_quad),
         "layers",
         [((piece, channels), F32)] + [((piece, channels), BF16)] * (n_ka - 1),
-        (own, *got),
+        (w_keep, w_late, *got),
         [(n_ka, up16(piece), channels)],
         after=(far,),
     )

time: 62.5 us -> 62 us (level)
  waiting for transfers between devices: 20.2 us -> 19.5 us
    ppermute x3 -> x4, waiting for transfers between devices: 3.01 us -> 2.3 us  [to_core(): return lax.ppermute(x, 'pb', flip(n_pb, 1))]
  transfers between devices with their start and end apart: 22 -> 23, of which waited for: 14 -> 14; matrix products, arithmetic and copies ran while one was open for 0% -> 0% of each run, Pallas kernels for 4% -> 4%
where the time goes in v5:
time: 62 us; the launch traced here: 61.9 us
  starting transfers between devices  31.5 us (51%)
  waiting for transfers between devices  19.5 us (31%)
  Pallas kernels  10.1 us (16%)
  between operations  0.77 us (1%)
    ppermute x9, starting transfers between devices, to_quad(): lax.ppermute(x, 'pb', flip(n_pb, 2 * s))  11.2 us
    ppermute x6, starting transfers between devices, to_far_layers(): lax.ppermute(x, 'ka', flip(n_ka, n_ka - i))  8.91 us
    ppermute x3, starting transfers between devices, to_layers(): lax.ppermute(x, 'ka', flip(n_ka, s))  6.88 us
    ppermute x6, waiting for transfers between devices, to_far_layers(): lax.ppermute(x, 'ka', flip(n_ka, n_ka - i))  6.27 us
    ppermute x9, waiting for transfers between devices, to_quad(): lax.ppermute(x, 'pb', flip(n_pb, 2 * s))  5.14 us
    pallas_call x1, Pallas kernels, correlate(): pl.pallas_call(functools.partial(corr_kernel, dims), in_specs=[hbm] * 5,...  4.8 us
    ppermute x3, waiting for transfers between devices, to_layers(): lax.ppermute(x, 'ka', flip(n_ka, s))  4.27 us
    ppermute x1, starting transfers between devices, body(): lax.ppermute(far, 'pb', [(i, i + 2) for i in firsts] + [(i + 3, i + 1) fo...  3.39 us
  transfers between devices with their start and end apart: 23, of which 14 were waited for; matrix products, arithmetic and copies ran while one was open for 0% of the time, Pallas kernels for 4%

profile of v5, /device:TPU:0, one launch (start us, length us, event | category | flops | bytes accessed | tf_op | source)
XLA Modules:
  0.0 61.9 jit_solution(11114919954736950292)
XLA Ops:
  0.7 4.8 %correlate.1 = (bf16[200,256]{1,0:T(8,128)(2,1)S(1)}, bf16[224,256]{1,0:T(8,128)(2,1)S(1)}, bf16[200,256]{1,0:T(8,128)(2,1)S(1)}, bf16[224,256]{1,0:T(8,128)(2,1...) custom-call(bf16[2040,768]{1,0:T(8,128)(2,1)} %bitcast.11, bf16[768,256]{1,0:T(8,128)(2,1)} %bitcast.13, ...), custom_call_target="tpu_custom_call" | custom-call | tf_op jit(solution)/shard_map/correlate/pallas_call | solution.py:155
  6.0 3.7 %collective-permute-start.1 = (bf16[200,256]{1,0:T(8,128)(2,1)S(1)}, bf16[200,256]{1,0:T(8,128)(2,1)S(1)}, u32[]{:S(2)}, u32[]{:S(2)}) collective-permute-start(bf16[200,256]{1,0:T(8,128)(2,1)S(1)} %get-tuple-element.37), channel_id=1, source_target_pairs={{0,2},{1,3},{2,0},{3,1},{4,6},{5,7},{6,4},{7,5},{8,10},{9,11},{10,... | collective-permute-start | bytes 307208 | tf_op jit(solution)/shard_map/ppermute | solution.py:426
  9.7 1.6 %collective-permute-start.4 = (bf16[256,256]{1,0:T(8,128)(2,1)S(1)}, bf16[256,256]{1,0:T(8,128)(2,1)S(1)}, u32[]{:S(2)}, u32[]{:S(2)}) collective-permute-start(bf16[256,256]{1,0:T(8,128)(2,1)S(1)} %get-tuple-element.42), channel_id=1, source_target_pairs={{0,8},{4,12},{8,0},{12,4},{16,24},{20,28},{24,16},{28,20},{1,9},{5... | collective-permute-start | bytes 393224 | tf_op jit(solution)/shard_map/ppermute | solution.py:423
  11.3 1.5 %collective-permute-start.6 = (bf16[256,256]{1,0:T(8,128)(2,1)S(1)}, bf16[256,256]{1,0:T(8,128)(2,1)S(1)}, u32[]{:S(2)}, u32[]{:S(2)}) collective-permute-start(bf16[256,256]{1,0:T(8,128)(2,1)S(1)} %get-tuple-element.44), channel_id=1, source_target_pairs={{0,24},{4,28},{8,16},{12,20},{16,8},{20,12},{24,0},{28,4},{1,25},{... | collective-permute-start | bytes 393224 | tf_op jit(solution)/shard_map/ppermute | solution.py:423
  12.8 1.6 %collective-permute-start = (bf16[224,256]{1,0:T(8,128)(2,1)S(1)}, bf16[224,256]{1,0:T(8,128)(2,1)S(1)}, u32[]{:S(2)}, u32[]{:S(2)}) collective-permute-start(bf16[224,256]{1,0:T(8,128)(2,1)S(1)} %get-tuple-element.36), channel_id=1, source_target_pairs={{0,1},{1,0},{2,3},{3,2},{4,5},{5,4},{6,7},{7,6},{8,9},{9,8},{10,11... | collective-permute-start | bytes 344072 | tf_op jit(solution)/shard_map/ppermute | solution.py:426
  14.4 1.6 %collective-permute-start.2 = (bf16[224,256]{1,0:T(8,128)(2,1)S(1)}, bf16[224,256]{1,0:T(8,128)(2,1)S(1)}, u32[]{:S(2)}, u32[]{:S(2)}) collective-permute-start(bf16[224,256]{1,0:T(8,128)(2,1)S(1)} %get-tuple-element.38), channel_id=1, source_target_pairs={{0,3},{1,2},{2,1},{3,0},{4,7},{5,6},{6,5},{7,4},{8,11},{9,10},{10,... | collective-permute-start | bytes 344072 | tf_op jit(solution)/shard_map/ppermute | solution.py:426
  17.9 3.4 %collective-permute-done.2.refs_3_ = bf16[224,256]{1,0:T(8,128)(2,1)S(1)} collective-permute-done((bf16[224,256]{1,0:T(8,128)(2,1)S(1)}, bf16[224,256]{1,0:T(8,128)(2,1)S(1)}, u32[]{:S(2)}, u32[]{:S(2)}) %collective-permute-start.2) | collective-permute-done | bytes 114720 | tf_op jit(solution)/shard_map/ppermute | solution.py:426
  23.2 1.4 %collective-permute-done.7.recv_ref = bf16[992,256]{1,0:T(8,128)(2,1)S(1)} collective-permute-done((bf16[992,256]{1,0:T(8,128)(2,1)S(1)}, bf16[992,256]{1,0:T(8,128)(2,1)S(1)}, u32[]{:S(2)}, u32[]{:S(2)}) %collective-permute-start.7) | collective-permute-done | bytes 507936 | tf_op jit(solution)/shard_map/ppermute | solution.py:420
  24.6 1.6 %collective-permute-start.10 = (bf16[288,256]{1,0:T(8,128)(2,1)S(1)}, bf16[288,256]{1,0:T(8,128)(2,1)S(1)}, u32[]{:S(2)}, u32[]{:S(2)}) collective-permute-start(bf16[288,256]{1,0:T(8,128)(2,1)S(1)} %get-tuple-element.53), channel_id=1, source_target_pairs={{0,8},{4,12},{8,0},{12,4},{16,24},{20,28},{24,16},{28,20},{1,9},{5... | collective-permute-start | bytes 442376 | tf_op jit(solution)/shard_map/ppermute | solution.py:423
  26.7 1.5 %collective-permute-start.12 = (bf16[288,256]{1,0:T(8,128)(2,1)S(1)}, bf16[288,256]{1,0:T(8,128)(2,1)S(1)}, u32[]{:S(2)}, u32[]{:S(2)}) collective-permute-start(bf16[288,256]{1,0:T(8,128)(2,1)S(1)} %get-tuple-element.55), channel_id=1, source_target_pairs={{0,24},{4,28},{8,16},{12,20},{16,8},{20,12},{24,0},{28,4},{1,25},{... | collective-permute-start | bytes 442376 | tf_op jit(solution)/shard_map/ppermute | solution.py:423
  28.2 3.4 %collective-permute-start.8 = (bf16[50,256]{1,0:T(8,128)(2,1)S(1)}, bf16[50,256]{1,0:T(8,128)(2,1)S(1)}, u32[]{:S(2)}, u32[]{:S(2)}) collective-permute-start(bf16[50,256]{1,0:T(8,128)(2,1)S(1)} %get-tuple-element.50), channel_id=1, source_target_pairs={{0,8},{8,16},{16,24},{12,4},{20,12},{28,20},{1,9},{9,17},{17,25},{... | collective-permute-start | bytes 76808 | tf_op jit(solution)/shard_map/ppermute | solution.py:473
  31.6 1.5 %collective-permute-done.8.refs_5_.far_ref = bf16[50,256]{1,0:T(8,128)(2,1)S(1)} collective-permute-done((bf16[50,256]{1,0:T(8,128)(2,1)S(1)}, bf16[50,256]{1,0:T(8,128)(2,1)S(1)}, u32[]{:S(2)}, u32[]{:S(2)}) %collective-permute-start.8) | collective-permute-done | bytes 25632 | tf_op jit(solution)/shard_map/ppermute | solution.py:473
  33.1 1.8 %collective-permute-done.11.refs_3_ = bf16[288,256]{1,0:T(8,128)(2,1)S(1)} collective-permute-done((bf16[288,256]{1,0:T(8,128)(2,1)S(1)}, bf16[288,256]{1,0:T(8,128)(2,1)S(1)}, u32[]{:S(2)}, u32[]{:S(2)}) %collective-permute-start.11) | collective-permute-done | bytes 147488 | tf_op jit(solution)/shard_map/ppermute | solution.py:423
  35.1 2.8 %collective-permute-start.13 = (bf16[72,256]{1,0:T(8,128)(2,1)S(1)}, bf16[72,256]{1,0:T(8,128)(2,1)S(1)}, u32[]{:S(2)}, u32[]{:S(2)}) collective-permute-start(bf16[72,256]{1,0:T(8,128)(2,1)S(1)} %get-tuple-element.57), channel_id=1, source_target_pairs={{0,3},{1,2},{2,1},{3,0},{4,7},{5,6},{6,5},{7,4},{8,11},{9,10},{10,... | collective-permute-start | bytes 110600 | tf_op jit(solution)/shard_map/ppermute | solution.py:429
  38.2 1.4 %collective-permute-start.15 = (bf16[72,256]{1,0:T(8,128)(2,1)S(1)}, bf16[72,256]{1,0:T(8,128)(2,1)S(1)}, u32[]{:S(2)}, u32[]{:S(2)}) collective-permute-start(bf16[72,256]{1,0:T(8,128)(2,1)S(1)} %get-tuple-element.59), channel_id=1, source_target_pairs={{0,1},{1,0},{2,3},{3,2},{4,5},{5,4},{6,7},{7,6},{8,9},{9,8},{10,11... | collective-permute-start | bytes 110600 | tf_op jit(solution)/shard_map/ppermute | solution.py:429
  39.6 1.5 %collective-permute-done.13.refs_1_ = bf16[72,256]{1,0:T(8,128)(2,1)S(1)} collective-permute-done((bf16[72,256]{1,0:T(8,128)(2,1)S(1)}, bf16[72,256]{1,0:T(8,128)(2,1)S(1)}, u32[]{:S(2)}, u32[]{:S(2)}) %collective-permute-start.13) | collective-permute-done | bytes 36896 | tf_op jit(solution)/shard_map/ppermute | solution.py:429
  41.0 1.8 %collective-permute-done.14.refs_2_ = bf16[72,256]{1,0:T(8,128)(2,1)S(1)} collective-permute-done((bf16[72,256]{1,0:T(8,128)(2,1)S(1)}, bf16[72,256]{1,0:T(8,128)(2,1)S(1)}, u32[]{:S(2)}, u32[]{:S(2)}) %collective-permute-start.14) | collective-permute-done | bytes 36896 | tf_op jit(solution)/shard_map/ppermute | solution.py:429
  43.0 1.9 %collective-permute-start.16 = (bf16[98,256]{1,0:T(8,128)(2,1)S(1)}, bf16[98,256]{1,0:T(8,128)(2,1)S(1)}, u32[]{:S(2)}, u32[]{:S(2)}) collective-permute-start(bf16[98,256]{1,0:T(8,128)(2,1)S(1)} %get-tuple-element.60), channel_id=1, source_target_pairs={{0,3},{1,2},{2,1},{3,0},{4,7},{5,6},{6,5},{7,4},{8,11},{9,10},{10,... | collective-permute-start | bytes 150536 | tf_op jit(solution)/shard_map/ppermute | solution.py:429
  45.2 2.2 %collective-permute-start.18 = (bf16[98,256]{1,0:T(8,128)(2,1)S(1)}, bf16[98,256]{1,0:T(8,128)(2,1)S(1)}, u32[]{:S(2)}, u32[]{:S(2)}) collective-permute-start(bf16[98,256]{1,0:T(8,128)(2,1)S(1)} %get-tuple-element.62), channel_id=1, source_target_pairs={{0,1},{1,0},{2,3},{3,2},{4,5},{5,4},{6,7},{7,6},{8,9},{9,8},{10,11... | collective-permute-start | bytes 150536 | tf_op jit(solution)/shard_map/ppermute | solution.py:429
  47.4 1.5 %collective-permute-done.16.rest_0_.refs_1_ = bf16[98,256]{1,0:T(8,128)(2,1)S(1)} collective-permute-done((bf16[98,256]{1,0:T(8,128)(2,1)S(1)}, bf16[98,256]{1,0:T(8,128)(2,1)S(1)}, u32[]{:S(2)}, u32[]{:S(2)}) %collective-permute-start.16) | collective-permute-done | bytes 50208 | tf_op jit(solution)/shard_map/ppermute | solution.py:429
  49.0 1.5 %collective-permute-done.17.rest_1_.refs_2_ = bf16[98,256]{1,0:T(8,128)(2,1)S(1)} collective-permute-done((bf16[98,256]{1,0:T(8,128)(2,1)S(1)}, bf16[98,256]{1,0:T(8,128)(2,1)S(1)}, u32[]{:S(2)}, u32[]{:S(2)}) %collective-permute-start.17) | collective-permute-done | bytes 50208 | tf_op jit(solution)/shard_map/ppermute | solution.py:429
  52.5 1.5 %collective-permute-start.19 = (bf16[288,256]{1,0:T(8,128)(2,1)S(1)}, bf16[288,256]{1,0:T(8,128)(2,1)S(1)}, u32[]{:S(2)}, u32[]{:S(2)}) collective-permute-start(bf16[288,256]{1,0:T(8,128)(2,1)S(1)} %gather.2.refs_0_), channel_id=1, source_target_pairs={{0,24},{4,28},{8,16},{12,20},{16,8},{20,12},{24,0},{28,4},{1,25},{... | collective-permute-start | bytes 442376 | tf_op jit(solution)/shard_map/ppermute | solution.py:423
  54.1 1.4 %images.1 = (bf16[192,256]{1,0:T(8,128)(2,1)}, bf16[192,256]{1,0:T(8,128)(2,1)}, f32[8,128]{1,0:T(8,128)S(1)}) custom-call(bf16[200,256]{1,0:T(8,128)(2,1)S(1)} %get-tuple-element.46.gq_ref, bf16[50,256]{1,0:T(8,128)(2,1)S(1)} %get-tuple-element.49.near_ref, bf16[50,256]{1,0:T(8,128)(2,1)S(1)} %collective-permute-done.8.refs_5_.far_ref, ...), custom_call_target="tpu_custom_call" | custom-call | tf_op jit(solution)/shard_map/images/pallas_call | solution.py:391
  56.8 1.8 %collective-permute-done.19.refs_1_ = bf16[288,256]{1,0:T(8,128)(2,1)S(1)} collective-permute-done((bf16[288,256]{1,0:T(8,128)(2,1)S(1)}, bf16[288,256]{1,0:T(8,128)(2,1)S(1)}, u32[]{:S(2)}, u32[]{:S(2)}) %collective-permute-start.19) | collective-permute-done | bytes 147488 | tf_op jit(solution)/shard_map/ppermute | solution.py:423
  (39 shorter events, 12.6 us)
Async XLA Ops:
  5.5 4.2 %collective-permute-start.3 = (bf16[928,256]{1,0:T(8,128)(2,1)S(1)}, bf16[928,256]{1,0:T(8,128)(2,1)S(1)}, u32[]{:S(2)}, u32[]{:S(2)}) collective-permute-start(bf16[928,256]{1,0:T(8,128)(2,1)S(1)} %get-tuple-element.40), channel_id=1, source_target_pairs={{0,4},{4,0},{8,12},{12,8},{16,20},{20,16},{24,28},{28,24},{1,5},{5... | collective-permute-start | bytes 1425416 | tf_op jit(solution)/shard_map/ppermute | solution.py:420
  6.0 10.0 %collective-permute-start.1 = (bf16[200,256]{1,0:T(8,128)(2,1)S(1)}, bf16[200,256]{1,0:T(8,128)(2,1)S(1)}, u32[]{:S(2)}, u32[]{:S(2)}) collective-permute-start(bf16[200,256]{1,0:T(8,128)(2,1)S(1)} %get-tuple-element.37), channel_id=1, source_target_pairs={{0,2},{1,3},{2,0},{3,1},{4,6},{5,7},{6,4},{7,5},{8,10},{9,11},{10,... | collective-permute-start | bytes 307208 | tf_op jit(solution)/shard_map/ppermute | solution.py:426
  9.7 11.7 %collective-permute-start.4 = (bf16[256,256]{1,0:T(8,128)(2,1)S(1)}, bf16[256,256]{1,0:T(8,128)(2,1)S(1)}, u32[]{:S(2)}, u32[]{:S(2)}) collective-permute-start(bf16[256,256]{1,0:T(8,128)(2,1)S(1)} %get-tuple-element.42), channel_id=1, source_target_pairs={{0,8},{4,12},{8,0},{12,4},{16,24},{20,28},{24,16},{28,20},{1,9},{5... | collective-permute-start | bytes 393224 | tf_op jit(solution)/shard_map/ppermute | solution.py:423
  11.3 10.1 %collective-permute-start.6 = (bf16[256,256]{1,0:T(8,128)(2,1)S(1)}, bf16[256,256]{1,0:T(8,128)(2,1)S(1)}, u32[]{:S(2)}, u32[]{:S(2)}) collective-permute-start(bf16[256,256]{1,0:T(8,128)(2,1)S(1)} %get-tuple-element.44), channel_id=1, source_target_pairs={{0,24},{4,28},{8,16},{12,20},{16,8},{20,12},{24,0},{28,4},{1,25},{... | collective-permute-start | bytes 393224 | tf_op jit(solution)/shard_map/ppermute | solution.py:423
  12.8 5.1 %collective-permute-start = (bf16[224,256]{1,0:T(8,128)(2,1)S(1)}, bf16[224,256]{1,0:T(8,128)(2,1)S(1)}, u32[]{:S(2)}, u32[]{:S(2)}) collective-permute-start(bf16[224,256]{1,0:T(8,128)(2,1)S(1)} %get-tuple-element.36), channel_id=1, source_target_pairs={{0,1},{1,0},{2,3},{3,2},{4,5},{5,4},{6,7},{7,6},{8,9},{9,8},{10,11... | collective-permute-start | bytes 344072 | tf_op jit(solution)/shard_map/ppermute | solution.py:426
  14.4 6.9 %collective-permute-start.2 = (bf16[224,256]{1,0:T(8,128)(2,1)S(1)}, bf16[224,256]{1,0:T(8,128)(2,1)S(1)}, u32[]{:S(2)}, u32[]{:S(2)}) collective-permute-start(bf16[224,256]{1,0:T(8,128)(2,1)S(1)} %get-tuple-element.38), channel_id=1, source_target_pairs={{0,3},{1,2},{2,1},{3,0},{4,7},{5,6},{6,5},{7,4},{8,11},{9,10},{10,... | collective-permute-start | bytes 344072 | tf_op jit(solution)/shard_map/ppermute | solution.py:426
  16.0 5.4 %collective-permute-start.5 = (bf16[208,256]{1,0:T(8,128)(2,1)S(1)}, bf16[208,256]{1,0:T(8,128)(2,1)S(1)}, u32[]{:S(2)}, u32[]{:S(2)}) collective-permute-start(bf16[208,256]{1,0:T(8,128)(2,1)S(1)} %get-tuple-element.43), channel_id=1, source_target_pairs={{0,16},{4,20},{8,24},{12,28},{16,0},{20,4},{24,8},{28,12},{1,17},{... | collective-permute-start | bytes 319496 | tf_op jit(solution)/shard_map/ppermute | solution.py:423
  22.6 31.5 %copy-start = (bf16[3,3,256,256]{3,2,1,0:T(8,128)(2,1)S(1)}, bf16[3,3,256,256]{3,2,1,0:T(8,128)(2,1)}, u32[]{:S(2)}) copy-start(bf16[3,3,256,256]{3,2,1,0:T(8,128)(2,1)} %param.11) | copy-start | bytes 3538948
  22.6 2.0 %collective-permute-start.7 = (bf16[992,256]{1,0:T(8,128)(2,1)S(1)}, bf16[992,256]{1,0:T(8,128)(2,1)S(1)}, u32[]{:S(2)}, u32[]{:S(2)}) collective-permute-start(bf16[992,256]{1,0:T(8,128)(2,1)S(1)} %get-tuple-element.48), channel_id=1, source_target_pairs={{0,4},{4,0},{8,12},{12,8},{16,20},{20,16},{24,28},{28,24},{1,5},{5... | collective-permute-start | bytes 1523720 | tf_op jit(solution)/shard_map/ppermute | solution.py:420
  22.7 8.9 %collective-permute-start.9 = (bf16[288,256]{1,0:T(8,128)(2,1)S(1)}, bf16[288,256]{1,0:T(8,128)(2,1)S(1)}, u32[]{:S(2)}, u32[]{:S(2)}) collective-permute-start(bf16[288,256]{1,0:T(8,128)(2,1)S(1)} %get-tuple-element.52), channel_id=1, source_target_pairs={{0,4},{4,0},{8,12},{12,8},{16,20},{20,16},{24,28},{28,24},{1,5},{5... | collective-permute-start | bytes 442376 | tf_op jit(solution)/shard_map/ppermute | solution.py:420
  24.6 8.5 %collective-permute-start.10 = (bf16[288,256]{1,0:T(8,128)(2,1)S(1)}, bf16[288,256]{1,0:T(8,128)(2,1)S(1)}, u32[]{:S(2)}, u32[]{:S(2)}) collective-permute-start(bf16[288,256]{1,0:T(8,128)(2,1)S(1)} %get-tuple-element.53), channel_id=1, source_target_pairs={{0,8},{4,12},{8,0},{12,4},{16,24},{20,28},{24,16},{28,20},{1,9},{5... | collective-permute-start | bytes 442376 | tf_op jit(solution)/shard_map/ppermute | solution.py:423
  26.2 8.8 %collective-permute-start.11 = (bf16[288,256]{1,0:T(8,128)(2,1)S(1)}, bf16[288,256]{1,0:T(8,128)(2,1)S(1)}, u32[]{:S(2)}, u32[]{:S(2)}) collective-permute-start(bf16[288,256]{1,0:T(8,128)(2,1)S(1)} %get-tuple-element.54), channel_id=1, source_target_pairs={{0,16},{4,20},{8,24},{12,28},{16,0},{20,4},{24,8},{28,12},{1,17},{... | collective-permute-start | bytes 442376 | tf_op jit(solution)/shard_map/ppermute | solution.py:423
  26.7 8.3 %collective-permute-start.12 = (bf16[288,256]{1,0:T(8,128)(2,1)S(1)}, bf16[288,256]{1,0:T(8,128)(2,1)S(1)}, u32[]{:S(2)}, u32[]{:S(2)}) collective-permute-start(bf16[288,256]{1,0:T(8,128)(2,1)S(1)} %get-tuple-element.55), channel_id=1, source_target_pairs={{0,24},{4,28},{8,16},{12,20},{16,8},{20,12},{24,0},{28,4},{1,25},{... | collective-permute-start | bytes 442376 | tf_op jit(solution)/shard_map/ppermute | solution.py:423
  28.2 4.9 %collective-permute-start.8 = (bf16[50,256]{1,0:T(8,128)(2,1)S(1)}, bf16[50,256]{1,0:T(8,128)(2,1)S(1)}, u32[]{:S(2)}, u32[]{:S(2)}) collective-permute-start(bf16[50,256]{1,0:T(8,128)(2,1)S(1)} %get-tuple-element.50), channel_id=1, source_target_pairs={{0,8},{8,16},{16,24},{12,4},{20,12},{28,20},{1,9},{9,17},{17,25},{... | collective-permute-start | bytes 76808 | tf_op jit(solution)/shard_map/ppermute | solution.py:473
  35.1 5.9 %collective-permute-start.13 = (bf16[72,256]{1,0:T(8,128)(2,1)S(1)}, bf16[72,256]{1,0:T(8,128)(2,1)S(1)}, u32[]{:S(2)}, u32[]{:S(2)}) collective-permute-start(bf16[72,256]{1,0:T(8,128)(2,1)S(1)} %get-tuple-element.57), channel_id=1, source_target_pairs={{0,3},{1,2},{2,1},{3,0},{4,7},{5,6},{6,5},{7,4},{8,11},{9,10},{10,... | collective-permute-start | bytes 110600 | tf_op jit(solution)/shard_map/ppermute | solution.py:429
  37.9 4.9 %collective-permute-start.14 = (bf16[72,256]{1,0:T(8,128)(2,1)S(1)}, bf16[72,256]{1,0:T(8,128)(2,1)S(1)}, u32[]{:S(2)}, u32[]{:S(2)}) collective-permute-start(bf16[72,256]{1,0:T(8,128)(2,1)S(1)} %get-tuple-element.58), channel_id=1, source_target_pairs={{0,2},{1,3},{2,0},{3,1},{4,6},{5,7},{6,4},{7,5},{8,10},{9,11},{10,... | collective-permute-start | bytes 110600 | tf_op jit(solution)/shard_map/ppermute | solution.py:429
  38.2 4.6 %collective-permute-start.15 = (bf16[72,256]{1,0:T(8,128)(2,1)S(1)}, bf16[72,256]{1,0:T(8,128)(2,1)S(1)}, u32[]{:S(2)}, u32[]{:S(2)}) collective-permute-start(bf16[72,256]{1,0:T(8,128)(2,1)S(1)} %get-tuple-element.59), channel_id=1, source_target_pairs={{0,1},{1,0},{2,3},{3,2},{4,5},{5,4},{6,7},{7,6},{8,9},{9,8},{10,11... | collective-permute-start | bytes 110600 | tf_op jit(solution)/shard_map/ppermute | solution.py:429
  43.0 6.0 %collective-permute-start.16 = (bf16[98,256]{1,0:T(8,128)(2,1)S(1)}, bf16[98,256]{1,0:T(8,128)(2,1)S(1)}, u32[]{:S(2)}, u32[]{:S(2)}) collective-permute-start(bf16[98,256]{1,0:T(8,128)(2,1)S(1)} %get-tuple-element.60), channel_id=1, source_target_pairs={{0,3},{1,2},{2,1},{3,0},{4,7},{5,6},{6,5},{7,4},{8,11},{9,10},{10,... | collective-permute-start | bytes 150536 | tf_op jit(solution)/shard_map/ppermute | solution.py:429
  44.8 5.6 %collective-permute-start.17 = (bf16[98,256]{1,0:T(8,128)(2,1)S(1)}, bf16[98,256]{1,0:T(8,128)(2,1)S(1)}, u32[]{:S(2)}, u32[]{:S(2)}) collective-permute-start(bf16[98,256]{1,0:T(8,128)(2,1)S(1)} %get-tuple-element.61), channel_id=1, source_target_pairs={{0,2},{1,3},{2,0},{3,1},{4,6},{5,7},{6,4},{7,5},{8,10},{9,11},{10,... | collective-permute-start | bytes 150536 | tf_op jit(solution)/shard_map/ppermute | solution.py:429
  45.2 5.2 %collective-permute-start.18 = (bf16[98,256]{1,0:T(8,128)(2,1)S(1)}, bf16[98,256]{1,0:T(8,128)(2,1)S(1)}, u32[]{:S(2)}, u32[]{:S(2)}) collective-permute-start(bf16[98,256]{1,0:T(8,128)(2,1)S(1)} %get-tuple-element.62), channel_id=1, source_target_pairs={{0,1},{1,0},{2,3},{3,2},{4,5},{5,4},{6,7},{7,6},{8,9},{9,8},{10,11... | collective-permute-start | bytes 150536 | tf_op jit(solution)/shard_map/ppermute | solution.py:429
  50.5 5.2 %collective-permute-start.21 = (bf16[288,256]{1,0:T(8,128)(2,1)S(1)}, bf16[288,256]{1,0:T(8,128)(2,1)S(1)}, u32[]{:S(2)}, u32[]{:S(2)}) collective-permute-start(bf16[288,256]{1,0:T(8,128)(2,1)S(1)} %gather.2.refs_0_), channel_id=1, source_target_pairs={{0,8},{4,12},{8,0},{12,4},{16,24},{20,28},{24,16},{28,20},{1,9},{5... | collective-permute-start | bytes 442376 | tf_op jit(solution)/shard_map/ppermute | solution.py:423
  51.7 5.1 %collective-permute-start.20 = (bf16[288,256]{1,0:T(8,128)(2,1)S(1)}, bf16[288,256]{1,0:T(8,128)(2,1)S(1)}, u32[]{:S(2)}, u32[]{:S(2)}) collective-permute-start(bf16[288,256]{1,0:T(8,128)(2,1)S(1)} %gather.2.refs_0_), channel_id=1, source_target_pairs={{0,16},{4,20},{8,24},{12,28},{16,0},{20,4},{24,8},{28,12},{1,17},{... | collective-permute-start | bytes 442376 | tf_op jit(solution)/shard_map/ppermute | solution.py:423
  52.5 6.0 %collective-permute-start.19 = (bf16[288,256]{1,0:T(8,128)(2,1)S(1)}, bf16[288,256]{1,0:T(8,128)(2,1)S(1)}, u32[]{:S(2)}, u32[]{:S(2)}) collective-permute-start(bf16[288,256]{1,0:T(8,128)(2,1)S(1)} %gather.2.refs_0_), channel_id=1, source_target_pairs={{0,24},{4,28},{8,16},{12,20},{16,8},{20,12},{24,0},{28,4},{1,25},{... | collective-permute-start | bytes 442376 | tf_op jit(solution)/shard_map/ppermute | solution.py:423
  58.7 2.1 %collective-permute-start.22 = (bf16[1152,256]{1,0:T(8,128)(2,1)S(1)}, bf16[1152,256]{1,0:T(8,128)(2,1)S(1)}, u32[]{:S(2)}, u32[]{:S(2)}) collective-permute-start(bf16[1152,256]{1,0:T(8,128)(2,1)S(1)} %gather.3.refs_0_), channel_id=1, source_target_pairs={{0,4},{4,0},{8,12},{12,8},{16,20},{20,16},{24,28},{28,24},{1,5},{5... | collective-permute-start | bytes 1769480 | tf_op jit(solution)/shard_map/ppermute | solution.py:420
  (2 other events, 41.6 us)

commit v6 on v5

--- a/solution.py
+++ b/solution.py
@@ -248,7 +248,7 @@
         for a in range(3):
             tap = a * 3 + b + 1
             acc_ref[tap * cin : (tap + 1) * cin, :] = part[a * cin : (a + 1) * cin]
-    quarter = late_ref.shape[0]
+    quarter = acc_ref.shape[0] // (2 * n_quad)
     half = n_quad * quarter
     for s in range(n_quad):
         mine = pl.multiple_of(core * half + (quad ^ s) * quarter, 16)
@@ -257,23 +257,24 @@
         if s:
             send_ref[(s - 1) * quarter : s * quarter, :] = acc_ref[pl.ds(other, quarter), :].astype(BF16)
         else:
-            late_ref[...] = acc_ref[pl.ds(other, quarter), :].astype(BF16)
-    base = half - quarter
-    send_ref[base : base + wide, :] = sum_ref[0:wide, :].astype(BF16)
-    send_ref[base + up16(wide) : base + up16(wide) + wide, :] = sum_ref[(rows - 1) * wide : rows * wide, :].astype(BF16)
-
-
-def piece_kernel(keep_ref, recv_ref, near_ref, onward_ref, *sends):
+            late_ref[0:quarter, :] = acc_ref[pl.ds(other, quarter), :].astype(BF16)
+    late_ref[quarter : quarter + wide, :] = sum_ref[0:wide, :].astype(BF16)
+    late_ref[quarter + up16(wide) : quarter + up16(wide) + wide, :] = sum_ref[(rows - 1) * wide : rows * wide, :].astype(BF16)
+
+
+def piece_kernel(keep_ref, recv_ref, *sends):
+    size = sends[0].shape[0]
+    for s, send in enumerate(sends, 1):
+        send[...] = (keep_ref[s * size : (s + 1) * size, :] + recv_ref[(s - 1) * size : s * size, :].astype(F32)).astype(BF16)
+
+
+def line_kernel(size, late_ref, near_ref, onward_ref):
     _, core, _ = place()
-    size = sends[0].shape[0]
     tile = near_ref.shape[0]
-    base = len(sends) * size
-    first = recv_ref[base : base + tile, :].astype(F32)
-    last = recv_ref[base + up16(tile) : base + up16(tile) + tile, :].astype(F32)
+    first = late_ref[size : size + tile, :].astype(F32)
+    last = late_ref[size + up16(tile) : size + up16(tile) + tile, :].astype(F32)
     near_ref[...] = jnp.where(core == 0, first, last).astype(BF16)
     onward_ref[...] = jnp.where(core == 0, last, first).astype(BF16)
-    for s, send in enumerate(sends, 1):
-        send[...] = (keep_ref[s * size : (s + 1) * size, :] + recv_ref[(s - 1) * size : s * size, :].astype(F32)).astype(BF16)
 
 
 def layer_kernel(n_quad, *refs):
@@ -281,11 +282,11 @@
     out_ref, *sends, stage_ref = refs[n_quad + 2 :]
     _, _, z = place()
     n_ka = len(sends) + 1
-    size = got[0].shape[0]
+    size = got[1].shape[0]
     piece = size // n_ka
     total = keep_ref[0:size, :]
     for ref in got:
-        total = total + ref[...].astype(F32)
+        total = total + ref[0:size, :].astype(F32)
     for k in range(n_ka):
         stage_ref[z ^ k, 0:piece, :] = total[k * piece : (k + 1) * piece]
     out_ref[...] = stage_ref[0, 0:piece, :]
@@ -380,7 +381,7 @@
         in_specs=[vmem] + [hbm] * len(more),
         out_specs=hbm,
         out_shape=jax.ShapeDtypeStruct((2 * rows, channels), F32),
-        scratch_shapes=[pltpu.VMEM((rows, channels), F32), pltpu.SemaphoreType.DMA((4,))],
+        scratch_shapes=[pltpu.VMEM((rows, channels), F32), pltpu.SemaphoreType.DMA((8,))],
         input_output_aliases={1: 0} if more else {},
         compiler_params=pltpu.CompilerParams(vmem_limit_bytes=SMALL_BYTES),
         name="widen",
@@ -450,8 +451,8 @@
     k_own, near, *k_pair = call(functools.partial(pair_kernel, size, tile_q), "pairs", outs, (k_keep, k_recv))
     k_more = to_quad(k_pair)
     outs = [
-        ((half - quarter + 2 * up16(wide), channels), BF16),
-        ((quarter, channels), BF16),
+        ((half - quarter, channels), BF16),
+        ((quarter + 2 * up16(wide), channels), BF16),
         ((half, channels), F32),
         ((strip_rows * wide, channels), BF16),
         ((size, channels), BF16),
@@ -466,8 +467,8 @@
 
     w_recv = to_core(w_send)
     w_late = to_core(w_late)
-    outs = [((wide, channels), BF16)] * 2 + [((quarter, channels), BF16)] * (n_quad - 1)
-    near, far, *sends = call(piece_kernel, "pieces", outs, (w_keep, w_recv))
+    sends = call(piece_kernel, "pieces", [((quarter, channels), BF16)] * (n_quad - 1), (w_keep, w_recv))
+    near, far = call(functools.partial(line_kernel, quarter), "lines", [((wide, channels), BF16)] * 2, (w_late,))
     got = to_quad(sends)
     firsts = range(0, n_pb - 2, 2)
     far = lax.ppermute(far, "pb", [(i, i + 2) for i in firsts] + [(i + 3, i + 1) for i in firsts])

time: 62 us -> 62 us (level)
    pallas_call x8 -> x9, Pallas kernels: 3.16 us -> 3.17 us  [call(): pl.pallas_call(kernel, in_specs=[pl.BlockSpec(memory_space=pltpu.VMEM)] *...]
where the time goes in v6:
time: 62 us; the launch traced here: 61.8 us
  starting transfers between devices  31.5 us (51%)
  waiting for transfers between devices  19.4 us (31%)
  Pallas kernels  10.2 us (16%)
  between operations  0.77 us (1%)
    ppermute x9, starting transfers between devices, to_quad(): lax.ppermute(x, 'pb', flip(n_pb, 2 * s))  11.2 us
    ppermute x6, starting transfers between devices, to_far_layers(): lax.ppermute(x, 'ka', flip(n_ka, n_ka - i))  8.91 us
    ppermute x3, starting transfers between devices, to_layers(): lax.ppermute(x, 'ka', flip(n_ka, s))  6.88 us
    ppermute x6, waiting for transfers between devices, to_far_layers(): lax.ppermute(x, 'ka', flip(n_ka, n_ka - i))  6.27 us
    ppermute x9, waiting for transfers between devices, to_quad(): lax.ppermute(x, 'pb', flip(n_pb, 2 * s))  5.12 us
    pallas_call x1, Pallas kernels, correlate(): pl.pallas_call(functools.partial(corr_kernel, dims), in_specs=[hbm] * 5,...  4.8 us
    ppermute x3, waiting for transfers between devices, to_layers(): lax.ppermute(x, 'ka', flip(n_ka, s))  4.27 us
    ppermute x1, starting transfers between devices, body(): lax.ppermute(far, 'pb', [(i, i + 2) for i in firsts] + [(i + 3, i + 1) fo...  3.4 us
  transfers between devices with their start and end apart: 23, of which 14 were waited for; matrix products, arithmetic and copies ran while one was open for 0% of the time, Pallas kernels for 4%

profile of v6, /device:TPU:0, one launch (start us, length us, event | category | flops | bytes accessed | tf_op | source)
XLA Modules:
  0.0 61.8 jit_solution(3623754457775559865)
XLA Ops:
  0.7 4.8 %correlate.1 = (bf16[200,256]{1,0:T(8,128)(2,1)S(1)}, bf16[224,256]{1,0:T(8,128)(2,1)S(1)}, bf16[200,256]{1,0:T(8,128)(2,1)S(1)}, bf16[224,256]{1,0:T(8,128)(2,1...) custom-call(bf16[2040,768]{1,0:T(8,128)(2,1)} %bitcast.11, bf16[768,256]{1,0:T(8,128)(2,1)} %bitcast.13, ...), custom_call_target="tpu_custom_call" | custom-call | tf_op jit(solution)/shard_map/correlate/pallas_call | solution.py:155
  6.0 3.7 %collective-permute-start.1 = (bf16[200,256]{1,0:T(8,128)(2,1)S(1)}, bf16[200,256]{1,0:T(8,128)(2,1)S(1)}, u32[]{:S(2)}, u32[]{:S(2)}) collective-permute-start(bf16[200,256]{1,0:T(8,128)(2,1)S(1)} %get-tuple-element.37), channel_id=1, source_target_pairs={{0,2},{1,3},{2,0},{3,1},{4,6},{5,7},{6,4},{7,5},{8,10},{9,11},{10,... | collective-permute-start | bytes 307208 | tf_op jit(solution)/shard_map/ppermute | solution.py:427
  9.7 1.6 %collective-permute-start.4 = (bf16[256,256]{1,0:T(8,128)(2,1)S(1)}, bf16[256,256]{1,0:T(8,128)(2,1)S(1)}, u32[]{:S(2)}, u32[]{:S(2)}) collective-permute-start(bf16[256,256]{1,0:T(8,128)(2,1)S(1)} %get-tuple-element.42), channel_id=1, source_target_pairs={{0,8},{4,12},{8,0},{12,4},{16,24},{20,28},{24,16},{28,20},{1,9},{5... | collective-permute-start | bytes 393224 | tf_op jit(solution)/shard_map/ppermute | solution.py:424
  11.3 1.5 %collective-permute-start.6 = (bf16[256,256]{1,0:T(8,128)(2,1)S(1)}, bf16[256,256]{1,0:T(8,128)(2,1)S(1)}, u32[]{:S(2)}, u32[]{:S(2)}) collective-permute-start(bf16[256,256]{1,0:T(8,128)(2,1)S(1)} %get-tuple-element.44), channel_id=1, source_target_pairs={{0,24},{4,28},{8,16},{12,20},{16,8},{20,12},{24,0},{28,4},{1,25},{... | collective-permute-start | bytes 393224 | tf_op jit(solution)/shard_map/ppermute | solution.py:424
  12.8 1.6 %collective-permute-start = (bf16[224,256]{1,0:T(8,128)(2,1)S(1)}, bf16[224,256]{1,0:T(8,128)(2,1)S(1)}, u32[]{:S(2)}, u32[]{:S(2)}) collective-permute-start(bf16[224,256]{1,0:T(8,128)(2,1)S(1)} %get-tuple-element.36), channel_id=1, source_target_pairs={{0,1},{1,0},{2,3},{3,2},{4,5},{5,4},{6,7},{7,6},{8,9},{9,8},{10,11... | collective-permute-start | bytes 344072 | tf_op jit(solution)/shard_map/ppermute | solution.py:427
  14.4 1.6 %collective-permute-start.2 = (bf16[224,256]{1,0:T(8,128)(2,1)S(1)}, bf16[224,256]{1,0:T(8,128)(2,1)S(1)}, u32[]{:S(2)}, u32[]{:S(2)}) collective-permute-start(bf16[224,256]{1,0:T(8,128)(2,1)S(1)} %get-tuple-element.38), channel_id=1, source_target_pairs={{0,3},{1,2},{2,1},{3,0},{4,7},{5,6},{6,5},{7,4},{8,11},{9,10},{10,... | collective-permute-start | bytes 344072 | tf_op jit(solution)/shard_map/ppermute | solution.py:427
  17.9 3.4 %collective-permute-done.2.refs_3_ = bf16[224,256]{1,0:T(8,128)(2,1)S(1)} collective-permute-done((bf16[224,256]{1,0:T(8,128)(2,1)S(1)}, bf16[224,256]{1,0:T(8,128)(2,1)S(1)}, u32[]{:S(2)}, u32[]{:S(2)}) %collective-permute-start.2) | collective-permute-done | bytes 114720 | tf_op jit(solution)/shard_map/ppermute | solution.py:427
  23.2 1.3 %collective-permute-done.9.recv_ref = bf16[864,256]{1,0:T(8,128)(2,1)S(1)} collective-permute-done((bf16[864,256]{1,0:T(8,128)(2,1)S(1)}, bf16[864,256]{1,0:T(8,128)(2,1)S(1)}, u32[]{:S(2)}, u32[]{:S(2)}) %collective-permute-start.9) | collective-permute-done | bytes 442400 | tf_op jit(solution)/shard_map/ppermute | solution.py:421
  24.6 1.6 %collective-permute-start.10 = (bf16[288,256]{1,0:T(8,128)(2,1)S(1)}, bf16[288,256]{1,0:T(8,128)(2,1)S(1)}, u32[]{:S(2)}, u32[]{:S(2)}) collective-permute-start(bf16[288,256]{1,0:T(8,128)(2,1)S(1)} %get-tuple-element.53), channel_id=1, source_target_pairs={{0,8},{4,12},{8,0},{12,4},{16,24},{20,28},{24,16},{28,20},{1,9},{5... | collective-permute-start | bytes 442376 | tf_op jit(solution)/shard_map/ppermute | solution.py:424
  26.6 1.5 %collective-permute-start.12 = (bf16[288,256]{1,0:T(8,128)(2,1)S(1)}, bf16[288,256]{1,0:T(8,128)(2,1)S(1)}, u32[]{:S(2)}, u32[]{:S(2)}) collective-permute-start(bf16[288,256]{1,0:T(8,128)(2,1)S(1)} %get-tuple-element.55), channel_id=1, source_target_pairs={{0,24},{4,28},{8,16},{12,20},{16,8},{20,12},{24,0},{28,4},{1,25},{... | collective-permute-start | bytes 442376 | tf_op jit(solution)/shard_map/ppermute | solution.py:424
  28.1 3.4 %collective-permute-start.8 = (bf16[50,256]{1,0:T(8,128)(2,1)S(1)}, bf16[50,256]{1,0:T(8,128)(2,1)S(1)}, u32[]{:S(2)}, u32[]{:S(2)}) collective-permute-start(bf16[50,256]{1,0:T(8,128)(2,1)S(1)} %get-tuple-element.49), channel_id=1, source_target_pairs={{0,8},{8,16},{16,24},{12,4},{20,12},{28,20},{1,9},{9,17},{17,25},{... | collective-permute-start | bytes 76808 | tf_op jit(solution)/shard_map/ppermute | solution.py:474
  31.5 1.5 %collective-permute-done.8.refs_5_.far_ref = bf16[50,256]{1,0:T(8,128)(2,1)S(1)} collective-permute-done((bf16[50,256]{1,0:T(8,128)(2,1)S(1)}, bf16[50,256]{1,0:T(8,128)(2,1)S(1)}, u32[]{:S(2)}, u32[]{:S(2)}) %collective-permute-start.8) | collective-permute-done | bytes 25632 | tf_op jit(solution)/shard_map/ppermute | solution.py:474
  33.1 1.8 %collective-permute-done.11.refs_3_ = bf16[288,256]{1,0:T(8,128)(2,1)S(1)} collective-permute-done((bf16[288,256]{1,0:T(8,128)(2,1)S(1)}, bf16[288,256]{1,0:T(8,128)(2,1)S(1)}, u32[]{:S(2)}, u32[]{:S(2)}) %collective-permute-start.11) | collective-permute-done | bytes 147488 | tf_op jit(solution)/shard_map/ppermute | solution.py:424
  35.0 2.8 %collective-permute-start.13 = (bf16[72,256]{1,0:T(8,128)(2,1)S(1)}, bf16[72,256]{1,0:T(8,128)(2,1)S(1)}, u32[]{:S(2)}, u32[]{:S(2)}) collective-permute-start(bf16[72,256]{1,0:T(8,128)(2,1)S(1)} %get-tuple-element.57), channel_id=1, source_target_pairs={{0,3},{1,2},{2,1},{3,0},{4,7},{5,6},{6,5},{7,4},{8,11},{9,10},{10,... | collective-permute-start | bytes 110600 | tf_op jit(solution)/shard_map/ppermute | solution.py:430
  38.1 1.3 %collective-permute-start.15 = (bf16[72,256]{1,0:T(8,128)(2,1)S(1)}, bf16[72,256]{1,0:T(8,128)(2,1)S(1)}, u32[]{:S(2)}, u32[]{:S(2)}) collective-permute-start(bf16[72,256]{1,0:T(8,128)(2,1)S(1)} %get-tuple-element.59), channel_id=1, source_target_pairs={{0,1},{1,0},{2,3},{3,2},{4,5},{5,4},{6,7},{7,6},{8,9},{9,8},{10,11... | collective-permute-start | bytes 110600 | tf_op jit(solution)/shard_map/ppermute | solution.py:430
  39.5 1.5 %collective-permute-done.13.refs_1_ = bf16[72,256]{1,0:T(8,128)(2,1)S(1)} collective-permute-done((bf16[72,256]{1,0:T(8,128)(2,1)S(1)}, bf16[72,256]{1,0:T(8,128)(2,1)S(1)}, u32[]{:S(2)}, u32[]{:S(2)}) %collective-permute-start.13) | collective-permute-done | bytes 36896 | tf_op jit(solution)/shard_map/ppermute | solution.py:430
  40.9 1.8 %collective-permute-done.14.refs_2_ = bf16[72,256]{1,0:T(8,128)(2,1)S(1)} collective-permute-done((bf16[72,256]{1,0:T(8,128)(2,1)S(1)}, bf16[72,256]{1,0:T(8,128)(2,1)S(1)}, u32[]{:S(2)}, u32[]{:S(2)}) %collective-permute-start.14) | collective-permute-done | bytes 36896 | tf_op jit(solution)/shard_map/ppermute | solution.py:430
  42.9 1.9 %collective-permute-start.16 = (bf16[98,256]{1,0:T(8,128)(2,1)S(1)}, bf16[98,256]{1,0:T(8,128)(2,1)S(1)}, u32[]{:S(2)}, u32[]{:S(2)}) collective-permute-start(bf16[98,256]{1,0:T(8,128)(2,1)S(1)} %get-tuple-element.60), channel_id=1, source_target_pairs={{0,3},{1,2},{2,1},{3,0},{4,7},{5,6},{6,5},{7,4},{8,11},{9,10},{10,... | collective-permute-start | bytes 150536 | tf_op jit(solution)/shard_map/ppermute | solution.py:430
  45.1 2.2 %collective-permute-start.18 = (bf16[98,256]{1,0:T(8,128)(2,1)S(1)}, bf16[98,256]{1,0:T(8,128)(2,1)S(1)}, u32[]{:S(2)}, u32[]{:S(2)}) collective-permute-start(bf16[98,256]{1,0:T(8,128)(2,1)S(1)} %get-tuple-element.62), channel_id=1, source_target_pairs={{0,1},{1,0},{2,3},{3,2},{4,5},{5,4},{6,7},{7,6},{8,9},{9,8},{10,11... | collective-permute-start | bytes 150536 | tf_op jit(solution)/shard_map/ppermute | solution.py:430
  47.3 1.5 %collective-permute-done.16.rest_0_.refs_1_ = bf16[98,256]{1,0:T(8,128)(2,1)S(1)} collective-permute-done((bf16[98,256]{1,0:T(8,128)(2,1)S(1)}, bf16[98,256]{1,0:T(8,128)(2,1)S(1)}, u32[]{:S(2)}, u32[]{:S(2)}) %collective-permute-start.16) | collective-permute-done | bytes 50208 | tf_op jit(solution)/shard_map/ppermute | solution.py:430
  48.9 1.5 %collective-permute-done.17.rest_1_.refs_2_ = bf16[98,256]{1,0:T(8,128)(2,1)S(1)} collective-permute-done((bf16[98,256]{1,0:T(8,128)(2,1)S(1)}, bf16[98,256]{1,0:T(8,128)(2,1)S(1)}, u32[]{:S(2)}, u32[]{:S(2)}) %collective-permute-start.17) | collective-permute-done | bytes 50208 | tf_op jit(solution)/shard_map/ppermute | solution.py:430
  52.5 1.5 %collective-permute-start.19 = (bf16[288,256]{1,0:T(8,128)(2,1)S(1)}, bf16[288,256]{1,0:T(8,128)(2,1)S(1)}, u32[]{:S(2)}, u32[]{:S(2)}) collective-permute-start(bf16[288,256]{1,0:T(8,128)(2,1)S(1)} %gather.2.refs_0_), channel_id=1, source_target_pairs={{0,24},{4,28},{8,16},{12,20},{16,8},{20,12},{24,0},{28,4},{1,25},{... | collective-permute-start | bytes 442376 | tf_op jit(solution)/shard_map/ppermute | solution.py:424
  54.0 1.3 %images.1 = (bf16[192,256]{1,0:T(8,128)(2,1)}, bf16[192,256]{1,0:T(8,128)(2,1)}, f32[8,128]{1,0:T(8,128)S(1)}) custom-call(bf16[200,256]{1,0:T(8,128)(2,1)S(1)} %get-tuple-element.46.gq_ref, bf16[50,256]{1,0:T(8,128)(2,1)S(1)} %get-tuple-element.48.near_ref, bf16[50,256]{1,0:T(8,128)(2,1)S(1)} %collective-permute-done.8.refs_5_.far_ref, ...), custom_call_target="tpu_custom_call" | custom-call | tf_op jit(solution)/shard_map/images/pallas_call | solution.py:392
  56.7 1.8 %collective-permute-done.19.refs_1_ = bf16[288,256]{1,0:T(8,128)(2,1)S(1)} collective-permute-done((bf16[288,256]{1,0:T(8,128)(2,1)S(1)}, bf16[288,256]{1,0:T(8,128)(2,1)S(1)}, u32[]{:S(2)}, u32[]{:S(2)}) %collective-permute-start.19) | collective-permute-done | bytes 147488 | tf_op jit(solution)/shard_map/ppermute | solution.py:424
  (40 shorter events, 12.7 us)
Async XLA Ops:
  5.5 4.2 %collective-permute-start.3 = (bf16[928,256]{1,0:T(8,128)(2,1)S(1)}, bf16[928,256]{1,0:T(8,128)(2,1)S(1)}, u32[]{:S(2)}, u32[]{:S(2)}) collective-permute-start(bf16[928,256]{1,0:T(8,128)(2,1)S(1)} %get-tuple-element.40), channel_id=1, source_target_pairs={{0,4},{4,0},{8,12},{12,8},{16,20},{20,16},{24,28},{28,24},{1,5},{5... | collective-permute-start | bytes 1425416 | tf_op jit(solution)/shard_map/ppermute | solution.py:421
  6.0 10.0 %collective-permute-start.1 = (bf16[200,256]{1,0:T(8,128)(2,1)S(1)}, bf16[200,256]{1,0:T(8,128)(2,1)S(1)}, u32[]{:S(2)}, u32[]{:S(2)}) collective-permute-start(bf16[200,256]{1,0:T(8,128)(2,1)S(1)} %get-tuple-element.37), channel_id=1, source_target_pairs={{0,2},{1,3},{2,0},{3,1},{4,6},{5,7},{6,4},{7,5},{8,10},{9,11},{10,... | collective-permute-start | bytes 307208 | tf_op jit(solution)/shard_map/ppermute | solution.py:427
  9.7 11.7 %collective-permute-start.4 = (bf16[256,256]{1,0:T(8,128)(2,1)S(1)}, bf16[256,256]{1,0:T(8,128)(2,1)S(1)}, u32[]{:S(2)}, u32[]{:S(2)}) collective-permute-start(bf16[256,256]{1,0:T(8,128)(2,1)S(1)} %get-tuple-element.42), channel_id=1, source_target_pairs={{0,8},{4,12},{8,0},{12,4},{16,24},{20,28},{24,16},{28,20},{1,9},{5... | collective-permute-start | bytes 393224 | tf_op jit(solution)/shard_map/ppermute | solution.py:424
  11.3 10.1 %collective-permute-start.6 = (bf16[256,256]{1,0:T(8,128)(2,1)S(1)}, bf16[256,256]{1,0:T(8,128)(2,1)S(1)}, u32[]{:S(2)}, u32[]{:S(2)}) collective-permute-start(bf16[256,256]{1,0:T(8,128)(2,1)S(1)} %get-tuple-element.44), channel_id=1, source_target_pairs={{0,24},{4,28},{8,16},{12,20},{16,8},{20,12},{24,0},{28,4},{1,25},{... | collective-permute-start | bytes 393224 | tf_op jit(solution)/shard_map/ppermute | solution.py:424
  12.8 5.1 %collective-permute-start = (bf16[224,256]{1,0:T(8,128)(2,1)S(1)}, bf16[224,256]{1,0:T(8,128)(2,1)S(1)}, u32[]{:S(2)}, u32[]{:S(2)}) collective-permute-start(bf16[224,256]{1,0:T(8,128)(2,1)S(1)} %get-tuple-element.36), channel_id=1, source_target_pairs={{0,1},{1,0},{2,3},{3,2},{4,5},{5,4},{6,7},{7,6},{8,9},{9,8},{10,11... | collective-permute-start | bytes 344072 | tf_op jit(solution)/shard_map/ppermute | solution.py:427
  14.4 6.9 %collective-permute-start.2 = (bf16[224,256]{1,0:T(8,128)(2,1)S(1)}, bf16[224,256]{1,0:T(8,128)(2,1)S(1)}, u32[]{:S(2)}, u32[]{:S(2)}) collective-permute-start(bf16[224,256]{1,0:T(8,128)(2,1)S(1)} %get-tuple-element.38), channel_id=1, source_target_pairs={{0,3},{1,2},{2,1},{3,0},{4,7},{5,6},{6,5},{7,4},{8,11},{9,10},{10,... | collective-permute-start | bytes 344072 | tf_op jit(solution)/shard_map/ppermute | solution.py:427
  16.0 5.4 %collective-permute-start.5 = (bf16[208,256]{1,0:T(8,128)(2,1)S(1)}, bf16[208,256]{1,0:T(8,128)(2,1)S(1)}, u32[]{:S(2)}, u32[]{:S(2)}) collective-permute-start(bf16[208,256]{1,0:T(8,128)(2,1)S(1)} %get-tuple-element.43), channel_id=1, source_target_pairs={{0,16},{4,20},{8,24},{12,28},{16,0},{20,4},{24,8},{28,12},{1,17},{... | collective-permute-start | bytes 319496 | tf_op jit(solution)/shard_map/ppermute | solution.py:424
  22.6 31.4 %copy-start = (bf16[3,3,256,256]{3,2,1,0:T(8,128)(2,1)S(1)}, bf16[3,3,256,256]{3,2,1,0:T(8,128)(2,1)}, u32[]{:S(2)}) copy-start(bf16[3,3,256,256]{3,2,1,0:T(8,128)(2,1)} %param.11) | copy-start | bytes 3538948
  22.6 1.9 %collective-permute-start.9 = (bf16[864,256]{1,0:T(8,128)(2,1)S(1)}, bf16[864,256]{1,0:T(8,128)(2,1)S(1)}, u32[]{:S(2)}, u32[]{:S(2)}) collective-permute-start(bf16[864,256]{1,0:T(8,128)(2,1)S(1)} %get-tuple-element.52), channel_id=1, source_target_pairs={{0,4},{4,0},{8,12},{12,8},{16,20},{20,16},{24,28},{28,24},{1,5},{5... | collective-permute-start | bytes 1327112 | tf_op jit(solution)/shard_map/ppermute | solution.py:421
  22.7 5.5 %collective-permute-start.7 = (bf16[416,256]{1,0:T(8,128)(2,1)S(1)}, bf16[416,256]{1,0:T(8,128)(2,1)S(1)}, u32[]{:S(2)}, u32[]{:S(2)}) collective-permute-start(bf16[416,256]{1,0:T(8,128)(2,1)S(1)} %get-tuple-element.47), channel_id=1, source_target_pairs={{0,4},{4,0},{8,12},{12,8},{16,20},{20,16},{24,28},{28,24},{1,5},{5... | collective-permute-start | bytes 638984 | tf_op jit(solution)/shard_map/ppermute | solution.py:421
  24.6 8.5 %collective-permute-start.10 = (bf16[288,256]{1,0:T(8,128)(2,1)S(1)}, bf16[288,256]{1,0:T(8,128)(2,1)S(1)}, u32[]{:S(2)}, u32[]{:S(2)}) collective-permute-start(bf16[288,256]{1,0:T(8,128)(2,1)S(1)} %get-tuple-element.53), channel_id=1, source_target_pairs={{0,8},{4,12},{8,0},{12,4},{16,24},{20,28},{24,16},{28,20},{1,9},{5... | collective-permute-start | bytes 442376 | tf_op jit(solution)/shard_map/ppermute | solution.py:424
  26.1 8.8 %collective-permute-start.11 = (bf16[288,256]{1,0:T(8,128)(2,1)S(1)}, bf16[288,256]{1,0:T(8,128)(2,1)S(1)}, u32[]{:S(2)}, u32[]{:S(2)}) collective-permute-start(bf16[288,256]{1,0:T(8,128)(2,1)S(1)} %get-tuple-element.54), channel_id=1, source_target_pairs={{0,16},{4,20},{8,24},{12,28},{16,0},{20,4},{24,8},{28,12},{1,17},{... | collective-permute-start | bytes 442376 | tf_op jit(solution)/shard_map/ppermute | solution.py:424
  26.6 8.3 %collective-permute-start.12 = (bf16[288,256]{1,0:T(8,128)(2,1)S(1)}, bf16[288,256]{1,0:T(8,128)(2,1)S(1)}, u32[]{:S(2)}, u32[]{:S(2)}) collective-permute-start(bf16[288,256]{1,0:T(8,128)(2,1)S(1)} %get-tuple-element.55), channel_id=1, source_target_pairs={{0,24},{4,28},{8,16},{12,20},{16,8},{20,12},{24,0},{28,4},{1,25},{... | collective-permute-start | bytes 442376 | tf_op jit(solution)/shard_map/ppermute | solution.py:424
  28.1 4.9 %collective-permute-start.8 = (bf16[50,256]{1,0:T(8,128)(2,1)S(1)}, bf16[50,256]{1,0:T(8,128)(2,1)S(1)}, u32[]{:S(2)}, u32[]{:S(2)}) collective-permute-start(bf16[50,256]{1,0:T(8,128)(2,1)S(1)} %get-tuple-element.49), channel_id=1, source_target_pairs={{0,8},{8,16},{16,24},{12,4},{20,12},{28,20},{1,9},{9,17},{17,25},{... | collective-permute-start | bytes 76808 | tf_op jit(solution)/shard_map/ppermute | solution.py:474
  35.0 5.9 %collective-permute-start.13 = (bf16[72,256]{1,0:T(8,128)(2,1)S(1)}, bf16[72,256]{1,0:T(8,128)(2,1)S(1)}, u32[]{:S(2)}, u32[]{:S(2)}) collective-permute-start(bf16[72,256]{1,0:T(8,128)(2,1)S(1)} %get-tuple-element.57), channel_id=1, source_target_pairs={{0,3},{1,2},{2,1},{3,0},{4,7},{5,6},{6,5},{7,4},{8,11},{9,10},{10,... | collective-permute-start | bytes 110600 | tf_op jit(solution)/shard_map/ppermute | solution.py:430
  37.9 4.9 %collective-permute-start.14 = (bf16[72,256]{1,0:T(8,128)(2,1)S(1)}, bf16[72,256]{1,0:T(8,128)(2,1)S(1)}, u32[]{:S(2)}, u32[]{:S(2)}) collective-permute-start(bf16[72,256]{1,0:T(8,128)(2,1)S(1)} %get-tuple-element.58), channel_id=1, source_target_pairs={{0,2},{1,3},{2,0},{3,1},{4,6},{5,7},{6,4},{7,5},{8,10},{9,11},{10,... | collective-permute-start | bytes 110600 | tf_op jit(solution)/shard_map/ppermute | solution.py:430
  38.1 4.6 %collective-permute-start.15 = (bf16[72,256]{1,0:T(8,128)(2,1)S(1)}, bf16[72,256]{1,0:T(8,128)(2,1)S(1)}, u32[]{:S(2)}, u32[]{:S(2)}) collective-permute-start(bf16[72,256]{1,0:T(8,128)(2,1)S(1)} %get-tuple-element.59), channel_id=1, source_target_pairs={{0,1},{1,0},{2,3},{3,2},{4,5},{5,4},{6,7},{7,6},{8,9},{9,8},{10,11... | collective-permute-start | bytes 110600 | tf_op jit(solution)/shard_map/ppermute | solution.py:430
  42.9 6.0 %collective-permute-start.16 = (bf16[98,256]{1,0:T(8,128)(2,1)S(1)}, bf16[98,256]{1,0:T(8,128)(2,1)S(1)}, u32[]{:S(2)}, u32[]{:S(2)}) collective-permute-start(bf16[98,256]{1,0:T(8,128)(2,1)S(1)} %get-tuple-element.60), channel_id=1, source_target_pairs={{0,3},{1,2},{2,1},{3,0},{4,7},{5,6},{6,5},{7,4},{8,11},{9,10},{10,... | collective-permute-start | bytes 150536 | tf_op jit(solution)/shard_map/ppermute | solution.py:430
  44.8 5.6 %collective-permute-start.17 = (bf16[98,256]{1,0:T(8,128)(2,1)S(1)}, bf16[98,256]{1,0:T(8,128)(2,1)S(1)}, u32[]{:S(2)}, u32[]{:S(2)}) collective-permute-start(bf16[98,256]{1,0:T(8,128)(2,1)S(1)} %get-tuple-element.61), channel_id=1, source_target_pairs={{0,2},{1,3},{2,0},{3,1},{4,6},{5,7},{6,4},{7,5},{8,10},{9,11},{10,... | collective-permute-start | bytes 150536 | tf_op jit(solution)/shard_map/ppermute | solution.py:430
  45.1 5.2 %collective-permute-start.18 = (bf16[98,256]{1,0:T(8,128)(2,1)S(1)}, bf16[98,256]{1,0:T(8,128)(2,1)S(1)}, u32[]{:S(2)}, u32[]{:S(2)}) collective-permute-start(bf16[98,256]{1,0:T(8,128)(2,1)S(1)} %get-tuple-element.62), channel_id=1, source_target_pairs={{0,1},{1,0},{2,3},{3,2},{4,5},{5,4},{6,7},{7,6},{8,9},{9,8},{10,11... | collective-permute-start | bytes 150536 | tf_op jit(solution)/shard_map/ppermute | solution.py:430
  50.4 5.2 %collective-permute-start.21 = (bf16[288,256]{1,0:T(8,128)(2,1)S(1)}, bf16[288,256]{1,0:T(8,128)(2,1)S(1)}, u32[]{:S(2)}, u32[]{:S(2)}) collective-permute-start(bf16[288,256]{1,0:T(8,128)(2,1)S(1)} %gather.2.refs_0_), channel_id=1, source_target_pairs={{0,8},{4,12},{8,0},{12,4},{16,24},{20,28},{24,16},{28,20},{1,9},{5... | collective-permute-start | bytes 442376 | tf_op jit(solution)/shard_map/ppermute | solution.py:424
  51.6 5.1 %collective-permute-start.20 = (bf16[288,256]{1,0:T(8,128)(2,1)S(1)}, bf16[288,256]{1,0:T(8,128)(2,1)S(1)}, u32[]{:S(2)}, u32[]{:S(2)}) collective-permute-start(bf16[288,256]{1,0:T(8,128)(2,1)S(1)} %gather.2.refs_0_), channel_id=1, source_target_pairs={{0,16},{4,20},{8,24},{12,28},{16,0},{20,4},{24,8},{28,12},{1,17},{... | collective-permute-start | bytes 442376 | tf_op jit(solution)/shard_map/ppermute | solution.py:424
  52.5 6.0 %collective-permute-start.19 = (bf16[288,256]{1,0:T(8,128)(2,1)S(1)}, bf16[288,256]{1,0:T(8,128)(2,1)S(1)}, u32[]{:S(2)}, u32[]{:S(2)}) collective-permute-start(bf16[288,256]{1,0:T(8,128)(2,1)S(1)} %gather.2.refs_0_), channel_id=1, source_target_pairs={{0,24},{4,28},{8,16},{12,20},{16,8},{20,12},{24,0},{28,4},{1,25},{... | collective-permute-start | bytes 442376 | tf_op jit(solution)/shard_map/ppermute | solution.py:424
  58.7 2.1 %collective-permute-start.22 = (bf16[1152,256]{1,0:T(8,128)(2,1)S(1)}, bf16[1152,256]{1,0:T(8,128)(2,1)S(1)}, u32[]{:S(2)}, u32[]{:S(2)}) collective-permute-start(bf16[1152,256]{1,0:T(8,128)(2,1)S(1)} %gather.3.refs_0_), channel_id=1, source_target_pairs={{0,4},{4,0},{8,12},{12,8},{16,20},{20,16},{24,28},{28,24},{1,5},{5... | collective-permute-start | bytes 1769480 | tf_op jit(solution)/shard_map/ppermute | solution.py:421
  (2 other events, 41.6 us)

commit v7 on v6

--- a/solution.py
+++ b/solution.py
@@ -381,7 +381,7 @@
         in_specs=[vmem] + [hbm] * len(more),
         out_specs=hbm,
         out_shape=jax.ShapeDtypeStruct((2 * rows, channels), F32),
-        scratch_shapes=[pltpu.VMEM((rows, channels), F32), pltpu.SemaphoreType.DMA((8,))],
+        scratch_shapes=[pltpu.VMEM((rows, channels), F32), pltpu.SemaphoreType.DMA((3,))],
         input_output_aliases={1: 0} if more else {},
         compiler_params=pltpu.CompilerParams(vmem_limit_bytes=SMALL_BYTES),
         name="widen",

time: 62 us -> 62 us (level)
  no operation moved by 1% of the time
where the time goes in v7:
time: 62 us; the launch traced here: 61.8 us
  starting transfers between devices  31.5 us (51%)
  waiting for transfers between devices  19.4 us (31%)
  Pallas kernels  10.1 us (16%)
  between operations  0.77 us (1%)
    ppermute x9, starting transfers between devices, to_quad(): lax.ppermute(x, 'pb', flip(n_pb, 2 * s))  11.2 us
    ppermute x6, starting transfers between devices, to_far_layers(): lax.ppermute(x, 'ka', flip(n_ka, n_ka - i))  8.91 us
    ppermute x3, starting transfers between devices, to_layers(): lax.ppermute(x, 'ka', flip(n_ka, s))  6.88 us
    ppermute x6, waiting for transfers between devices, to_far_layers(): lax.ppermute(x, 'ka', flip(n_ka, n_ka - i))  6.27 us
    ppermute x9, waiting for transfers between devices, to_quad(): lax.ppermute(x, 'pb', flip(n_pb, 2 * s))  5.12 us
    pallas_call x1, Pallas kernels, correlate(): pl.pallas_call(functools.partial(corr_kernel, dims), in_specs=[hbm] * 5,...  4.8 us
    ppermute x3, waiting for transfers between devices, to_layers(): lax.ppermute(x, 'ka', flip(n_ka, s))  4.27 us
    ppermute x1, starting transfers between devices, body(): lax.ppermute(far, 'pb', [(i, i + 2) for i in firsts] + [(i + 3, i + 1) fo...  3.4 us
  transfers between devices with their start and end apart: 23, of which 14 were waited for; matrix products, arithmetic and copies ran while one was open for 0% of the time, Pallas kernels for 4%

profile of v7, /device:TPU:0, one launch (start us, length us, event | category | flops | bytes accessed | tf_op | source)
XLA Modules:
  0.0 61.8 jit_solution(9715127463528113962)
XLA Ops:
  0.7 4.8 %correlate.1 = (bf16[200,256]{1,0:T(8,128)(2,1)S(1)}, bf16[224,256]{1,0:T(8,128)(2,1)S(1)}, bf16[200,256]{1,0:T(8,128)(2,1)S(1)}, bf16[224,256]{1,0:T(8,128)(2,1...) custom-call(bf16[2040,768]{1,0:T(8,128)(2,1)} %bitcast.11, bf16[768,256]{1,0:T(8,128)(2,1)} %bitcast.13, ...), custom_call_target="tpu_custom_call" | custom-call | tf_op jit(solution)/shard_map/correlate/pallas_call | solution.py:155
  6.0 3.7 %collective-permute-start.1 = (bf16[200,256]{1,0:T(8,128)(2,1)S(1)}, bf16[200,256]{1,0:T(8,128)(2,1)S(1)}, u32[]{:S(2)}, u32[]{:S(2)}) collective-permute-start(bf16[200,256]{1,0:T(8,128)(2,1)S(1)} %get-tuple-element.37), channel_id=1, source_target_pairs={{0,2},{1,3},{2,0},{3,1},{4,6},{5,7},{6,4},{7,5},{8,10},{9,11},{10,... | collective-permute-start | bytes 307208 | tf_op jit(solution)/shard_map/ppermute | solution.py:427
  9.7 1.6 %collective-permute-start.4 = (bf16[256,256]{1,0:T(8,128)(2,1)S(1)}, bf16[256,256]{1,0:T(8,128)(2,1)S(1)}, u32[]{:S(2)}, u32[]{:S(2)}) collective-permute-start(bf16[256,256]{1,0:T(8,128)(2,1)S(1)} %get-tuple-element.42), channel_id=1, source_target_pairs={{0,8},{4,12},{8,0},{12,4},{16,24},{20,28},{24,16},{28,20},{1,9},{5... | collective-permute-start | bytes 393224 | tf_op jit(solution)/shard_map/ppermute | solution.py:424
  11.3 1.5 %collective-permute-start.6 = (bf16[256,256]{1,0:T(8,128)(2,1)S(1)}, bf16[256,256]{1,0:T(8,128)(2,1)S(1)}, u32[]{:S(2)}, u32[]{:S(2)}) collective-permute-start(bf16[256,256]{1,0:T(8,128)(2,1)S(1)} %get-tuple-element.44), channel_id=1, source_target_pairs={{0,24},{4,28},{8,16},{12,20},{16,8},{20,12},{24,0},{28,4},{1,25},{... | collective-permute-start | bytes 393224 | tf_op jit(solution)/shard_map/ppermute | solution.py:424
  12.8 1.6 %collective-permute-start = (bf16[224,256]{1,0:T(8,128)(2,1)S(1)}, bf16[224,256]{1,0:T(8,128)(2,1)S(1)}, u32[]{:S(2)}, u32[]{:S(2)}) collective-permute-start(bf16[224,256]{1,0:T(8,128)(2,1)S(1)} %get-tuple-element.36), channel_id=1, source_target_pairs={{0,1},{1,0},{2,3},{3,2},{4,5},{5,4},{6,7},{7,6},{8,9},{9,8},{10,11... | collective-permute-start | bytes 344072 | tf_op jit(solution)/shard_map/ppermute | solution.py:427
  14.4 1.6 %collective-permute-start.2 = (bf16[224,256]{1,0:T(8,128)(2,1)S(1)}, bf16[224,256]{1,0:T(8,128)(2,1)S(1)}, u32[]{:S(2)}, u32[]{:S(2)}) collective-permute-start(bf16[224,256]{1,0:T(8,128)(2,1)S(1)} %get-tuple-element.38), channel_id=1, source_target_pairs={{0,3},{1,2},{2,1},{3,0},{4,7},{5,6},{6,5},{7,4},{8,11},{9,10},{10,... | collective-permute-start | bytes 344072 | tf_op jit(solution)/shard_map/ppermute | solution.py:427
  17.9 3.4 %collective-permute-done.2.refs_3_ = bf16[224,256]{1,0:T(8,128)(2,1)S(1)} collective-permute-done((bf16[224,256]{1,0:T(8,128)(2,1)S(1)}, bf16[224,256]{1,0:T(8,128)(2,1)S(1)}, u32[]{:S(2)}, u32[]{:S(2)}) %collective-permute-start.2) | collective-permute-done | bytes 114720 | tf_op jit(solution)/shard_map/ppermute | solution.py:427
  23.2 1.3 %collective-permute-done.9.recv_ref = bf16[864,256]{1,0:T(8,128)(2,1)S(1)} collective-permute-done((bf16[864,256]{1,0:T(8,128)(2,1)S(1)}, bf16[864,256]{1,0:T(8,128)(2,1)S(1)}, u32[]{:S(2)}, u32[]{:S(2)}) %collective-permute-start.9) | collective-permute-done | bytes 442400 | tf_op jit(solution)/shard_map/ppermute | solution.py:421
  24.6 1.6 %collective-permute-start.10 = (bf16[288,256]{1,0:T(8,128)(2,1)S(1)}, bf16[288,256]{1,0:T(8,128)(2,1)S(1)}, u32[]{:S(2)}, u32[]{:S(2)}) collective-permute-start(bf16[288,256]{1,0:T(8,128)(2,1)S(1)} %get-tuple-element.53), channel_id=1, source_target_pairs={{0,8},{4,12},{8,0},{12,4},{16,24},{20,28},{24,16},{28,20},{1,9},{5... | collective-permute-start | bytes 442376 | tf_op jit(solution)/shard_map/ppermute | solution.py:424
  26.6 1.5 %collective-permute-start.12 = (bf16[288,256]{1,0:T(8,128)(2,1)S(1)}, bf16[288,256]{1,0:T(8,128)(2,1)S(1)}, u32[]{:S(2)}, u32[]{:S(2)}) collective-permute-start(bf16[288,256]{1,0:T(8,128)(2,1)S(1)} %get-tuple-element.55), channel_id=1, source_target_pairs={{0,24},{4,28},{8,16},{12,20},{16,8},{20,12},{24,0},{28,4},{1,25},{... | collective-permute-start | bytes 442376 | tf_op jit(solution)/shard_map/ppermute | solution.py:424
  28.1 3.4 %collective-permute-start.8 = (bf16[50,256]{1,0:T(8,128)(2,1)S(1)}, bf16[50,256]{1,0:T(8,128)(2,1)S(1)}, u32[]{:S(2)}, u32[]{:S(2)}) collective-permute-start(bf16[50,256]{1,0:T(8,128)(2,1)S(1)} %get-tuple-element.49), channel_id=1, source_target_pairs={{0,8},{8,16},{16,24},{12,4},{20,12},{28,20},{1,9},{9,17},{17,25},{... | collective-permute-start | bytes 76808 | tf_op jit(solution)/shard_map/ppermute | solution.py:474
  31.5 1.5 %collective-permute-done.8.refs_5_.far_ref = bf16[50,256]{1,0:T(8,128)(2,1)S(1)} collective-permute-done((bf16[50,256]{1,0:T(8,128)(2,1)S(1)}, bf16[50,256]{1,0:T(8,128)(2,1)S(1)}, u32[]{:S(2)}, u32[]{:S(2)}) %collective-permute-start.8) | collective-permute-done | bytes 25632 | tf_op jit(solution)/shard_map/ppermute | solution.py:474
  33.1 1.8 %collective-permute-done.11.refs_3_ = bf16[288,256]{1,0:T(8,128)(2,1)S(1)} collective-permute-done((bf16[288,256]{1,0:T(8,128)(2,1)S(1)}, bf16[288,256]{1,0:T(8,128)(2,1)S(1)}, u32[]{:S(2)}, u32[]{:S(2)}) %collective-permute-start.11) | collective-permute-done | bytes 147488 | tf_op jit(solution)/shard_map/ppermute | solution.py:424
  35.0 2.8 %collective-permute-start.13 = (bf16[72,256]{1,0:T(8,128)(2,1)S(1)}, bf16[72,256]{1,0:T(8,128)(2,1)S(1)}, u32[]{:S(2)}, u32[]{:S(2)}) collective-permute-start(bf16[72,256]{1,0:T(8,128)(2,1)S(1)} %get-tuple-element.57), channel_id=1, source_target_pairs={{0,3},{1,2},{2,1},{3,0},{4,7},{5,6},{6,5},{7,4},{8,11},{9,10},{10,... | collective-permute-start | bytes 110600 | tf_op jit(solution)/shard_map/ppermute | solution.py:430
  38.1 1.3 %collective-permute-start.15 = (bf16[72,256]{1,0:T(8,128)(2,1)S(1)}, bf16[72,256]{1,0:T(8,128)(2,1)S(1)}, u32[]{:S(2)}, u32[]{:S(2)}) collective-permute-start(bf16[72,256]{1,0:T(8,128)(2,1)S(1)} %get-tuple-element.59), channel_id=1, source_target_pairs={{0,1},{1,0},{2,3},{3,2},{4,5},{5,4},{6,7},{7,6},{8,9},{9,8},{10,11... | collective-permute-start | bytes 110600 | tf_op jit(solution)/shard_map/ppermute | solution.py:430
  39.5 1.5 %collective-permute-done.13.refs_1_ = bf16[72,256]{1,0:T(8,128)(2,1)S(1)} collective-permute-done((bf16[72,256]{1,0:T(8,128)(2,1)S(1)}, bf16[72,256]{1,0:T(8,128)(2,1)S(1)}, u32[]{:S(2)}, u32[]{:S(2)}) %collective-permute-start.13) | collective-permute-done | bytes 36896 | tf_op jit(solution)/shard_map/ppermute | solution.py:430
  40.9 1.8 %collective-permute-done.14.refs_2_ = bf16[72,256]{1,0:T(8,128)(2,1)S(1)} collective-permute-done((bf16[72,256]{1,0:T(8,128)(2,1)S(1)}, bf16[72,256]{1,0:T(8,128)(2,1)S(1)}, u32[]{:S(2)}, u32[]{:S(2)}) %collective-permute-start.14) | collective-permute-done | bytes 36896 | tf_op jit(solution)/shard_map/ppermute | solution.py:430
  42.9 1.9 %collective-permute-start.16 = (bf16[98,256]{1,0:T(8,128)(2,1)S(1)}, bf16[98,256]{1,0:T(8,128)(2,1)S(1)}, u32[]{:S(2)}, u32[]{:S(2)}) collective-permute-start(bf16[98,256]{1,0:T(8,128)(2,1)S(1)} %get-tuple-element.60), channel_id=1, source_target_pairs={{0,3},{1,2},{2,1},{3,0},{4,7},{5,6},{6,5},{7,4},{8,11},{9,10},{10,... | collective-permute-start | bytes 150536 | tf_op jit(solution)/shard_map/ppermute | solution.py:430
  45.1 2.2 %collective-permute-start.18 = (bf16[98,256]{1,0:T(8,128)(2,1)S(1)}, bf16[98,256]{1,0:T(8,128)(2,1)S(1)}, u32[]{:S(2)}, u32[]{:S(2)}) collective-permute-start(bf16[98,256]{1,0:T(8,128)(2,1)S(1)} %get-tuple-element.62), channel_id=1, source_target_pairs={{0,1},{1,0},{2,3},{3,2},{4,5},{5,4},{6,7},{7,6},{8,9},{9,8},{10,11... | collective-permute-start | bytes 150536 | tf_op jit(solution)/shard_map/ppermute | solution.py:430
  47.3 1.5 %collective-permute-done.16.rest_0_.refs_1_ = bf16[98,256]{1,0:T(8,128)(2,1)S(1)} collective-permute-done((bf16[98,256]{1,0:T(8,128)(2,1)S(1)}, bf16[98,256]{1,0:T(8,128)(2,1)S(1)}, u32[]{:S(2)}, u32[]{:S(2)}) %collective-permute-start.16) | collective-permute-done | bytes 50208 | tf_op jit(solution)/shard_map/ppermute | solution.py:430
  48.9 1.5 %collective-permute-done.17.rest_1_.refs_2_ = bf16[98,256]{1,0:T(8,128)(2,1)S(1)} collective-permute-done((bf16[98,256]{1,0:T(8,128)(2,1)S(1)}, bf16[98,256]{1,0:T(8,128)(2,1)S(1)}, u32[]{:S(2)}, u32[]{:S(2)}) %collective-permute-start.17) | collective-permute-done | bytes 50208 | tf_op jit(solution)/shard_map/ppermute | solution.py:430
  52.5 1.5 %collective-permute-start.19 = (bf16[288,256]{1,0:T(8,128)(2,1)S(1)}, bf16[288,256]{1,0:T(8,128)(2,1)S(1)}, u32[]{:S(2)}, u32[]{:S(2)}) collective-permute-start(bf16[288,256]{1,0:T(8,128)(2,1)S(1)} %gather.2.refs_0_), channel_id=1, source_target_pairs={{0,24},{4,28},{8,16},{12,20},{16,8},{20,12},{24,0},{28,4},{1,25},{... | collective-permute-start | bytes 442376 | tf_op jit(solution)/shard_map/ppermute | solution.py:424
  54.0 1.3 %images.1 = (bf16[192,256]{1,0:T(8,128)(2,1)}, bf16[192,256]{1,0:T(8,128)(2,1)}, f32[8,128]{1,0:T(8,128)S(1)}) custom-call(bf16[200,256]{1,0:T(8,128)(2,1)S(1)} %get-tuple-element.46.gq_ref, bf16[50,256]{1,0:T(8,128)(2,1)S(1)} %get-tuple-element.48.near_ref, bf16[50,256]{1,0:T(8,128)(2,1)S(1)} %collective-permute-done.8.refs_5_.far_ref, ...), custom_call_target="tpu_custom_call" | custom-call | tf_op jit(solution)/shard_map/images/pallas_call | solution.py:392
  56.7 1.8 %collective-permute-done.19.refs_1_ = bf16[288,256]{1,0:T(8,128)(2,1)S(1)} collective-permute-done((bf16[288,256]{1,0:T(8,128)(2,1)S(1)}, bf16[288,256]{1,0:T(8,128)(2,1)S(1)}, u32[]{:S(2)}, u32[]{:S(2)}) %collective-permute-start.19) | collective-permute-done | bytes 147488 | tf_op jit(solution)/shard_map/ppermute | solution.py:424
  (40 shorter events, 12.7 us)
Async XLA Ops:
  5.5 4.2 %collective-permute-start.3 = (bf16[928,256]{1,0:T(8,128)(2,1)S(1)}, bf16[928,256]{1,0:T(8,128)(2,1)S(1)}, u32[]{:S(2)}, u32[]{:S(2)}) collective-permute-start(bf16[928,256]{1,0:T(8,128)(2,1)S(1)} %get-tuple-element.40), channel_id=1, source_target_pairs={{0,4},{4,0},{8,12},{12,8},{16,20},{20,16},{24,28},{28,24},{1,5},{5... | collective-permute-start | bytes 1425416 | tf_op jit(solution)/shard_map/ppermute | solution.py:421
  6.0 10.0 %collective-permute-start.1 = (bf16[200,256]{1,0:T(8,128)(2,1)S(1)}, bf16[200,256]{1,0:T(8,128)(2,1)S(1)}, u32[]{:S(2)}, u32[]{:S(2)}) collective-permute-start(bf16[200,256]{1,0:T(8,128)(2,1)S(1)} %get-tuple-element.37), channel_id=1, source_target_pairs={{0,2},{1,3},{2,0},{3,1},{4,6},{5,7},{6,4},{7,5},{8,10},{9,11},{10,... | collective-permute-start | bytes 307208 | tf_op jit(solution)/shard_map/ppermute | solution.py:427
  9.7 11.7 %collective-permute-start.4 = (bf16[256,256]{1,0:T(8,128)(2,1)S(1)}, bf16[256,256]{1,0:T(8,128)(2,1)S(1)}, u32[]{:S(2)}, u32[]{:S(2)}) collective-permute-start(bf16[256,256]{1,0:T(8,128)(2,1)S(1)} %get-tuple-element.42), channel_id=1, source_target_pairs={{0,8},{4,12},{8,0},{12,4},{16,24},{20,28},{24,16},{28,20},{1,9},{5... | collective-permute-start | bytes 393224 | tf_op jit(solution)/shard_map/ppermute | solution.py:424
  11.3 10.1 %collective-permute-start.6 = (bf16[256,256]{1,0:T(8,128)(2,1)S(1)}, bf16[256,256]{1,0:T(8,128)(2,1)S(1)}, u32[]{:S(2)}, u32[]{:S(2)}) collective-permute-start(bf16[256,256]{1,0:T(8,128)(2,1)S(1)} %get-tuple-element.44), channel_id=1, source_target_pairs={{0,24},{4,28},{8,16},{12,20},{16,8},{20,12},{24,0},{28,4},{1,25},{... | collective-permute-start | bytes 393224 | tf_op jit(solution)/shard_map/ppermute | solution.py:424
  12.8 5.1 %collective-permute-start = (bf16[224,256]{1,0:T(8,128)(2,1)S(1)}, bf16[224,256]{1,0:T(8,128)(2,1)S(1)}, u32[]{:S(2)}, u32[]{:S(2)}) collective-permute-start(bf16[224,256]{1,0:T(8,128)(2,1)S(1)} %get-tuple-element.36), channel_id=1, source_target_pairs={{0,1},{1,0},{2,3},{3,2},{4,5},{5,4},{6,7},{7,6},{8,9},{9,8},{10,11... | collective-permute-start | bytes 344072 | tf_op jit(solution)/shard_map/ppermute | solution.py:427
  14.4 6.9 %collective-permute-start.2 = (bf16[224,256]{1,0:T(8,128)(2,1)S(1)}, bf16[224,256]{1,0:T(8,128)(2,1)S(1)}, u32[]{:S(2)}, u32[]{:S(2)}) collective-permute-start(bf16[224,256]{1,0:T(8,128)(2,1)S(1)} %get-tuple-element.38), channel_id=1, source_target_pairs={{0,3},{1,2},{2,1},{3,0},{4,7},{5,6},{6,5},{7,4},{8,11},{9,10},{10,... | collective-permute-start | bytes 344072 | tf_op jit(solution)/shard_map/ppermute | solution.py:427
  16.0 5.4 %collective-permute-start.5 = (bf16[208,256]{1,0:T(8,128)(2,1)S(1)}, bf16[208,256]{1,0:T(8,128)(2,1)S(1)}, u32[]{:S(2)}, u32[]{:S(2)}) collective-permute-start(bf16[208,256]{1,0:T(8,128)(2,1)S(1)} %get-tuple-element.43), channel_id=1, source_target_pairs={{0,16},{4,20},{8,24},{12,28},{16,0},{20,4},{24,8},{28,12},{1,17},{... | collective-permute-start | bytes 319496 | tf_op jit(solution)/shard_map/ppermute | solution.py:424
  22.6 31.4 %copy-start = (bf16[3,3,256,256]{3,2,1,0:T(8,128)(2,1)S(1)}, bf16[3,3,256,256]{3,2,1,0:T(8,128)(2,1)}, u32[]{:S(2)}) copy-start(bf16[3,3,256,256]{3,2,1,0:T(8,128)(2,1)} %param.11) | copy-start | bytes 3538948
  22.6 1.9 %collective-permute-start.9 = (bf16[864,256]{1,0:T(8,128)(2,1)S(1)}, bf16[864,256]{1,0:T(8,128)(2,1)S(1)}, u32[]{:S(2)}, u32[]{:S(2)}) collective-permute-start(bf16[864,256]{1,0:T(8,128)(2,1)S(1)} %get-tuple-element.52), channel_id=1, source_target_pairs={{0,4},{4,0},{8,12},{12,8},{16,20},{20,16},{24,28},{28,24},{1,5},{5... | collective-permute-start | bytes 1327112 | tf_op jit(solution)/shard_map/ppermute | solution.py:421
  22.7 5.5 %collective-permute-start.7 = (bf16[416,256]{1,0:T(8,128)(2,1)S(1)}, bf16[416,256]{1,0:T(8,128)(2,1)S(1)}, u32[]{:S(2)}, u32[]{:S(2)}) collective-permute-start(bf16[416,256]{1,0:T(8,128)(2,1)S(1)} %get-tuple-element.47), channel_id=1, source_target_pairs={{0,4},{4,0},{8,12},{12,8},{16,20},{20,16},{24,28},{28,24},{1,5},{5... | collective-permute-start | bytes 638984 | tf_op jit(solution)/shard_map/ppermute | solution.py:421
  24.6 8.5 %collective-permute-start.10 = (bf16[288,256]{1,0:T(8,128)(2,1)S(1)}, bf16[288,256]{1,0:T(8,128)(2,1)S(1)}, u32[]{:S(2)}, u32[]{:S(2)}) collective-permute-start(bf16[288,256]{1,0:T(8,128)(2,1)S(1)} %get-tuple-element.53), channel_id=1, source_target_pairs={{0,8},{4,12},{8,0},{12,4},{16,24},{20,28},{24,16},{28,20},{1,9},{5... | collective-permute-start | bytes 442376 | tf_op jit(solution)/shard_map/ppermute | solution.py:424
  26.1 8.8 %collective-permute-start.11 = (bf16[288,256]{1,0:T(8,128)(2,1)S(1)}, bf16[288,256]{1,0:T(8,128)(2,1)S(1)}, u32[]{:S(2)}, u32[]{:S(2)}) collective-permute-start(bf16[288,256]{1,0:T(8,128)(2,1)S(1)} %get-tuple-element.54), channel_id=1, source_target_pairs={{0,16},{4,20},{8,24},{12,28},{16,0},{20,4},{24,8},{28,12},{1,17},{... | collective-permute-start | bytes 442376 | tf_op jit(solution)/shard_map/ppermute | solution.py:424
  26.6 8.3 %collective-permute-start.12 = (bf16[288,256]{1,0:T(8,128)(2,1)S(1)}, bf16[288,256]{1,0:T(8,128)(2,1)S(1)}, u32[]{:S(2)}, u32[]{:S(2)}) collective-permute-start(bf16[288,256]{1,0:T(8,128)(2,1)S(1)} %get-tuple-element.55), channel_id=1, source_target_pairs={{0,24},{4,28},{8,16},{12,20},{16,8},{20,12},{24,0},{28,4},{1,25},{... | collective-permute-start | bytes 442376 | tf_op jit(solution)/shard_map/ppermute | solution.py:424
  28.1 4.9 %collective-permute-start.8 = (bf16[50,256]{1,0:T(8,128)(2,1)S(1)}, bf16[50,256]{1,0:T(8,128)(2,1)S(1)}, u32[]{:S(2)}, u32[]{:S(2)}) collective-permute-start(bf16[50,256]{1,0:T(8,128)(2,1)S(1)} %get-tuple-element.49), channel_id=1, source_target_pairs={{0,8},{8,16},{16,24},{12,4},{20,12},{28,20},{1,9},{9,17},{17,25},{... | collective-permute-start | bytes 76808 | tf_op jit(solution)/shard_map/ppermute | solution.py:474
  35.0 5.9 %collective-permute-start.13 = (bf16[72,256]{1,0:T(8,128)(2,1)S(1)}, bf16[72,256]{1,0:T(8,128)(2,1)S(1)}, u32[]{:S(2)}, u32[]{:S(2)}) collective-permute-start(bf16[72,256]{1,0:T(8,128)(2,1)S(1)} %get-tuple-element.57), channel_id=1, source_target_pairs={{0,3},{1,2},{2,1},{3,0},{4,7},{5,6},{6,5},{7,4},{8,11},{9,10},{10,... | collective-permute-start | bytes 110600 | tf_op jit(solution)/shard_map/ppermute | solution.py:430
  37.9 4.9 %collective-permute-start.14 = (bf16[72,256]{1,0:T(8,128)(2,1)S(1)}, bf16[72,256]{1,0:T(8,128)(2,1)S(1)}, u32[]{:S(2)}, u32[]{:S(2)}) collective-permute-start(bf16[72,256]{1,0:T(8,128)(2,1)S(1)} %get-tuple-element.58), channel_id=1, source_target_pairs={{0,2},{1,3},{2,0},{3,1},{4,6},{5,7},{6,4},{7,5},{8,10},{9,11},{10,... | collective-permute-start | bytes 110600 | tf_op jit(solution)/shard_map/ppermute | solution.py:430
  38.1 4.6 %collective-permute-start.15 = (bf16[72,256]{1,0:T(8,128)(2,1)S(1)}, bf16[72,256]{1,0:T(8,128)(2,1)S(1)}, u32[]{:S(2)}, u32[]{:S(2)}) collective-permute-start(bf16[72,256]{1,0:T(8,128)(2,1)S(1)} %get-tuple-element.59), channel_id=1, source_target_pairs={{0,1},{1,0},{2,3},{3,2},{4,5},{5,4},{6,7},{7,6},{8,9},{9,8},{10,11... | collective-permute-start | bytes 110600 | tf_op jit(solution)/shard_map/ppermute | solution.py:430
  42.9 6.0 %collective-permute-start.16 = (bf16[98,256]{1,0:T(8,128)(2,1)S(1)}, bf16[98,256]{1,0:T(8,128)(2,1)S(1)}, u32[]{:S(2)}, u32[]{:S(2)}) collective-permute-start(bf16[98,256]{1,0:T(8,128)(2,1)S(1)} %get-tuple-element.60), channel_id=1, source_target_pairs={{0,3},{1,2},{2,1},{3,0},{4,7},{5,6},{6,5},{7,4},{8,11},{9,10},{10,... | collective-permute-start | bytes 150536 | tf_op jit(solution)/shard_map/ppermute | solution.py:430
  44.8 5.6 %collective-permute-start.17 = (bf16[98,256]{1,0:T(8,128)(2,1)S(1)}, bf16[98,256]{1,0:T(8,128)(2,1)S(1)}, u32[]{:S(2)}, u32[]{:S(2)}) collective-permute-start(bf16[98,256]{1,0:T(8,128)(2,1)S(1)} %get-tuple-element.61), channel_id=1, source_target_pairs={{0,2},{1,3},{2,0},{3,1},{4,6},{5,7},{6,4},{7,5},{8,10},{9,11},{10,... | collective-permute-start | bytes 150536 | tf_op jit(solution)/shard_map/ppermute | solution.py:430
  45.1 5.2 %collective-permute-start.18 = (bf16[98,256]{1,0:T(8,128)(2,1)S(1)}, bf16[98,256]{1,0:T(8,128)(2,1)S(1)}, u32[]{:S(2)}, u32[]{:S(2)}) collective-permute-start(bf16[98,256]{1,0:T(8,128)(2,1)S(1)} %get-tuple-element.62), channel_id=1, source_target_pairs={{0,1},{1,0},{2,3},{3,2},{4,5},{5,4},{6,7},{7,6},{8,9},{9,8},{10,11... | collective-permute-start | bytes 150536 | tf_op jit(solution)/shard_map/ppermute | solution.py:430
  50.4 5.2 %collective-permute-start.21 = (bf16[288,256]{1,0:T(8,128)(2,1)S(1)}, bf16[288,256]{1,0:T(8,128)(2,1)S(1)}, u32[]{:S(2)}, u32[]{:S(2)}) collective-permute-start(bf16[288,256]{1,0:T(8,128)(2,1)S(1)} %gather.2.refs_0_), channel_id=1, source_target_pairs={{0,8},{4,12},{8,0},{12,4},{16,24},{20,28},{24,16},{28,20},{1,9},{5... | collective-permute-start | bytes 442376 | tf_op jit(solution)/shard_map/ppermute | solution.py:424
  51.6 5.1 %collective-permute-start.20 = (bf16[288,256]{1,0:T(8,128)(2,1)S(1)}, bf16[288,256]{1,0:T(8,128)(2,1)S(1)}, u32[]{:S(2)}, u32[]{:S(2)}) collective-permute-start(bf16[288,256]{1,0:T(8,128)(2,1)S(1)} %gather.2.refs_0_), channel_id=1, source_target_pairs={{0,16},{4,20},{8,24},{12,28},{16,0},{20,4},{24,8},{28,12},{1,17},{... | collective-permute-start | bytes 442376 | tf_op jit(solution)/shard_map/ppermute | solution.py:424
  52.5 6.0 %collective-permute-start.19 = (bf16[288,256]{1,0:T(8,128)(2,1)S(1)}, bf16[288,256]{1,0:T(8,128)(2,1)S(1)}, u32[]{:S(2)}, u32[]{:S(2)}) collective-permute-start(bf16[288,256]{1,0:T(8,128)(2,1)S(1)} %gather.2.refs_0_), channel_id=1, source_target_pairs={{0,24},{4,28},{8,16},{12,20},{16,8},{20,12},{24,0},{28,4},{1,25},{... | collective-permute-start | bytes 442376 | tf_op jit(solution)/shard_map/ppermute | solution.py:424
  58.7 2.1 %collective-permute-start.22 = (bf16[1152,256]{1,0:T(8,128)(2,1)S(1)}, bf16[1152,256]{1,0:T(8,128)(2,1)S(1)}, u32[]{:S(2)}, u32[]{:S(2)}) collective-permute-start(bf16[1152,256]{1,0:T(8,128)(2,1)S(1)} %gather.3.refs_0_), channel_id=1, source_target_pairs={{0,4},{4,0},{8,12},{12,8},{16,20},{20,16},{24,28},{28,24},{1,5},{5... | collective-permute-start | bytes 1769480 | tf_op jit(solution)/shard_map/ppermute | solution.py:421
  (2 other events, 41.6 us)
